TPU v7x, 32 devices: a whole 2x2x4 slice. The times are simulated.
32 devices in a mesh: dp: 4 (over y, core), ctx: 2 (over x), tp: 4 (over z).
Axes of the slice: x: 2, y: 2, z: 4, core: 2. Of those that a mesh axis runs over, the one named last changes fastest.
Arguments:
- tokens: bfloat16 [32768, 2048], P(('dp', 'ctx')), may hold values from -6 to 6
- cotangent: bfloat16 [32768, 2048], P(('dp', 'ctx')), may hold values from -6 to 6
- membership: int32 [4, 16], P('dp'), may hold values from 0 to 1
- ln_gain: bfloat16 [2048], replicated, may hold values from 0.099609375 to 1.8984375
- ln_bias: bfloat16 [2048], replicated, may hold values from -1.5 to 1.5
- w_query: bfloat16 [2048, 2048], P(('dp', 'ctx'), 'tp'), may hold values from -0.125 to 0.125
- b_query: bfloat16 [2048], P('tp'), may hold values from -1.5 to 1.5
- w_key: bfloat16 [2048, 2048], P(('dp', 'ctx'), 'tp'), may hold values from -0.125 to 0.125
- b_key: bfloat16 [2048], P('tp'), may hold values from -1.5 to 1.5
- w_value: bfloat16 [2048, 2048], P(('dp', 'ctx'), 'tp'), may hold values from -0.125 to 0.125
- b_value: bfloat16 [2048], P('tp'), may hold values from -1.5 to 1.5
- w_dense: bfloat16 [2048, 2048], P('tp', ('dp', 'ctx')), may hold values from -1 to 1
- b_dense: bfloat16 [2048], replicated, may hold values from -1.5 to 1.5
- w_fc1: bfloat16 [2048, 8192], P(('dp', 'ctx'), 'tp'), may hold values from -0.125 to 0.125
- b_fc1: bfloat16 [8192], P('tp'), may hold values from -1.5 to 1.5
- w_fc2: bfloat16 [8192, 2048], P('tp', ('dp', 'ctx')), may hold values from -0.0625 to 0.0625
- b_fc2: bfloat16 [2048], replicated, may hold values from -1.5 to 1.5
Outputs:
- layer_out: bfloat16 [32768, 2048], P(('dp', 'ctx'))
- grad_tokens: float32 [32768, 2048], P(('dp', 'ctx'))
- grad_ln_gain: float32 [2048], replicated
- grad_ln_bias: float32 [2048], replicated
- grad_w_query: float32 [2048, 2048], P(('dp', 'ctx'), 'tp')
- grad_b_query: float32 [2048], P('tp')
- grad_w_key: float32 [2048, 2048], P(('dp', 'ctx'), 'tp')
- grad_b_key: float32 [2048], P('tp')
- grad_w_value: float32 [2048, 2048], P(('dp', 'ctx'), 'tp')
- grad_b_value: float32 [2048], P('tp')
- grad_w_dense: float32 [2048, 2048], P('tp', ('dp', 'ctx'))
- grad_b_dense: float32 [2048], replicated
- grad_w_fc1: float32 [2048, 8192], P(('dp', 'ctx'), 'tp')
- grad_b_fc1: float32 [8192], P('tp')
- grad_w_fc2: float32 [8192, 2048], P('tp', ('dp', 'ctx'))
- grad_b_fc2: float32 [2048], replicated
Inputs may be any that keep to these rules, and one draw needn't show every extreme that they name: `membership`: entry c of row r names the group, among the 2 of row r, whose prompt continuation c of row r attends to.
All inputs are finite; a program needn't handle non-finite values.
Results may differ from a plain program's by a relative error of at most 0.012.
The roundings to bfloat16 on the way count: a program that leaves them out, or rounds other values in their place, can miss the bound.
Values may be sent and summed in bfloat16 or wider, within the bound.
A program may use at most 512 MiB of HBM per device.

v0:
```python
import jax
import jax.numpy as jnp
from jax import lax
from jax.sharding import PartitionSpec as P

HDIM = 64
ROT = 32
PLEN = 2048
CLEN = 256
GPR = 2


def broadcast(block, axis, holder):
    block = jnp.where(lax.axis_index(axis) == holder, block, jnp.zeros_like(block))
    return lax.psum(block, axis)


def norm_apply(matrix, norm_gain, norm_shift):
    center = matrix - jnp.mean(matrix, axis=-1, keepdims=True)
    spread = jnp.mean(center * center, axis=-1, keepdims=True)
    return center * lax.rsqrt(spread + 1e-05) * norm_gain + norm_shift


def rotary_tables(positions):
    half_rot = ROT // 2
    frequency = 10000.0 ** (-2.0 * jnp.arange(half_rot, dtype=jnp.float32) / ROT)
    angles = positions.astype(jnp.float32)[:, None] * frequency[None, :]
    return (jnp.cos(angles)[:, None, :], jnp.sin(angles)[:, None, :])


def rotate_heads(head_values, cosine, sine_table):
    half_rot = ROT // 2
    first_half = head_values[..., :half_rot]
    second_half = head_values[..., half_rot:ROT]
    return jnp.concatenate(
        [
            first_half * cosine - second_half * sine_table,
            second_half * cosine + first_half * sine_table,
            head_values[..., ROT:],
        ],
        axis=-1,
    )


def gelu_tanh(inputs):
    return jax.nn.gelu(inputs, approximate=True)


def transpose_dot(left, right):
    return jnp.einsum("ra,rb->ab", left, right, preferred_element_type=jnp.float32)


def dot_back(left, right):
    return jnp.einsum("rb,ab->ra", left, right, preferred_element_type=jnp.float32)


def scored(query_part, key_part, allowed):
    scores = jnp.einsum(
        "qhd,khd->hqk", query_part, key_part, preferred_element_type=jnp.float32
    ) * HDIM ** (-0.5)
    return jnp.where(allowed[None], scores, -1e30)


def stat_add(state, scores):
    row_peak, row_total = state
    new_peak = jnp.maximum(row_peak, jnp.max(scores, axis=-1))
    new_total = row_total * jnp.exp(row_peak - new_peak) + jnp.sum(
        jnp.exp(scores - new_peak[..., None]), axis=-1
    )
    return (new_peak, new_total)


def out_add(state, scores, row_peak, row_total, grad_part, value_part):
    result, center = state
    chance = jnp.exp(scores - row_peak[..., None]) / row_total[..., None]
    result = result + jnp.einsum(
        "hqk,khd->qhd", chance.astype(jnp.bfloat16), value_part, preferred_element_type=jnp.float32
    )
    grad_chance = jnp.einsum(
        "qhd,khd->hqk", grad_part, value_part, preferred_element_type=jnp.float32
    )
    return (result, center + jnp.sum(chance * grad_chance, axis=-1))


def back_add(scores, row_peak, row_total, center, query_part, grad_part, key_part, value_part):
    chance = jnp.exp(scores - row_peak[..., None]) / row_total[..., None]
    grad_chance = jnp.einsum(
        "qhd,khd->hqk", grad_part, value_part, preferred_element_type=jnp.float32
    )
    grad_scores = (chance * (grad_chance - center[..., None])).astype(jnp.bfloat16)
    grad_query = jnp.einsum(
        "hqk,khd->qhd", grad_scores, key_part, preferred_element_type=jnp.float32
    ) * HDIM ** (-0.5)
    key_step = jnp.einsum(
        "hqk,qhd->khd", grad_scores, query_part, preferred_element_type=jnp.float32
    ) * HDIM ** (-0.5)
    value_step = jnp.einsum(
        "hqk,qhd->khd", chance.astype(jnp.bfloat16), grad_part, preferred_element_type=jnp.float32
    )
    return (grad_query, key_step, value_step)


def add_rows(buffer, first, update):
    current = lax.dynamic_slice_in_dim(buffer, first, update.shape[0], 0)
    return lax.dynamic_update_slice_in_dim(buffer, current + update, first, 0)


def body(
    tokens,
    cotangent,
    membership,
    ln_gain,
    ln_bias,
    w_query,
    b_query,
    w_key,
    b_key,
    w_value,
    b_value,
    w_dense,
    b_dense,
    w_fc1,
    b_fc1,
    w_fc2,
    b_fc2,
):
    row_count = tokens.shape[0]
    ctx_count = lax.axis_size("ctx")
    holders = ctx_count // 2
    ctx_index = lax.axis_index("ctx")
    query_weight, key_weight, value_weight, dense_weight, expand_weight, shrink_weight = (
        lax.all_gather(w_query, ("dp", "ctx"), axis=0, tiled=True),
        lax.all_gather(w_key, ("dp", "ctx"), axis=0, tiled=True),
        lax.all_gather(w_value, ("dp", "ctx"), axis=0, tiled=True),
        lax.all_gather(w_dense, ("dp", "ctx"), axis=1, tiled=True),
        lax.all_gather(w_fc1, ("dp", "ctx"), axis=0, tiled=True),
        lax.all_gather(w_fc2, ("dp", "ctx"), axis=1, tiled=True),
    )
    local_width = query_weight.shape[1]
    heads_dev = local_width // HDIM
    token_index = ctx_index * row_count + jnp.arange(row_count, dtype=jnp.int32)
    prompt_total = GPR * PLEN
    is_prompt = ctx_index < holders
    cont_offset = token_index - prompt_total
    member_row = membership[0]
    positions = jnp.where(is_prompt, token_index % PLEN, PLEN + cont_offset % CLEN)
    cont_first = (ctx_index * row_count - prompt_total) // CLEN
    x_float = tokens.astype(jnp.float32)
    gain_float = ln_gain.astype(jnp.float32)
    shift_float = ln_bias.astype(jnp.float32)
    hidden = norm_apply(x_float, gain_float, shift_float).astype(jnp.bfloat16)
    cosine, sine_table = rotary_tables(positions)

    def project(weight_matrix, bias_row):
        return jnp.dot(hidden, weight_matrix, preferred_element_type=jnp.float32) + bias_row.astype(
            jnp.float32
        )

    query_lin = project(query_weight, b_query)
    key_lin = project(key_weight, b_key)
    value_lin = project(value_weight, b_value)
    queries = rotate_heads(
        query_lin.reshape(row_count, heads_dev, HDIM), cosine, sine_table
    ).astype(jnp.bfloat16)
    key_rows = (
        rotate_heads(key_lin.reshape(row_count, heads_dev, HDIM), cosine, sine_table)
        .astype(jnp.bfloat16)
        .reshape(row_count, local_width)
    )
    value_rows = value_lin.astype(jnp.bfloat16)
    local_pair = jnp.stack([key_rows, value_rows])

    def fetch(running, holder_index):
        return (running, broadcast(local_pair, "ctx", holder_index))

    _, far_pairs = lax.scan(fetch, jnp.int32(0), jnp.arange(holders, dtype=jnp.int32))
    prompt_keys = far_pairs[:, 0].reshape(prompt_total, heads_dev, HDIM)
    prompt_values = far_pairs[:, 1].reshape(prompt_total, heads_dev, HDIM)
    own_keys = key_rows.reshape(row_count, heads_dev, HDIM)
    own_values = value_rows.reshape(row_count, heads_dev, HDIM)
    grad_float = cotangent.astype(jnp.float32)
    grad_attended = dot_back(cotangent, dense_weight).astype(jnp.bfloat16)
    grad_att_heads = grad_attended.reshape(row_count, heads_dev, HDIM)
    block = min(512, row_count, PLEN)
    per_prompt = PLEN // block
    prompt_blocks = row_count // block
    cont_blocks = row_count // CLEN
    block_range = jnp.arange(block, dtype=jnp.int32)
    causal = (
        jnp.arange(CLEN, dtype=jnp.int32)[:, None] >= jnp.arange(CLEN, dtype=jnp.int32)[None, :]
    )
    open_mask = jnp.ones((CLEN, block), dtype=bool)

    def prompt_setup(step_index):
        first_row = step_index * block
        first_global = ctx_index * row_count + first_row
        lowest = first_global // PLEN * per_prompt
        highest = first_global // block + 1
        query_part = lax.dynamic_slice_in_dim(queries, first_row, block, 0)
        grad_part = lax.dynamic_slice_in_dim(grad_att_heads, first_row, block, 0)
        return (first_row, lowest, highest, first_global + block_range, query_part, grad_part)

    def prompt_span(query_part, query_index, span_index):
        key_part = lax.dynamic_slice_in_dim(prompt_keys, span_index * block, block, 0)
        key_index = span_index * block + block_range
        return scored(query_part, key_part, key_index[None, :] <= query_index[:, None])

    def cont_setup(step_index):
        first_row = step_index * CLEN
        which = lax.dynamic_index_in_dim(
            member_row,
            jnp.clip(cont_first + step_index, 0, member_row.shape[0] - 1),
            0,
            keepdims=False,
        )
        query_part = lax.dynamic_slice_in_dim(queries, first_row, CLEN, 0)
        grad_part = lax.dynamic_slice_in_dim(grad_att_heads, first_row, CLEN, 0)
        own_k = lax.dynamic_slice_in_dim(own_keys, first_row, CLEN, 0)
        own_v = lax.dynamic_slice_in_dim(own_values, first_row, CLEN, 0)
        return (first_row, which * per_prompt, query_part, grad_part, own_k, own_v)

    def far_span(query_part, span_index):
        key_part = lax.dynamic_slice_in_dim(prompt_keys, span_index * block, block, 0)
        return scored(query_part, key_part, open_mask)

    def far_values(span_index):
        return lax.dynamic_slice_in_dim(prompt_values, span_index * block, block, 0)

    def start_stats(count):
        return (
            jnp.full((heads_dev, count), -1e30, jnp.float32),
            jnp.zeros((heads_dev, count), jnp.float32),
        )

    def prompt_forward(step_index):
        first_row, lowest, highest, query_index, query_part, grad_part = prompt_setup(step_index)
        row_peak, row_total = lax.fori_loop(
            lowest,
            highest,
            lambda span_index, state: stat_add(
                state, prompt_span(query_part, query_index, span_index)
            ),
            start_stats(block),
        )

        def prompt_out_step(span_index, state):
            return out_add(
                state,
                prompt_span(query_part, query_index, span_index),
                row_peak,
                row_total,
                grad_part,
                far_values(span_index),
            )

        result, center = lax.fori_loop(
            lowest,
            highest,
            prompt_out_step,
            (
                jnp.zeros((block, heads_dev, HDIM), jnp.float32),
                jnp.zeros((heads_dev, block), jnp.float32),
            ),
        )
        return (result, row_peak.T, row_total.T, center.T)

    def cont_forward(step_index):
        first_row, lowest, query_part, grad_part, own_k, own_v = cont_setup(step_index)
        own_scores = scored(query_part, own_k, causal)
        state = stat_add(start_stats(CLEN), own_scores)
        row_peak, row_total = lax.fori_loop(
            lowest,
            lowest + per_prompt,
            lambda span_index, inner: stat_add(inner, far_span(query_part, span_index)),
            state,
        )
        start = out_add(
            (
                jnp.zeros((CLEN, heads_dev, HDIM), jnp.float32),
                jnp.zeros((heads_dev, CLEN), jnp.float32),
            ),
            own_scores,
            row_peak,
            row_total,
            grad_part,
            own_v,
        )

        def cont_out_step(span_index, inner):
            return out_add(
                inner,
                far_span(query_part, span_index),
                row_peak,
                row_total,
                grad_part,
                far_values(span_index),
            )

        result, center = lax.fori_loop(lowest, lowest + per_prompt, cont_out_step, start)
        return (result, row_peak.T, row_total.T, center.T)

    def flatten_forward(outputs):
        result, row_peak, row_total, center = outputs
        return (
            result.reshape(row_count, heads_dev, HDIM),
            row_peak.reshape(row_count, heads_dev),
            row_total.reshape(row_count, heads_dev),
            center.reshape(row_count, heads_dev),
        )

    attended, peaks, totals, centers = lax.cond(
        is_prompt,
        lambda: flatten_forward(
            lax.map(prompt_forward, jnp.arange(prompt_blocks, dtype=jnp.int32))
        ),
        lambda: flatten_forward(lax.map(cont_forward, jnp.arange(cont_blocks, dtype=jnp.int32))),
    )
    attended_low = attended.reshape(row_count, local_width).astype(jnp.bfloat16)
    attn_part = jnp.dot(attended_low, dense_weight, preferred_element_type=jnp.float32)
    expand_lin = project(expand_weight, b_fc1)
    activated = gelu_tanh(expand_lin).astype(jnp.bfloat16)
    mlp_part = jnp.dot(activated, shrink_weight, preferred_element_type=jnp.float32)
    branches = lax.psum(attn_part + mlp_part, "tp")
    layer_out = (
        x_float + branches + b_dense.astype(jnp.float32) + b_fc2.astype(jnp.float32)
    ).astype(jnp.bfloat16)
    grad_bias_out = jnp.sum(grad_float, axis=0)
    grad_dense_local = transpose_dot(attended_low, cotangent)
    grad_shrink_local = transpose_dot(activated, cotangent)
    grad_activated = dot_back(cotangent, shrink_weight)
    _, gelu_pull = jax.vjp(gelu_tanh, expand_lin)
    grad_expand = gelu_pull(grad_activated)[0].astype(jnp.bfloat16)
    grad_b_expand = jnp.sum(grad_expand.astype(jnp.float32), axis=0)
    grad_expand_local = transpose_dot(hidden, grad_expand)
    grad_hidden = dot_back(grad_expand, expand_weight)

    def row_stats(first_row, count):
        return tuple(
            (
                lax.dynamic_slice_in_dim(array, first_row, count, 0).T
                for array in (peaks, totals, centers)
            )
        )

    zero_prompt = jnp.zeros((prompt_total, heads_dev, HDIM), jnp.float32)
    zero_own = jnp.zeros((row_count, heads_dev, HDIM), jnp.float32)

    def prompt_backward(running, step_index):
        prompt_gk, prompt_gv = running
        first_row, lowest, highest, query_index, query_part, grad_part = prompt_setup(step_index)
        row_peak, row_total, center = row_stats(first_row, block)

        def prompt_span_step(span_index, inner):
            grad_query, buffer_k, buffer_v = inner
            key_part = lax.dynamic_slice_in_dim(prompt_keys, span_index * block, block, 0)
            scores = prompt_span(query_part, query_index, span_index)
            query_step, key_step, value_step = back_add(
                scores,
                row_peak,
                row_total,
                center,
                query_part,
                grad_part,
                key_part,
                far_values(span_index),
            )
            return (
                grad_query + query_step,
                add_rows(buffer_k, span_index * block, key_step),
                add_rows(buffer_v, span_index * block, value_step),
            )

        grad_query, prompt_gk, prompt_gv = lax.fori_loop(
            lowest,
            highest,
            prompt_span_step,
            (jnp.zeros((block, heads_dev, HDIM), jnp.float32), prompt_gk, prompt_gv),
        )
        return ((prompt_gk, prompt_gv), grad_query)

    def cont_backward(running, step_index):
        prompt_gk, prompt_gv, own_gk, own_gv = running
        first_row, lowest, query_part, grad_part, own_k, own_v = cont_setup(step_index)
        row_peak, row_total, center = row_stats(first_row, CLEN)
        own_scores = scored(query_part, own_k, causal)
        start_query, own_key_step, own_value_step = back_add(
            own_scores, row_peak, row_total, center, query_part, grad_part, own_k, own_v
        )
        own_gk = add_rows(own_gk, first_row, own_key_step)
        own_gv = add_rows(own_gv, first_row, own_value_step)

        def cont_span_step(span_index, inner):
            grad_query, buffer_k, buffer_v = inner
            key_part = lax.dynamic_slice_in_dim(prompt_keys, span_index * block, block, 0)
            query_step, key_step, value_step = back_add(
                far_span(query_part, span_index),
                row_peak,
                row_total,
                center,
                query_part,
                grad_part,
                key_part,
                far_values(span_index),
            )
            return (
                grad_query + query_step,
                add_rows(buffer_k, span_index * block, key_step),
                add_rows(buffer_v, span_index * block, value_step),
            )

        grad_query, prompt_gk, prompt_gv = lax.fori_loop(
            lowest, lowest + per_prompt, cont_span_step, (start_query, prompt_gk, prompt_gv)
        )
        return ((prompt_gk, prompt_gv, own_gk, own_gv), grad_query)

    def prompt_path():
        (prompt_gk, prompt_gv), grad_queries = lax.scan(
            prompt_backward, (zero_prompt, zero_prompt), jnp.arange(prompt_blocks, dtype=jnp.int32)
        )
        return (
            grad_queries.reshape(row_count, heads_dev, HDIM),
            prompt_gk,
            prompt_gv,
            zero_own,
            zero_own,
        )

    def cont_path():
        (prompt_gk, prompt_gv, own_gk, own_gv), grad_queries = lax.scan(
            cont_backward,
            (zero_prompt, zero_prompt, zero_own, zero_own),
            jnp.arange(cont_blocks, dtype=jnp.int32),
        )
        return (
            grad_queries.reshape(row_count, heads_dev, HDIM),
            prompt_gk,
            prompt_gv,
            own_gk,
            own_gv,
        )

    grad_queries, prompt_gk, prompt_gv, own_gk, own_gv = lax.cond(is_prompt, prompt_path, cont_path)
    far_grads = jnp.stack(
        [
            prompt_gk.reshape(holders, row_count, local_width),
            prompt_gv.reshape(holders, row_count, local_width),
        ],
        axis=1,
    )

    def collect(running, holder_index):
        summed = lax.psum(
            lax.dynamic_index_in_dim(far_grads, holder_index, 0, keepdims=False), "ctx"
        )
        return (running + jnp.where(holder_index == ctx_index, summed, 0.0), None)

    returned, _ = lax.scan(
        collect,
        jnp.zeros((2, row_count, local_width), jnp.float32),
        jnp.arange(holders, dtype=jnp.int32),
    )
    key_grad_total = own_gk.reshape(row_count, local_width) + returned[0]
    value_grad_total = own_gv.reshape(row_count, local_width) + returned[1]
    grad_query_lin = (
        rotate_heads(grad_queries, cosine, -sine_table)
        .reshape(row_count, local_width)
        .astype(jnp.bfloat16)
    )
    grad_key_lin = (
        rotate_heads(key_grad_total.reshape(row_count, heads_dev, HDIM), cosine, -sine_table)
        .reshape(row_count, local_width)
        .astype(jnp.bfloat16)
    )
    grad_value_lin = value_grad_total.astype(jnp.bfloat16)
    grad_b_query_local = jnp.sum(grad_query_lin.astype(jnp.float32), axis=0)
    grad_b_key_local = jnp.sum(grad_key_lin.astype(jnp.float32), axis=0)
    grad_b_value_local = jnp.sum(grad_value_lin.astype(jnp.float32), axis=0)
    grad_query_local = transpose_dot(hidden, grad_query_lin)
    grad_key_local = transpose_dot(hidden, grad_key_lin)
    grad_value_local = transpose_dot(hidden, grad_value_lin)
    grad_hidden = (
        grad_hidden
        + dot_back(grad_query_lin, query_weight)
        + dot_back(grad_key_lin, key_weight)
        + dot_back(grad_value_lin, value_weight)
    )
    hidden_total = lax.psum(grad_hidden, "tp")
    _, norm_pull = jax.vjp(norm_apply, x_float, gain_float, shift_float)
    grad_x_norm, grad_gain_local, grad_shift_local = norm_pull(hidden_total)
    grad_tokens = grad_float + grad_x_norm
    small_sums = lax.psum(
        (
            grad_gain_local,
            grad_shift_local,
            grad_b_query_local,
            grad_b_key_local,
            grad_b_value_local,
            grad_b_expand,
            grad_bias_out,
        ),
        ("dp", "ctx"),
    )
    (
        grad_query_out,
        grad_key_out,
        grad_value_out,
        grad_dense_out,
        grad_expand_out,
        grad_shrink_out,
    ) = (
        lax.psum_scatter(grad_query_local, ("dp", "ctx"), scatter_dimension=0, tiled=True),
        lax.psum_scatter(grad_key_local, ("dp", "ctx"), scatter_dimension=0, tiled=True),
        lax.psum_scatter(grad_value_local, ("dp", "ctx"), scatter_dimension=0, tiled=True),
        lax.psum_scatter(grad_dense_local, ("dp", "ctx"), scatter_dimension=1, tiled=True),
        lax.psum_scatter(grad_expand_local, ("dp", "ctx"), scatter_dimension=0, tiled=True),
        lax.psum_scatter(grad_shrink_local, ("dp", "ctx"), scatter_dimension=1, tiled=True),
    )
    return (
        layer_out,
        grad_tokens,
        small_sums[0],
        small_sums[1],
        grad_query_out,
        small_sums[2],
        grad_key_out,
        small_sums[3],
        grad_value_out,
        small_sums[4],
        grad_dense_out,
        small_sums[6],
        grad_expand_out,
        small_sums[5],
        grad_shrink_out,
        small_sums[6],
    )


def solution(mesh):
    placed = (
        P(("dp", "ctx"), None),
        P(("dp", "ctx"), None),
        P("dp", None),
        P(),
        P(),
        P(("dp", "ctx"), "tp"),
        P("tp"),
        P(("dp", "ctx"), "tp"),
        P("tp"),
        P(("dp", "ctx"), "tp"),
        P("tp"),
        P("tp", ("dp", "ctx")),
        P(),
        P(("dp", "ctx"), "tp"),
        P("tp"),
        P("tp", ("dp", "ctx")),
        P(),
    )
    return jax.shard_map(
        body,
        mesh=mesh,
        in_specs=placed,
        out_specs=(
            P(("dp", "ctx"), None),
            P(("dp", "ctx"), None),
            P(),
            P(),
            P(("dp", "ctx"), "tp"),
            P("tp"),
            P(("dp", "ctx"), "tp"),
            P("tp"),
            P(("dp", "ctx"), "tp"),
            P("tp"),
            P("tp", ("dp", "ctx")),
            P(),
            P(("dp", "ctx"), "tp"),
            P("tp"),
            P("tp", ("dp", "ctx")),
            P(),
        ),
        check_vma=False,
    )
```

profile of v0, /device:TPU:0, one launch (start us, length us, event | category | flops | bytes accessed | tf_op | source)
XLA Modules:
  0.0 5364.2 jit_solution(10879168385648474379)
XLA Ops:
  144.7 186.3 %all-reduce.6.cloned.1.call-done = bf16[1,2,4096,512]{2,3,1,0:T(8,128)(2,1)} async-done(((bf16[1,2,4096,512]{2,3,1,0:T(8,128)(2,1)}), bf16[1,2,4096,512]{2,3,1,0:T(8,128)(2,1)}) %all-reduce.6.cloned.1.call-update) | async-done | bytes 8388624 | tf_op jit(solution)/shard_map/while/body/eval_jaxpr/psum | solution.py:15
  337.6 342.6 %conditional.4 = (f32[4096,8]{1,0:T(8,128)}, f32[4096,8]{1,0:T(8,128)}, f32[4096,8]{1,0:T(8,128)S(1)}, bf16[4096,512]{0,1:T(8,128)(2,1)S(1)}) conditional(s32[]{:T(128)} %convert_element_type.145, (s32[]{:T(128)}, s32[16]{0:T(128)}, bf16[4096,8,64]{0,2,1:T(8,128)(2,1)}, pred[256,256]{1,0:T(8,128)(4,1)S(1)}, bf16[4096,8,64]{0,2,1:T(8,128)(2,1)}, ...), branch_computations={%region_3.16_spmd, %region_16.26_spmd} | conditional | flops 1103898112 | bytes 72308352
  337.9 330.5 %while.217 = (s32[]{:T(128)}, bf16[8,512,8,64]{1,3,2,0:T(8,128)(2,1)}, f32[8,512,8]{1,2,0:T(8,128)S(1)}, f32[8,512,8]{1,2,0:T(8,128)S(1)}, f32[8,512,8]{1,2,0:T(...) while((s32[]{:T(128)}, ...), condition=%wide.region_25.25_spmd, body=%wide.region_17.24_spmd.sunk | while | flops 1103898112 | bytes 54744344 | solution.py:314
  465.9 36.6 while.227
  630.7 36.6 while.227
  682.3 454.7 %conditional.5 = (f32[4096,8,64]{0,2,1:T(8,128)}, f32[4096,8,64]{0,2,1:T(8,128)}, f32[4096,8,64]{0,2,1:T(8,128)}, f32[4096,8,64]{0,2,1:T(8,128)}, f32[4096,8,16]...) conditional(s32[]{:T(128)} %convert_element_type.145, (s32[]{:T(128)}, ...), branch_computations={%region_27.32_spmd.clone, %region_32.37_spmd.clone} | conditional | flops 1360528384 | bytes 129930632 | solution.py:442
  709.8 343.1 %while.223 = (s32[]{:T(128)}, f32[4096,8,64]{0,2,1:T(8,128)}, f32[4096,8,64]{0,2,1:T(8,128)}, f32[8,512,8,64]{1,3,2,0:T(8,128)}, s32[8]{0:T(128)S(1)}, /*index=5...) while((s32[]{:T(128)}, f32[4096,8,64]{0,2,1:T(8,128)}, ...), condition=%wide.region_36.36_spmd, body=%wide.region_33.35_spmd.sunk | while | flops 1360528384 | bytes 53638148 | solution.py:417
  767.2 47.0 while.224
  818.0 62.6 %while.224 = (s32[]{:T(128)}, f32[512,8,64]{0,2,1:T(8,128)S(1)}, f32[4096,8,64]{0,2,1:T(8,128)}, f32[4096,8,64]{0,2,1:T(8,128)}, s32[]{:T(128)}, /*index=5*/bf16...) while((s32[]{:T(128)}, f32[512,8,64]{0,2,1:T(8,128)S(1)}, ...), condition=%wide.region_35.34_spmd, body=%wide.region_34.33_spmd.sunk | while | flops 1360527872 | bytes 48292076 | solution.py:373
  939.0 46.6 while.224
  989.5 62.2 %while.224 = (s32[]{:T(128)}, f32[512,8,64]{0,2,1:T(8,128)S(1)}, f32[4096,8,64]{0,2,1:T(8,128)}, f32[4096,8,64]{0,2,1:T(8,128)}, s32[]{:T(128)}, /*index=5*/bf16...) while((s32[]{:T(128)}, f32[512,8,64]{0,2,1:T(8,128)S(1)}, ...), condition=%wide.region_35.34_spmd, body=%wide.region_34.33_spmd.sunk | while | flops 1360527872 | bytes 48292076 | solution.py:373
  1169.5 43.2 fusion.152
  1212.6 49.9 convolution_add_fusion
  1262.6 64.1 %convert_reduce_fusion.2 = (f32[2048]{0:T(1024)}, bf16[4096,2048]{1,0:T(8,128)(2,1)}) fusion(f32[4096,2048]{1,0:T(8,128)} %fusion.152, f32[2048]{0:T(1024)S(1)} %copy-done.31, bf16[4096,2048]{1,0:T(8,128)(2,1)} %param.42, bf16[2048,2048]{1,0:T(8,128)(2,1)} %all-gather.17.cloned.1.call-done), kind=kOutput, calls=%fused_computation.180 | convolution fusion | flops 34552676352 | bytes 75513856 | tf_op jit(solution)/shard_map/rb,ab->ra/dot_general | solution.py:54
  1326.7 1216.8 %all-reduce.8.cloned.1.call-done = f32[2,4096,512]{1,2,0:T(8,128)} async-done(((f32[2,4096,512]{1,2,0:T(8,128)}), f32[2,4096,512]{1,2,0:T(8,128)}) %all-reduce.8.cloned.1.call-update) | async-done | bytes 16777232 | tf_op jit(solution)/shard_map/while/body/eval_jaxpr/psum | solution.py:452
  2642.3 61.3 %add_add_fusion.1 = f32[4096,2048]{1,0:T(8,128)} fusion(f32[4096,2048]{1,0:T(8,128)} %fusion.155, f32[4096,2048]{1,0:T(8,128)} %fusion.154, f32[4096,2048]{1,0:T(8,128)} %fusion.153, bf16[4096,2048]{1,0:T(8,128)(2,1)} %get-tuple-element.1593, bf16[2048,2048]{1,0:T(8,128)(2,1)} %all-gather.15.cloned.1.call-done), kind=kOutput, calls=%fused_computation.181 | convolution fusion | flops 34384904192 | bytes 159383552 | tf_op jit(solution)/shard_map/rb,ab->ra/dot_general | solution.py:54
  2764.7 43.7 fusion.160
  2809.0 50.9 fusion.143
  2867.7 2027.4 %all-reduce.10.cloned.1.call-done = (f32[4096,2048]{1,0:T(8,128)}, f32[4096,2048]{1,0:T(8,128)}) async-done(((f32[4096,2048]{1,0:T(8,128)}, f32[4096,2048]{1,0:T(8,128)}), (f32[4096,2048]{1,0:T(8,128)}, f32[4096,2048]{1,0:T(8,128)})) %all-reduce.10.cloned.1.call-update) | async-done | bytes 67108880 | tf_op jit(solution)/shard_map/psum | solution.py:323
  4938.2 51.4 convert_reduce_fusion.1
  5014.8 46.0 reduce-scatter.7.cloned.1.call-done
  5060.8 55.3 %reduce-scatter.11.cloned.1.call-done = f32[256,512]{1,0:T(8,128)} async-done(((f32[2048,512]{1,0:T(8,128)}), f32[256,512]{1,0:T(8,128)}) %reduce-scatter.11.cloned.1.call-update) | async-done | bytes 524304 | tf_op jit(solution)/shard_map/reduce_scatter | solution.py:513
  5116.1 120.4 %reduce-scatter.15.cloned.1.call-done = f32[256,2048]{1,0:T(8,128)} async-done(((f32[2048,2048]{1,0:T(8,128)}), f32[256,2048]{1,0:T(8,128)}) %reduce-scatter.15.cloned.1.call-update) | async-done | bytes 2097168 | tf_op jit(solution)/shard_map/reduce_scatter | solution.py:515
  5236.5 120.4 %reduce-scatter.17.cloned.1.call-done = f32[2048,256]{1,0:T(8,128)} async-done(((f32[2048,2048]{1,0:T(8,128)}), f32[2048,256]{1,0:T(8,128)}) %reduce-scatter.17.cloned.1.call-update) | async-done | bytes 2097168 | tf_op jit(solution)/shard_map/reduce_scatter | solution.py:516
  (767 shorter events, 1490.1 us)
Async XLA Ops:
  7.2 36.0 all-gather.11.cloned.1.call-start
  7.9 62.4 %all-gather.9.cloned.1.call-start = ((), (), s32[]{:S(2)}) async-start(), calls=%async_computation.7 | async-start | bytes 2359296 | tf_op jit(solution)/shard_map/all_gather | solution.py:132
  8.7 91.5 %all-gather.7.cloned.1.call-start = ((), (), s32[]{:S(2)}) async-start(), calls=%async_computation.6 | async-start | bytes 2359296 | tf_op jit(solution)/shard_map/all_gather | solution.py:134
  9.4 120.7 %all-gather.13.cloned.1.call-start = ((), (), s32[]{:S(2)}) async-start(), calls=%async_computation.10 | async-start | bytes 2359296 | tf_op jit(solution)/shard_map/all_gather | solution.py:135
  10.0 321.0 %all-reduce.6.cloned.1.call-start = ((), (), s32[]{:S(2)}) async-start(), calls=%async_computation.9 | async-start | bytes 16777216 | tf_op jit(solution)/shard_map/while/body/eval_jaxpr/psum | solution.py:15
  33.4 52.6 copy-start.12
  121.1 1048.4 %all-gather.15.cloned.1.call-start = ((), (), s32[]{:S(2)}) async-start(), calls=%async_computation.11 | async-start | bytes 9437184 | tf_op jit(solution)/shard_map/all_gather | solution.py:136
  121.6 1091.0 %all-gather.17.cloned.1.call-start = ((), (), s32[]{:S(2)}) async-start(), calls=%async_computation.12 | async-start | bytes 9437184 | tf_op jit(solution)/shard_map/all_gather | solution.py:137
  122.4 2421.1 %all-reduce.8.cloned.1.call-start = ((), (), s32[]{:S(2)}) async-start(), calls=%async_computation.13 | async-start | bytes 33554432 | tf_op jit(solution)/shard_map/while/body/eval_jaxpr/psum | solution.py:452
  123.1 214.5 %copy-start.22 = (pred[256,256]{1,0:T(8,128)(4,1)}, pred[256,256]{1,0:T(8,128)(4,1)S(1)}, u32[]{:S(2)}) copy-start(pred[256,256]{1,0:T(8,128)(4,1)S(1)} %iota_compare_fusion) | copy-start | bytes 196612
  1149.4 3745.7 %all-reduce.10.cloned.1.call-start = ((), (), s32[]{:S(2)}) async-start(), calls=%async_computation.20 | async-start | bytes 134217728 | tf_op jit(solution)/shard_map/psum | solution.py:323
  1169.4 43.2 copy-start.31
  2590.9 35.9 copy-start.11
  2703.6 2311.2 %reduce-scatter.13.cloned.1.call-start = ((), (), s32[]{:S(2)}) async-start(), calls=%async_computation.17 | async-start | bytes 4718592 | tf_op jit(solution)/shard_map/reduce_scatter | solution.py:514
  2718.7 2296.1 %reduce-scatter.9.cloned.1.call-start = ((), (), s32[]{:S(2)}) async-start(), calls=%async_computation.15 | async-start | bytes 4718592 | tf_op jit(solution)/shard_map/reduce_scatter | solution.py:512
  2734.0 2326.8 %reduce-scatter.7.cloned.1.call-start = ((), (), s32[]{:S(2)}) async-start(), calls=%async_computation.14 | async-start | bytes 4718592 | tf_op jit(solution)/shard_map/reduce_scatter | solution.py:511
  2749.1 2367.0 %reduce-scatter.11.cloned.1.call-start = ((), (), s32[]{:S(2)}) async-start(), calls=%async_computation.16 | async-start | bytes 4718592 | tf_op jit(solution)/shard_map/reduce_scatter | solution.py:513
  2764.6 2471.9 %reduce-scatter.15.cloned.1.call-start = ((), (), s32[]{:S(2)}) async-start(), calls=%async_computation.18 | async-start | bytes 18874368 | tf_op jit(solution)/shard_map/reduce_scatter | solution.py:515
  2808.4 2548.5 %reduce-scatter.17.cloned.1.call-start = ((), (), s32[]{:S(2)}) async-start(), calls=%async_computation.19 | async-start | bytes 18874368 | tf_op jit(solution)/shard_map/reduce_scatter | solution.py:516
  2860.7 2034.5 %copy-start.19 = (f32[4096]{0:T(1024)S(1)}, f32[4096]{0:T(1024)}, u32[]{:S(2)}) copy-start(f32[4096]{0:T(1024)} %copy-done.18) | copy-start | bytes 49156
  2860.7 2034.4 %copy-start.25 = (f32[2048]{0:T(1024)S(1)}, f32[2048]{0:T(1024)}, u32[]{:S(2)}) copy-start(f32[2048]{0:T(1024)} %copy-done.24) | copy-start | bytes 24580
  4895.1 23.5 slice-start
  4938.2 51.5 copy-start.30
  5014.8 342.7 %copy-start.33 = (f32[2048]{0:T(1024)}, f32[2048]{0:T(1024)S(1)}, u32[]{:S(2)}) copy-start(f32[2048]{0:T(1024)S(1)} %get-tuple-element.3279) | copy-start | bytes 24580
  (33 other events, 370.0 us)
Sparse Core Ops, SparseCore 0:
  9.9 30.5 all-gather.10
  42.4 27.8 all-gather.8
  72.2 27.8 all-gather.6
  101.9 28.1 all-gather.12
  133.0 197.9 all-reduce.5
  332.8 54.7 all-gather.14
  389.4 55.9 all-gather.16
  1149.5 1393.9 all-reduce.7
  2703.7 2191.3 all-reduce.9
  4899.3 50.2 reduce-scatter.12
  4953.5 51.7 reduce-scatter.8
  5009.4 51.2 reduce-scatter.6
  5064.7 51.3 reduce-scatter.10
  5120.5 115.9 reduce-scatter.14
  5240.9 115.9 reduce-scatter.16
where the time goes:
time: 5400 us; the launch traced here: 5360 us
  waiting for transfers between devices  3790 us (70%)
  matrix products  1030 us (19%)
  other arithmetic  274 us (5%)
  local copies, waits for them, and re-layouts  199 us (4%)
    psum x1, waiting for transfers between devices, body(): branches = lax.psum(attn_part + mlp_part, 'tp')  2030 us
    psum x1, waiting for transfers between devices, collect(): lax.psum(lax.dynamic_index_in_dim(far_grads, holder_index, 0, keepdims=Fa...  1220 us
    dot_general x60, matrix products, scored(): jnp.einsum('qhd,khd->hqk', query_part, key_part, preferred_element_type=j...  202 us
    dot_general x6, matrix products, dot_back(): jnp.einsum('rb,ab->ra', left, right, preferred_element_type=jnp.float32)  191 us
    psum x1, waiting for transfers between devices, broadcast(): return lax.psum(block, axis)  186 us
    dot_general x6, matrix products, transpose_dot(): jnp.einsum('ra,rb->ab', left, right, preferred_element_type=jnp.float32)  155 us
    reduce_scatter x1, waiting for transfers between devices, body(): lax.psum_scatter(grad_expand_local, ('dp', 'ctx'), scatter_dimension=0, t...  120 us
    reduce_scatter x1, waiting for transfers between devices, body(): lax.psum_scatter(grad_shrink_local, ('dp', 'ctx'), scatter_dimension=1, t...  120 us
  transfers between devices with their start and end apart: 15, of which 10 were waited for; matrix products, arithmetic and copies ran while one was open for 25% of the time, Pallas kernels for 0%

commit v1 on v0

v1 whole, which is shorter than its diff:
```python
import functools

import jax
import jax.numpy as jnp
from jax import lax
from jax.experimental import pallas as pl
from jax.experimental.pallas import tpu as pltpu
from jax.sharding import PartitionSpec as P

HDIM = 64
ROT = 32
PLEN = 2048
CLEN = 256
GPR = 2
ROWS_OUT = 1024
VMEM = 56 * 2**20
F32 = jnp.float32
BF16 = jnp.bfloat16
NT = (((1,), (1,)), ((), ()))
NN = (((1,), (0,)), ((), ()))


def dot(left, right, dims):
    return lax.dot_general(left, right, dims, preferred_element_type=F32)


def transpose_dot(left, right):
    return jnp.einsum("ra,rb->ab", left, right, preferred_element_type=F32)


def dot_back(left, right):
    return jnp.einsum("rb,ab->ra", left, right, preferred_element_type=F32)


def norm_apply(matrix, norm_gain, norm_shift):
    center = matrix - jnp.mean(matrix, axis=-1, keepdims=True)
    spread = jnp.mean(center * center, axis=-1, keepdims=True)
    return center * lax.rsqrt(spread + 1e-05) * norm_gain + norm_shift


def gelu_tanh(inputs):
    return jax.nn.gelu(inputs, approximate=True)


def rotary_tables():
    half = ROT // 2
    positions = jnp.arange(PLEN + CLEN, dtype=F32)
    frequency = 10000.0 ** (-2.0 * jnp.arange(half, dtype=F32) / ROT)
    angles = positions[:, None] * frequency[None, :]
    cosine, sine = jnp.cos(angles), jnp.sin(angles)
    ones = jnp.ones((PLEN + CLEN, HDIM - ROT), F32)
    zeros = jnp.zeros_like(ones)
    none = jnp.zeros_like(sine)
    head = (
        jnp.concatenate([cosine, cosine, ones], axis=1),
        jnp.concatenate([-sine, none, zeros], axis=1),
        jnp.concatenate([none, sine, zeros], axis=1),
    )
    return tuple(jnp.concatenate([table, table], axis=1) for table in head)


def rotated(values, cosine, first, second):
    half = ROT // 2
    return (
        values * cosine
        + pltpu.roll(values, 2 * HDIM - half, 1) * first
        + pltpu.roll(values, half, 1) * second
    )


def qkv_kernel(
    share, where_ref, x_ref, gain_ref, shift_ref, weight_ref, bias_ref, cos_ref, first_ref,
    second_ref, hidden_ref, out_ref,
):
    x = x_ref[...].astype(F32)
    hidden = norm_apply(x, gain_ref[...], shift_ref[...]).astype(BF16)
    hidden_ref[...] = hidden
    cosine, first, second = cos_ref[...], first_ref[...], second_ref[...]
    lane = lax.broadcasted_iota(jnp.int32, (1, 2 * HDIM), 1)
    for begin in range(0, out_ref.shape[1], 512):
        lin = dot(hidden, weight_ref[:, begin : begin + 512], NN) + bias_ref[:, begin : begin + 512]
        for column in range(0, 512, 2 * HDIM):
            part = lin[:, column : column + 2 * HDIM]
            turns = [((begin + column + off) // share) % 3 < 2 for off in (0, HDIM)]
            if any(turns):
                turned = rotated(part, cosine, first, second)
                if not all(turns):
                    keep = lane < HDIM if turns[0] else lane >= HDIM
                    turned = jnp.where(keep, turned, part)
                part = turned
            out_ref[:, begin + column : begin + column + 2 * HDIM] = part.astype(BF16)


def qkv_project(x, gain, shift, weight, bias, tables, spots, share):
    rows, width = x.shape
    outs = weight.shape[1]
    count = 256
    whole = lambda shape: pl.BlockSpec(shape, lambda i, *_: (0, 0))
    table = pl.BlockSpec((count, 2 * HDIM), lambda i, spots: (spots[i], 0))
    return pl.pallas_call(
        functools.partial(qkv_kernel, share),
        grid_spec=pltpu.PrefetchScalarGridSpec(
            num_scalar_prefetch=1,
            grid=(rows // count,),
            in_specs=[
                pl.BlockSpec((count, width), lambda i, *_: (i, 0)),
                whole((1, width)),
                whole((1, width)),
                whole((width, outs)),
                whole((1, outs)),
                table,
                table,
                table,
            ],
            out_specs=[
                pl.BlockSpec((count, width), lambda i, *_: (i, 0)),
                pl.BlockSpec((count, outs), lambda i, *_: (i, 0)),
            ],
        ),
        out_shape=[
            jax.ShapeDtypeStruct((rows, width), BF16),
            jax.ShapeDtypeStruct((rows, outs), BF16),
        ],
        compiler_params=pltpu.CompilerParams(vmem_limit_bytes=VMEM),
        cost_estimate=pl.CostEstimate(
            flops=2 * rows * width * outs, bytes_accessed=2 * rows * (2 * width + outs),
            transcendentals=0,
        ),
        name="qkv_project",
    )(spots, x, gain, shift, weight, bias, *tables)


def heads_split(array, heads):
    if heads == 1:
        return [array]
    lane = lax.broadcasted_iota(jnp.int32, array.shape, 1)
    return [jnp.where(lane // HDIM == h, array, jnp.zeros((), array.dtype)) for h in range(heads)]


def near_mask():
    key = lax.broadcasted_iota(jnp.int32, (CLEN, CLEN), 0)
    query = lax.broadcasted_iota(jnp.int32, (CLEN, CLEN), 1)
    return key <= query


def over_far(base, count, big, step):
    per = big // CLEN
    full = count // per

    @pl.loop(0, full)
    def _(i):
        step(pl.multiple_of(base + i * big, CLEN), big)

    @pl.loop(full * per, count)
    def _(i):
        step(pl.multiple_of(base + i * CLEN, CLEN), CLEN)


def attend_kernel(
    big, group_ref, far_ref, q_ref, ko_ref, vo_ref, kp_ref, vp_ref, o_ref, ot_ref, lse_ref,
    vt_s, m_s, l_s, acc_s,
):
    heads = q_ref.shape[1] // HDIM
    item = pl.program_id(1)
    base = group_ref[item] * PLEN

    @pl.when(item == 0)
    def _():
        @pl.loop(0, vp_ref.shape[0] // CLEN)
        def _(i):
            rows = pl.ds(pl.multiple_of(i * CLEN, CLEN), CLEN)
            vt_s[:, rows] = vp_ref[rows, :].T

    queries = heads_split(q_ref[...] * BF16(HDIM**-0.5), heads)
    mask = near_mask()
    keys = ko_ref[...]
    values = vo_ref[...].T
    spans = [slice(h * HDIM, (h + 1) * HDIM) for h in range(heads)]
    scores = [dot(keys, queries[h], NT) for h in range(heads)]
    for h in range(heads):
        s = jnp.where(mask, scores[h], -1e30)
        m = jnp.max(s, axis=0, keepdims=True)
        p = jnp.exp(s - m)
        m_s[h] = m
        l_s[h] = jnp.sum(p, axis=0, keepdims=True)
        acc_s[h] = dot(values[spans[h]], p.astype(BF16), NN)

    def step(first, size):
        k = kp_ref[pl.ds(first, size), :]
        scores = [dot(k, queries[h], NT) for h in range(heads)]
        for h in range(heads):
            old = m_s[h]
            m = jnp.maximum(old, jnp.max(scores[h], axis=0, keepdims=True))
            p = jnp.exp(scores[h] - m)
            a = jnp.exp(old - m)
            m_s[h] = m
            l_s[h] = l_s[h] * a + jnp.sum(p, axis=0, keepdims=True)
            acc_s[h] = acc_s[h] * a + dot(vt_s[spans[h], pl.ds(first, size)], p.astype(BF16), NN)

    over_far(base, far_ref[item], big, step)
    for h in range(heads):
        ot_ref[spans[h], :] = acc_s[h] * (1.0 / l_s[h])
        lse_ref[0, h : h + 1, :] = m_s[h] + jnp.log(l_s[h])
    o_ref[...] = ot_ref[...].T.astype(BF16)


def attend_back_kernel(
    big, group_ref, far_ref, spot_ref, q_ref, ko_ref, vo_ref, do_ref, ot_ref, lse_ref, kp_ref,
    vp_ref, cos_ref, first_ref, second_ref, dq_ref, dk_ref, dv_ref, kt_s, dq_s, dk_s, dv_s,
):
    width = q_ref.shape[1]
    heads = width // HDIM
    item = pl.program_id(1)
    base = group_ref[item] * PLEN

    @pl.when(item == 0)
    def _():
        dk_s[...] = jnp.zeros_like(dk_s)
        dv_s[...] = jnp.zeros_like(dv_s)

        @pl.loop(0, kp_ref.shape[0] // CLEN)
        def _(i):
            rows = pl.ds(pl.multiple_of(i * CLEN, CLEN), CLEN)
            kt_s[:, rows] = kp_ref[rows, :].T

    do = do_ref[...]
    queries = heads_split(q_ref[...] * BF16(HDIM**-0.5), heads)
    grads = heads_split(do, heads)
    query_cat = jnp.concatenate(queries, axis=0)
    grad_cat = jnp.concatenate(grads, axis=0)
    spans = [slice(h * HDIM, (h + 1) * HDIM) for h in range(heads)]
    product = ot_ref[...] * do.astype(F32).T
    center = [jnp.sum(product[span], axis=0, keepdims=True) for span in spans]
    lse = [lse_ref[0, h : h + 1, :] for h in range(heads)]
    mask = near_mask()

    def piece(k, v, kt, row, size, near):
        chance, grad_scores = [], []
        scores = [dot(k, queries[h], NT) for h in range(heads)]
        grad_chance = [dot(v, grads[h], NT) for h in range(heads)]
        for h in range(heads):
            p = jnp.exp(scores[h] - lse[h])
            if near:
                p = jnp.where(mask, p, 0.0)
            grad_scores.append((p * (grad_chance[h] - center[h])).astype(BF16))
            chance.append(p.astype(BF16))
        for h in range(heads):
            step = dot(kt(spans[h]), grad_scores[h], NN)
            if near:
                dq_s[spans[h], :] = step
            else:
                dq_s[spans[h], :] += step
        dk_s[pl.ds(row, size), :] += dot(jnp.concatenate(grad_scores, axis=1), query_cat, NN)
        dv_s[pl.ds(row, size), :] += dot(jnp.concatenate(chance, axis=1), grad_cat, NN)

    own = ko_ref[...]
    own_t = own.T
    piece(
        own, vo_ref[...], lambda span: own_t[span], pl.multiple_of(item * CLEN, CLEN), CLEN, True
    )

    def step(first, size):
        rows = pl.ds(first, size)
        piece(kp_ref[rows, :], vp_ref[rows, :], lambda span: kt_s[span, rows], first, size, False)

    over_far(base, far_ref[item], big, step)

    def turned_back(values, spot):
        rows = pl.ds(pl.multiple_of(spot * CLEN, CLEN), CLEN)
        wide = 2 * HDIM
        if width < wide:
            values = jnp.concatenate([values, values], axis=1)
        parts = [
            rotated(
                values[:, c : c + wide], cos_ref[rows, :], -first_ref[rows, :], -second_ref[rows, :]
            )
            for c in range(0, values.shape[1], wide)
        ]
        out = parts[0] if len(parts) == 1 else jnp.concatenate(parts, axis=1)
        return out[:, :width].astype(BF16)

    dq_ref[...] = turned_back((dq_s[...] * (HDIM**-0.5)).T, spot_ref[item])

    @pl.when(item == pl.num_programs(1) - 1)
    def _():
        @pl.loop(0, dk_ref.shape[0] // CLEN)
        def _(i):
            rows = pl.ds(pl.multiple_of(i * CLEN, CLEN), CLEN)
            dk_ref[rows, :] = turned_back(dk_s[rows, :], spot_ref[i])
            dv_ref[rows, :] = dv_s[rows, :].astype(BF16)


def attention_specs(rows, width):
    wide = min(4 * HDIM, width)
    heads = wide // HDIM
    block = lambda at: pl.BlockSpec((CLEN, wide), lambda h, i, *_: (i, at + h))
    return (
        wide,
        heads,
        block,
        pl.BlockSpec((wide, CLEN), lambda h, i, *_: (h, i)),
        lambda at: pl.BlockSpec((GPR * PLEN, wide), lambda h, i, *_: (0, at + h)),
        pl.BlockSpec((1, heads, CLEN), lambda h, i, *_: (h, 0, i)),
    )


def split_columns(qkv, width):
    wide = min(4 * HDIM, width)
    if wide % 128 == 0:
        return (qkv, qkv, qkv), tuple(t * width // wide for t in range(3))
    return tuple(qkv[:, t * width : (t + 1) * width] for t in range(3)), (0, 0, 0)


def attend(qkv, width, group, far):
    rows = qkv.shape[0]
    wide, heads, block, turned, prompts, stats = attention_specs(rows, width)
    (q, k, v), (qa, ka, va) = split_columns(qkv, width)
    pairs = rows * (PLEN + CLEN) * width // HDIM
    return pl.pallas_call(
        functools.partial(attend_kernel, 1024),
        grid_spec=pltpu.PrefetchScalarGridSpec(
            num_scalar_prefetch=2,
            grid=(width // wide, rows // CLEN),
            in_specs=[block(qa), block(ka), block(va), prompts(ka), prompts(va)],
            out_specs=[block(0), turned, stats],
            scratch_shapes=[
                pltpu.VMEM((wide, GPR * PLEN), BF16),
                pltpu.VMEM((heads, 1, CLEN), F32),
                pltpu.VMEM((heads, 1, CLEN), F32),
                pltpu.VMEM((heads, HDIM, CLEN), F32),
            ],
        ),
        out_shape=[
            jax.ShapeDtypeStruct((rows, width), BF16),
            jax.ShapeDtypeStruct((width, rows), F32),
            jax.ShapeDtypeStruct((width // wide, heads, rows), F32),
        ],
        compiler_params=pltpu.CompilerParams(vmem_limit_bytes=VMEM),
        cost_estimate=pl.CostEstimate(
            flops=4 * pairs * 256, bytes_accessed=rows * width * 12, transcendentals=pairs
        ),
        name="attend",
    )(group, far, q, k, v, k, v)


def attend_back(qkv, width, grad, turned_out, lse, tables, group, far, spots):
    rows = qkv.shape[0]
    wide, heads, block, turned, prompts, stats = attention_specs(rows, width)
    (q, k, v), (qa, ka, va) = split_columns(qkv, width)
    table = pl.BlockSpec(tables[0].shape, lambda h, i, *_: (0, 0))
    column = pl.BlockSpec((rows, wide), lambda h, i, *_: (0, h))
    pairs = rows * (PLEN + CLEN) * width // HDIM
    return pl.pallas_call(
        functools.partial(attend_back_kernel, 1024),
        grid_spec=pltpu.PrefetchScalarGridSpec(
            num_scalar_prefetch=3,
            grid=(width // wide, rows // CLEN),
            in_specs=[
                block(qa), block(ka), block(va), block(0), turned, stats, prompts(ka), prompts(va),
                table, table, table,
            ],
            out_specs=[block(0), column, column],
            scratch_shapes=[
                pltpu.VMEM((wide, GPR * PLEN), BF16),
                pltpu.VMEM((wide, CLEN), F32),
                pltpu.VMEM((rows, wide), F32),
                pltpu.VMEM((rows, wide), F32),
            ],
        ),
        out_shape=[jax.ShapeDtypeStruct((rows, width), BF16)] * 3,
        compiler_params=pltpu.CompilerParams(vmem_limit_bytes=VMEM),
        cost_estimate=pl.CostEstimate(
            flops=8 * pairs * 256, bytes_accessed=rows * width * 24, transcendentals=pairs
        ),
        name="attend_back",
    )(group, far, spots, q, k, v, grad, turned_out, lse, k, v, *tables)


def tp_sum(part, extra=None):
    total = lax.psum(part, "tp").astype(F32)
    if extra is not None:
        total = total + extra[0].astype(F32) + extra[1]
    return total.astype(BF16)


def body(
    tokens, cotangent, membership, ln_gain, ln_bias, w_query, b_query, w_key, b_key, w_value,
    b_value, w_dense, b_dense, w_fc1, b_fc1, w_fc2, b_fc2,
):
    rows, width = tokens.shape
    ctx_count = lax.axis_size("ctx")
    ctx_index = lax.axis_index("ctx")
    local = w_query.shape[1]
    share = local // ctx_count

    def mixed(query, key, value):
        lead = query.shape[:-1]
        stacked = jnp.stack(
            [a.reshape(*lead, ctx_count, share) for a in (query, key, value)], axis=-2
        )
        return stacked.reshape(*lead, 3 * local)

    gather = functools.partial(lax.all_gather, axis_name=("dp", "ctx"), tiled=True)
    qkv_weight = gather(mixed(w_query, w_key, w_value), axis=0)
    dense_weight = gather(w_dense, axis=1)
    expand_weight = gather(w_fc1, axis=0)
    shrink_weight = gather(w_fc2, axis=1)
    qkv_bias = mixed(b_query, b_key, b_value).astype(F32)[None]

    per_prompt = PLEN // CLEN
    prompt_items = GPR * per_prompt
    all_items = rows * ctx_count // CLEN
    items = jnp.arange(all_items, dtype=jnp.int32)
    spots = jnp.where(items < prompt_items, items % per_prompt, per_prompt)
    far = spots
    group = jnp.concatenate([items[:prompt_items] // per_prompt, membership[0]])
    own_spots = lax.dynamic_slice_in_dim(spots, ctx_index * (rows // CLEN), rows // CLEN)
    tables = rotary_tables()

    gain = ln_gain.astype(F32)
    shift = ln_bias.astype(F32)
    hidden, qkv = qkv_project(
        tokens, gain[None], shift[None], qkv_weight, qkv_bias, tables, own_spots, share
    )
    swap = functools.partial(lax.all_to_all, axis_name="ctx", tiled=True)
    qkv_all = swap(qkv, split_axis=1, concat_axis=0)
    grad_attended = dot_back(cotangent, dense_weight).astype(BF16)
    grad_all = swap(grad_attended, split_axis=1, concat_axis=0)

    out_all, turned_out, lse = attend(qkv_all, share, group, far)
    attended = swap(out_all, split_axis=0, concat_axis=1)
    grads_all = attend_back(
        qkv_all, share, grad_all, turned_out, lse, tables, group, far, spots
    )
    grad_qkv = swap(jnp.concatenate(grads_all, axis=1), split_axis=0, concat_axis=1)

    expand_lin = jnp.dot(hidden, expand_weight, preferred_element_type=F32) + b_fc1.astype(F32)
    activated = gelu_tanh(expand_lin).astype(BF16)
    _, gelu_pull = jax.vjp(gelu_tanh, expand_lin)
    grad_expand = gelu_pull(dot_back(cotangent, shrink_weight))[0].astype(BF16)

    blocks = rows // ROWS_OUT
    cut = lambda array, i: array[i * ROWS_OUT : (i + 1) * ROWS_OUT]
    biases = b_dense.astype(F32) + b_fc2.astype(F32)
    outs = []
    for i in range(blocks):
        part = jnp.dot(cut(attended, i), dense_weight, preferred_element_type=F32) + jnp.dot(
            cut(activated, i), shrink_weight, preferred_element_type=F32
        )
        outs.append(tp_sum(part.astype(BF16), (cut(tokens, i), biases)))
    layer_out = jnp.concatenate(outs, axis=0)

    sums = []
    for i in range(blocks):
        part = dot_back(cut(grad_expand, i), expand_weight) + dot_back(cut(grad_qkv, i), qkv_weight)
        sums.append(tp_sum(part.astype(BF16)))
    hidden_total = jnp.concatenate(sums, axis=0).astype(F32)
    _, norm_pull = jax.vjp(norm_apply, tokens.astype(F32), gain, shift)
    grad_x, grad_gain, grad_shift = norm_pull(hidden_total)
    grad_tokens = cotangent.astype(F32) + grad_x

    small = (
        grad_gain,
        grad_shift,
        jnp.sum(grad_qkv.astype(F32), axis=0),
        jnp.sum(grad_expand.astype(F32), axis=0),
        jnp.sum(cotangent.astype(F32), axis=0),
    )
    sizes = [array.shape[0] for array in small]
    packed = lax.psum(jnp.concatenate(small), ("dp", "ctx"))
    ends = [sum(sizes[: i + 1]) for i in range(len(sizes))]
    gain_sum, shift_sum, qkv_sum, expand_sum, out_sum = (
        packed[end - size : end] for end, size in zip(ends, sizes)
    )

    def scatter(array, axis):
        summed = lax.psum_scatter(
            array.astype(BF16), ("dp", "ctx"), scatter_dimension=axis, tiled=True
        )
        return summed.astype(F32)

    def unmixed(array):
        lead = array.shape[:-1]
        parts = array.reshape(*lead, ctx_count, 3, share)
        return tuple(parts[..., t, :].reshape(*lead, local) for t in range(3))

    grad_query, grad_key, grad_value = unmixed(scatter(transpose_dot(hidden, grad_qkv), 0))
    grad_dense = scatter(transpose_dot(attended, cotangent), 1)
    grad_fc1 = scatter(transpose_dot(hidden, grad_expand), 0)
    grad_fc2 = scatter(transpose_dot(activated, cotangent), 1)
    sum_query, sum_key, sum_value = unmixed(qkv_sum)
    return (
        layer_out, grad_tokens, gain_sum, shift_sum, grad_query, sum_query, grad_key, sum_key,
        grad_value, sum_value, grad_dense, out_sum, grad_fc1, expand_sum, grad_fc2, out_sum,
    )


def solution(mesh):
    rows = P(("dp", "ctx"), None)
    down, across = P(("dp", "ctx"), "tp"), P("tp", ("dp", "ctx"))
    wide = P("tp")
    ins = (
        rows, rows, P("dp", None), P(), P(), down, wide, down, wide, down, wide, across, P(), down,
        wide, across, P(),
    )
    outs = (
        rows, rows, P(), P(), down, wide, down, wide, down, wide, across, P(), down, wide, across,
        P(),
    )
    return jax.shard_map(body, mesh=mesh, in_specs=ins, out_specs=outs, check_vma=False)
```

time: 5400 us -> 2460 us (0.46)
  waiting for transfers between devices: 3790 us -> 1350 us
  matrix products: 1030 us -> 434 us
  Pallas kernels: 0 us -> 360 us
  local copies, waits for them, and re-layouts: 199 us -> 77.2 us
  other arithmetic: 274 us -> 162 us
    psum x3 -> x1, waiting for transfers between devices: 3430 us -> 1110 us  [tp_sum(): total = lax.psum(part, 'tp').astype(F32)]
    dot_general x198 -> x23, matrix products: 1030 us -> 434 us  [the longest x10 178 us: dot_back(): return jnp.einsum('rb,ab->ra', left, right, preferred_element_type=F32)]
    pallas_call x0 -> x3, Pallas kernels: none -> 360 us  [the longest x1 199 us: attend_back(): pl.pallas_call(functools.partial(attend_back_kernel, 1024), grid_spec=plt...]
    reduce_scatter x6 -> x4, waiting for transfers between devices: 342 us -> 0.05 us  [scatter(): lax.psum_scatter(array.astype(BF16), ('dp', 'ctx'), scatter_dimension=axi...]
    all_to_all x0 -> x4, waiting for transfers between devices: none -> 221 us  [the longest x1 136 us: body(): qkv_all = swap(qkv, split_axis=1, concat_axis=0)]
  transfers between devices with their start and end apart: 15 -> 13, of which waited for: 10 -> 4; matrix products, arithmetic and copies ran while one was open for 25% -> 22% of each run, Pallas kernels for 0% -> 15%
where the time goes in v1:
time: 2460 us; the launch traced here: 2450 us
  waiting for transfers between devices  1350 us (55%)
  matrix products  434 us (18%)
  Pallas kernels  360 us (15%)
  other arithmetic  162 us (7%)
  local copies, waits for them, and re-layouts  77.2 us (3%)
  starting transfers between devices  29.3 us (1%)
  blocking collectives  24.7 us (1%)
    psum x1, waiting for transfers between devices, tp_sum(): total = lax.psum(part, 'tp').astype(F32)  1110 us
    pallas_call x1, Pallas kernels, attend_back(): pl.pallas_call(functools.partial(attend_back_kernel, 1024), grid_spec=plt...  199 us
    dot_general x10, matrix products, dot_back(): return jnp.einsum('rb,ab->ra', left, right, preferred_element_type=F32)  178 us
    dot_general x4, matrix products, transpose_dot(): return jnp.einsum('ra,rb->ab', left, right, preferred_element_type=F32)  136 us
    all_to_all x1, waiting for transfers between devices, body(): qkv_all = swap(qkv, split_axis=1, concat_axis=0)  136 us
    pallas_call x1, Pallas kernels, attend(): pl.pallas_call(functools.partial(attend_kernel, 1024), grid_spec=pltpu.Pr...  115 us
    all_to_all x1, waiting for transfers between devices, body(): swap(jnp.concatenate(grads_all, axis=1), split_axis=0, concat_axis=1)  85 us
    dot_general x4, matrix products, body(): jnp.dot(cut(activated, i), shrink_weight, preferred_element_type=F32)  53.3 us
  transfers between devices with their start and end apart: 13, of which 4 were waited for; matrix products, arithmetic and copies ran while one was open for 22% of the time, Pallas kernels for 15%

profile of v1, /device:TPU:0, one launch (start us, length us, event | category | flops | bytes accessed | tf_op | source)
XLA Modules:
  0.0 2451.6 jit_solution(9684738618928952422)
XLA Ops:
  40.2 20.0 all-gather.5.cloned.1.call-done.weight_ref
  60.1 45.8 %qkv_project.1 = (bf16[4096,2048]{1,0:T(8,128)(2,1)}, bf16[4096,1536]{1,0:T(8,128)(2,1)}) custom-call(s32[16]{0:T(128)} %dynamic_slice.3.where_ref, bf16[4096,2048]{1,0:T(8,128)(2,1)} %x_ref.1, f32[1,2048]{1,0:T(1,128)} %bitcast.101, f32[1,2048]{1,0:T(1,128)} %bitcast.102, bf16[2048,1536]{1,0:T(8,128)(2,1)} %all-gather.5.cloned.1.call-done.weight_ref, ...), custom_call_target="tpu_custom_call" | custom-call | flops 25769803776 | bytes 46137344 | tf_op jit(solution)/shard_map/qkv_project/pallas_call | solution.py:100
  125.3 44.0 %fusion.42 = f32[4096,2048]{1,0:T(8,128)} fusion(bf16[4096,2048]{1,0:T(8,128)(2,1)} %get-tuple-element.26, bf16[2048,2048]{1,0:T(8,128)(2,1)} %all-gather.9.cloned.1.call-done), kind=kOutput, calls=%fused_computation.97 | convolution fusion | flops 34359738368 | bytes 58720256 | tf_op jit(solution)/shard_map/dot_general | solution.py:437
  169.2 136.0 %all-to-all-done = bf16[4096,2,768]{2,0,1:T(8,128)(2,1)} async-done(((bf16[4096,2,768]{2,0,1:T(8,128)(2,1)}), bf16[4096,2,768]{2,0,1:T(8,128)(2,1)}, u32[]{:S(2)}, u32[]{:S(2)}) %all-to-all-start) | async-done | bytes 12582944 | tf_op jit(solution)/shard_map/all_to_all | solution.py:426
  305.3 114.6 %attend.1 = (bf16[8192,256]{1,0:T(8,128)(2,1)}, f32[256,8192]{1,0:T(8,128)}, f32[1,4,8192]{2,1,0:T(4,128)}) custom-call(s32[32]{0:T(128)} %pad_add_fusion.group_ref, s32[32]{0:T(128)} %copy-done.8, bf16[8192,768]{1,0:T(8,128)(2,1)} %bitcast.8.q_ref.ko_ref.vo_ref.kp_ref.vp_ref, bf16[8192,768]{1,0:T(8,128)(2,1)} %bitcast.8.q_ref.ko_ref.vo_ref.kp_ref.vp_ref, ...), custom_call_target="tpu_custom_call" | custom-call | flops 77309411328 | bytes 25165824 | tf_op jit(solution)/shard_map/attend/pallas_call | solution.py:319
  432.5 66.7 %convert_reduce_fusion.3 = (f32[2048]{0:T(1024)}, bf16[4096,2048]{1,0:T(8,128)(2,1)}, bf16[4096,2048]{1,0:T(8,128)(2,1)}) fusion(f32[4096,2048]{1,0:T(8,128)} %fusion.42, f32[2048]{0:T(1024)S(1)} %copy-done.2, bf16[4096,2048]{1,0:T(8,128)(2,1)} %param.18, bf16[2048,2048]{1,0:T(8,128)(2,1)} %all-gather.11.cloned.1.call-done), kind=kOutput, calls=%fused_computation.25 | convolution fusion | flops 34569453568 | bytes 92291072 | tf_op jit(solution)/shard_map/rb,ab->ra/dot_general | solution.py:32
  499.2 14.5 convolution_convert_fusion.4
  514.0 43.4 %convolution_convert_fusion.1 = bf16[2048,2048]{1,0:T(8,128)(2,1)} fusion(bf16[4096,2048]{1,0:T(8,128)(2,1)} %get-tuple-element.26, bf16[4096,2048]{1,0:T(8,128)(2,1)} %get-tuple-element.62), kind=kOutput, calls=%fused_computation.46 | convolution fusion | flops 34363932672 | bytes 41943040 | tf_op jit(solution)/shard_map/ra,rb->ab/dot_general | solution.py:28
  557.4 14.4 convolution_convert_fusion.3
  584.2 44.0 %convolution_convert_fusion = bf16[2048,2048]{1,0:T(8,128)(2,1)} fusion(bf16[4096,2048]{1,0:T(8,128)(2,1)} %get-tuple-element.63, bf16[4096,2048]{1,0:T(8,128)(2,1)} %param.18), kind=kOutput, calls=%fused_computation.45 | convolution fusion | flops 34363932672 | bytes 41943040 | tf_op jit(solution)/shard_map/ra,rb->ab/dot_general | solution.py:28
  628.2 14.8 fusion.16
  643.0 15.1 fusion.18
  658.2 13.1 fusion.20
  710.2 199.4 %attend_back.1 = (bf16[8192,256]{1,0:T(8,128)(2,1)}, bf16[8192,256]{1,0:T(8,128)(2,1)}, bf16[8192,256]{1,0:T(8,128)(2,1)}) custom-call(s32[32]{0:T(128)} %pad_add_fusion.group_ref, s32[32]{0:T(128)} %copy-done.8, s32[32]{0:T(128)} %copy-done.8, bf16[8192,768]{1,0:T(8,128)(2,1)} %bitcast.8.q_ref.ko_ref.vo_ref.kp_ref.vp_ref, ...), custom_call_target="tpu_custom_call" | custom-call | flops 154618822656 | bytes 50331648 | tf_op jit(solution)/shard_map/attend_back/pallas_call | solution.py:353
  919.8 15.8 copy.46
  956.8 14.8 fusion.30
  996.4 85.0 %all-to-all-done.3 = bf16[2,4096,768]{1,2,0:T(8,128)(2,1)} async-done(((bf16[2,4096,768]{1,2,0:T(8,128)(2,1)}), bf16[2,4096,768]{1,2,0:T(8,128)(2,1)}, u32[]{:S(2)}, u32[]{:S(2)}) %all-to-all-start.3) | async-done | bytes 12582944 | tf_op jit(solution)/shard_map/all_to_all | solution.py:435
  1081.4 34.4 %convolution_convert_fusion.2 = bf16[2048,1536]{1,0:T(8,128)(2,1)} fusion(bf16[4096,2048]{1,0:T(8,128)(2,1)} %get-tuple-element.26, bf16[4096,1536]{0,1:T(8,128)(2,1)} %bitcast.25), kind=kOutput, calls=%fused_computation.47 | convolution fusion | flops 25772949504 | bytes 35651584 | tf_op jit(solution)/shard_map/ra,rb->ab/dot_general | solution.py:28
  1190.5 1106.8 %all-reduce.3.cloned.1.call-done = (bf16[1024,2048]{1,0:T(8,128)(2,1)}, bf16[1024,2048]{1,0:T(8,128)(2,1)}, bf16[1024,2048]{1,0:T(8,128)(2,1)}, bf16[1024,2048]{...) async-done(((bf16[1024,2048]{1,0:T(8,128)(2,1)}, ...) | async-done | bytes 33554448 | tf_op jit(solution)/shard_map/psum | solution.py:380
  2297.3 28.6 %fusion.5 = (f32[4096]{0:T(1024)S(1)}, f32[4096]{0:T(1024)S(1)}, f32[2048]{0:T(1024)S(1)}) fusion(bf16[4096,2048]{1,0:T(8,128)(2,1)} %x_ref.1, f32[4096]{0:T(1024)S(1)} %broadcast_multiply_fusion, f32[2048]{0:T(1024)S(1)} %copy-done, bf16[1024,2048]{1,0:T(8,128)(2,1)} %get-tuple-element.57, bf16[1024,2048]{1,0:T(8,128)(2,1)} %get-tuple-element.58, ...), kind=kLoop, calls=%fused_computation.15 | loop fusion | flops 134207488 | bytes 33619968 | tf_op jit(solution)/shard_map/jvp()/reduce_sum | solution.py:37
  2326.0 32.2 %fusion.14 = (f32[2048]{0:T(1024)S(1)}, f32[4096]{0:T(1024)S(1)}) fusion(bf16[4096,2048]{1,0:T(8,128)(2,1)} %x_ref.1, f32[4096]{0:T(1024)S(1)} %get-tuple-element.86, f32[4096]{0:T(1024)S(1)} %broadcast_multiply_fusion, bf16[1024,2048]{1,0:T(8,128)(2,1)} %get-tuple-element.57, bf16[1024,2048]{1,0:T(8,128)(2,1)} %get-tuple-element.58, ...), kind=kLoop, calls=%fused_computation.24 | loop fusion | flops 159377408 | bytes 33636352 | tf_op jit(solution)/shard_map/transpose(jvp())/reduce_sum | solution.py:38
  2358.2 38.3 %convert_reduce_fusion.2 = (f32[2048]{0:T(1024)S(1)}, f32[4096,2048]{1,0:T(8,128)}) fusion(bf16[4096,2048]{1,0:T(8,128)(2,1)} %param.18, f32[4096]{0:T(1024)S(1)} %negate_multiply_fusion, f32[4096]{0:T(1024)S(1)} %get-tuple-element.85, f32[4096]{0:T(1024)S(1)} %broadcast_multiply_fusion, bf16[4096,2048]{1,0:T(8,128)(2,1)} %x_ref.1, ...), kind=kLoop, calls=%fused_computation.12 | loop fusion | flops 159381504 | bytes 83968000 | tf_op jit(solution)/shard_map/reduce_sum | solution.py:467
  2396.5 24.7 %psum.71 = f32[9728]{0:T(1024)S(1)} all-reduce(f32[9728]{0:T(1024)S(1)} %constant_dynamic-update-slice_fusion), channel_id=1, replica_groups=mesh['dp'=4,'ctx'=2,'tp'=4] {'dp','ctx'}, use_global_device_ids=true, to_apply=%region_17.18 | all-reduce | flops 9728 | bytes 77824 | tf_op jit(solution)/shard_map/psum | solution.py:470
  2422.5 14.2 add_convert_fusion.10
  (150 shorter events, 256.2 us)
Async XLA Ops:
  7.2 53.0 %all-gather.5.cloned.1.call-start = ((), (), s32[]{:S(2)}) async-start(), calls=%async_computation.8 | async-start | bytes 7077888 | tf_op jit(solution)/shard_map/all_gather | solution.py:404
  11.8 113.5 %all-gather.9.cloned.1.call-start = ((), (), s32[]{:S(2)}) async-start(), calls=%async_computation.10 | async-start | bytes 9437184 | tf_op jit(solution)/shard_map/all_gather | solution.py:406
  12.5 419.9 %all-gather.11.cloned.1.call-start = ((), (), s32[]{:S(2)}) async-start(), calls=%async_computation.11 | async-start | bytes 9437184 | tf_op jit(solution)/shard_map/all_gather | solution.py:407
  13.3 544.1 %all-gather.7.cloned.1.call-start = ((), (), s32[]{:S(2)}) async-start(), calls=%async_computation.9 | async-start | bytes 2359296 | tf_op jit(solution)/shard_map/all_gather | solution.py:405
  13.8 21.9 copy-start.8
  116.5 188.7 %all-to-all-start = ((bf16[4096,2,768]{2,0,1:T(8,128)(2,1)}), bf16[4096,2,768]{2,0,1:T(8,128)(2,1)}, u32[]{:S(2)}, u32[]{:S(2)}) async-start(bf16[4096,2,768]{2,0,1:T(8,128)(2,1)} %bitcast.80), calls=%async_computation | async-start | bytes 25165824 | tf_op jit(solution)/shard_map/all_to_all | solution.py:426
  426.3 72.9 %all-to-all-start.1 = ((bf16[2,4096,256]{1,2,0:T(8,128)(2,1)}), bf16[2,4096,256]{1,2,0:T(8,128)(2,1)}, u32[]{:S(2)}, u32[]{:S(2)}) async-start(bf16[2,4096,256]{1,2,0:T(8,128)(2,1)} %copy.44), calls=%async_computation.1 | async-start | bytes 8388608 | tf_op jit(solution)/shard_map/all_to_all | solution.py:431
  432.0 740.0 %reduce-scatter.7.cloned.1.call-start = ((), (), s32[]{:S(2)}) async-start(), calls=%async_computation.13 | async-start | bytes 2359296 | tf_op jit(solution)/shard_map/reduce_scatter | solution.py:477
  513.8 666.5 %reduce-scatter.9.cloned.1.call-start = ((), (), s32[]{:S(2)}) async-start(), calls=%async_computation.14 | async-start | bytes 9437184 | tf_op jit(solution)/shard_map/reduce_scatter | solution.py:477
  578.6 131.6 %all-to-all-start.2 = ((bf16[4096,2,256]{2,0,1:T(8,128)(2,1)}), bf16[4096,2,256]{2,0,1:T(8,128)(2,1)}, u32[]{:S(2)}, u32[]{:S(2)}) async-start(bf16[4096,2,256]{2,0,1:T(8,128)(2,1)} %copy.45), calls=%async_computation.2 | async-start | bytes 8388608 | tf_op jit(solution)/shard_map/all_to_all | solution.py:428
  584.2 598.9 %reduce-scatter.11.cloned.1.call-start = ((), (), s32[]{:S(2)}) async-start(), calls=%async_computation.15 | async-start | bytes 9437184 | tf_op jit(solution)/shard_map/reduce_scatter | solution.py:477
  628.2 29.9 %slice-start.2 = ((s8[8388608]{0:T(1024)(128)(4,1)}), s8[4194304]{0:T(1024)(128)(4,1)S(1)}, s32[]{:S(2)}) async-start(s8[8388608]{0:T(1024)(128)(4,1)} %bitcast.108), calls=%async_computation.19 | async-start | bytes 8388608
  643.0 15.1 slice-start.3
  658.2 26.2 %slice-start = ((s8[8388608]{0:T(1024)(128)(4,1)}), s8[4194304]{0:T(1024)(128)(4,1)S(1)}, s32[]{:S(2)}) async-start(s8[8388608]{0:T(1024)(128)(4,1)} %bitcast.106), calls=%async_computation.17 | async-start | bytes 8388608
  671.3 13.0 slice-start.1
  935.6 145.7 %all-to-all-start.3 = ((bf16[2,4096,768]{1,2,0:T(8,128)(2,1)}), bf16[2,4096,768]{1,2,0:T(8,128)(2,1)}, u32[]{:S(2)}, u32[]{:S(2)}) async-start(bf16[2,4096,768]{1,2,0:T(8,128)(2,1)} %copy.46), calls=%async_computation.3 | async-start | bytes 25165824 | tf_op jit(solution)/shard_map/all_to_all | solution.py:435
  944.1 241.7 %reduce-scatter.5.cloned.1.call-start = ((), (), s32[]{:S(2)}) async-start(), calls=%async_computation.12 | async-start | bytes 7077888 | tf_op jit(solution)/shard_map/reduce_scatter | solution.py:477
  944.2 30.3 %slice-start.8 = ((s8[8388608]{0:T(1024)(128)(4,1)}), s8[4194304]{0:T(1024)(128)(4,1)S(1)}, s32[]{:S(2)}) async-start(s8[8388608]{0:T(1024)(128)(4,1)} %bitcast.115), calls=%async_computation.25 | async-start | bytes 8388608
  956.8 17.7 slice-start.9
  1115.8 1181.6 %all-reduce.3.cloned.1.call-start = ((), (), s32[]{:S(2)}) async-start(), calls=%async_computation.16 | async-start | bytes 67108864 | tf_op jit(solution)/shard_map/psum | solution.py:380
  1134.0 21.4 slice-start.10
  1180.2 1117.1 %copy-start = (f32[2048]{0:T(1024)S(1)}, f32[2048]{0:T(1024)}, u32[]{:S(2)}) copy-start(f32[2048]{0:T(1024)} %convert_element_type.142) | copy-start | bytes 24580
  2358.2 38.3 %copy-start.3 = (f32[2048]{0:T(1024)S(1)}, f32[2048]{0:T(1024)}, u32[]{:S(2)}) copy-start(f32[2048]{0:T(1024)} %get-tuple-element.61) | copy-start | bytes 24580
  2421.9 22.2 copy-start.1
  (10 other events, 62.7 us)
Sparse Core Ops, SparseCore 0:
  11.9 48.2 all-gather.4
  62.0 54.3 all-gather.8
  118.3 87.7 all-gather.10
  207.9 36.4 all-gather.6
  513.9 42.3 reduce-scatter.6
  560.0 104.8 reduce-scatter.8
  668.4 71.2 reduce-scatter.10
  1115.9 61.4 reduce-scatter.4
  1181.4 1115.8 all-reduce.2

commit v2 on v1

v2 whole, which is shorter than its diff:
```python
import functools

import jax
import jax.numpy as jnp
from jax import lax
from jax.experimental import pallas as pl
from jax.experimental.pallas import tpu as pltpu
from jax.sharding import PartitionSpec as P

HDIM = 64
ROT = 32
PLEN = 2048
CLEN = 256
GPR = 2
BLOCK = 1024
VMEM = 56 * 2**20
F32 = jnp.float32
BF16 = jnp.bfloat16
NT = (((1,), (1,)), ((), ()))
NN = (((1,), (0,)), ((), ()))


def dot(left, right, dims):
    return lax.dot_general(left, right, dims, preferred_element_type=F32)


def transpose_dot(left, right):
    return jnp.einsum("ra,rb->ab", left, right, preferred_element_type=F32)


def dot_back(left, right):
    return jnp.einsum("rb,ab->ra", left, right, preferred_element_type=F32)


def norm_apply(matrix, norm_gain, norm_shift):
    center = matrix - jnp.mean(matrix, axis=-1, keepdims=True)
    spread = jnp.mean(center * center, axis=-1, keepdims=True)
    return center * lax.rsqrt(spread + 1e-05) * norm_gain + norm_shift


def gelu_parts(v):
    scale = (2.0 / jnp.pi) ** 0.5
    t = jnp.tanh(scale * (v + 0.044715 * v * v * v))
    value = 0.5 * v * (1.0 + t)
    slope = 0.5 * (1.0 + t) + 0.5 * v * (1.0 - t * t) * (scale * (1.0 + 3 * 0.044715 * v * v))
    return value, slope


def rotary_tables():
    half = ROT // 2
    positions = jnp.arange(PLEN + CLEN, dtype=F32)
    frequency = 10000.0 ** (-2.0 * jnp.arange(half, dtype=F32) / ROT)
    angles = positions[:, None] * frequency[None, :]
    cosine, sine = jnp.cos(angles), jnp.sin(angles)
    ones = jnp.ones((PLEN + CLEN, HDIM - ROT), F32)
    zeros = jnp.zeros_like(ones)
    none = jnp.zeros_like(sine)
    head = (
        jnp.concatenate([cosine, cosine, ones], axis=1),
        jnp.concatenate([-sine, none, zeros], axis=1),
        jnp.concatenate([none, sine, zeros], axis=1),
    )
    return tuple(jnp.concatenate([table, table], axis=1) for table in head)


def rotated(values, cosine, first, second):
    half = ROT // 2
    return (
        values * cosine
        + pltpu.roll(values, 2 * HDIM - half, 1) * first
        + pltpu.roll(values, half, 1) * second
    )


def qkv_kernel(
    share, where_ref, x_ref, gain_ref, shift_ref, weight_ref, bias_ref, cos_ref, first_ref,
    second_ref, hidden_ref, out_ref,
):
    x = x_ref[...].astype(F32)
    hidden = norm_apply(x, gain_ref[...], shift_ref[...]).astype(BF16)
    hidden_ref[...] = hidden
    cosine, first, second = cos_ref[...], first_ref[...], second_ref[...]
    lane = lax.broadcasted_iota(jnp.int32, (1, 2 * HDIM), 1)
    member_width = out_ref.shape[2]
    for begin in range(0, weight_ref.shape[1], 512):
        lin = dot(hidden, weight_ref[:, begin : begin + 512], NN) + bias_ref[:, begin : begin + 512]
        for column in range(0, 512, 2 * HDIM):
            part = lin[:, column : column + 2 * HDIM]
            turns = [((begin + column + off) // share) % 3 < 2 for off in (0, HDIM)]
            if any(turns):
                turned = rotated(part, cosine, first, second)
                if not all(turns):
                    keep = lane < HDIM if turns[0] else lane >= HDIM
                    turned = jnp.where(keep, turned, part)
                part = turned
            part = part.astype(BF16)
            for off in range(0, 2 * HDIM, min(2 * HDIM, share)):
                size = min(2 * HDIM, share)
                member, place = divmod(begin + column + off, member_width)
                out_ref[member, :, place : place + size] = part[:, off : off + size]


def qkv_project(x, gain, shift, weight, bias, tables, spots, share):
    rows, width = x.shape
    outs = weight.shape[1]
    count = 256
    whole = lambda shape: pl.BlockSpec(shape, lambda i, *_: (0, 0))
    table = pl.BlockSpec((count, 2 * HDIM), lambda i, spots: (spots[i], 0))
    return pl.pallas_call(
        functools.partial(qkv_kernel, share),
        grid_spec=pltpu.PrefetchScalarGridSpec(
            num_scalar_prefetch=1,
            grid=(rows // count,),
            in_specs=[
                pl.BlockSpec((count, width), lambda i, *_: (i, 0)),
                whole((1, width)),
                whole((1, width)),
                whole((width, outs)),
                whole((1, outs)),
                table,
                table,
                table,
            ],
            out_specs=[
                pl.BlockSpec((count, width), lambda i, *_: (i, 0)),
                pl.BlockSpec((outs // (3 * share), count, 3 * share), lambda i, *_: (0, i, 0)),
            ],
        ),
        out_shape=[
            jax.ShapeDtypeStruct((rows, width), BF16),
            jax.ShapeDtypeStruct((outs // (3 * share), rows, 3 * share), BF16),
        ],
        compiler_params=pltpu.CompilerParams(vmem_limit_bytes=VMEM),
        cost_estimate=pl.CostEstimate(
            flops=2 * rows * width * outs, bytes_accessed=2 * rows * (2 * width + outs),
            transcendentals=0,
        ),
        name="qkv_project",
    )(spots, x, gain, shift, weight, bias, *tables)


def expand_kernel(hidden_ref, weight_ref, bias_ref, lin_ref, out_ref):
    hidden = hidden_ref[...]
    for begin in range(0, weight_ref.shape[1], 512):
        at = slice(begin, begin + 512)
        lin = dot(hidden, weight_ref[:, at], NN) + bias_ref[:, at]
        lin_ref[:, at] = lin
        out_ref[:, at] = gelu_parts(lin)[0].astype(BF16)


def shrink_kernel(act_ref, cot_ref, lin_ref, weight_ref, out_ref, grad_ref, sum_ref, cot_sum_ref):
    @pl.when(pl.program_id(0) == 0)
    def _():
        sum_ref[...] = jnp.zeros_like(sum_ref)
        cot_sum_ref[...] = jnp.zeros_like(cot_sum_ref)

    act, cot = act_ref[...], cot_ref[...]
    for begin in range(0, weight_ref.shape[0], 512):
        at = slice(begin, begin + 512)
        slope = gelu_parts(lin_ref[:, at])[1]
        grad = (slope * dot(cot, weight_ref[at, :], NT)).astype(BF16)
        grad_ref[:, at] = grad
        sum_ref[:, at] += jnp.sum(grad.astype(F32), axis=0, keepdims=True)
    for begin in range(0, weight_ref.shape[1], 512):
        at = slice(begin, begin + 512)
        out_ref[:, at] = dot(act, weight_ref[:, at], NN).astype(BF16)
        cot_sum_ref[:, at] += jnp.sum(cot_ref[:, at].astype(F32), axis=0, keepdims=True)


def row_call(kernel, name, count, rows, in_arrays, outs, flops):
    def spec(shape):
        if shape[0] == rows:
            return pl.BlockSpec((count, shape[1]), lambda i: (i, 0))
        return pl.BlockSpec(shape, lambda i: (0, 0))

    return pl.pallas_call(
        kernel,
        grid=(rows // count,),
        in_specs=[spec(a.shape) for a in in_arrays],
        out_specs=[spec(o.shape) for o in outs],
        out_shape=outs,
        compiler_params=pltpu.CompilerParams(vmem_limit_bytes=VMEM),
        cost_estimate=pl.CostEstimate(
            flops=flops,
            bytes_accessed=sum(a.size * a.dtype.itemsize for a in (*in_arrays, *outs)),
            transcendentals=0,
        ),
        name=name,
    )(*in_arrays)


def products_kernel(kinds, has_base, *refs):
    out_ref = refs[-1]
    base_ref = refs[0] if has_base else None
    pairs = refs[has_base:-1]
    count = 256

    @pl.loop(0, out_ref.shape[0] // count)
    def _(i):
        rows = pl.ds(pl.multiple_of(i * count, count), count)
        total = base_ref[rows, :].astype(F32) if has_base else None
        for n, dims in enumerate(kinds):
            step = dot(pairs[2 * n][rows, :], pairs[2 * n + 1][...], dims)
            total = step if total is None else total + step
        out_ref[rows, :] = total.astype(BF16)


def products(count, outs, base, pairs, name):
    tile = 512
    arrays, specs, kinds = [], [], []
    flops = 0
    if base is not None:
        arrays.append(base[0])
        specs.append(pl.BlockSpec((count, tile), lambda n, at=base[1]: (at, n)))
    for left, at, right, right_at in pairs:
        depth = left.shape[1]
        arrays += [left, right]
        specs.append(pl.BlockSpec((count, depth), lambda n, at=at: (at, 0)))
        if right_at is None:
            specs.append(pl.BlockSpec((tile, depth), lambda n: (n, 0)))
            kinds.append(NT)
        else:
            specs.append(pl.BlockSpec((depth, tile), lambda n, at=right_at: (at, n)))
            kinds.append(NN)
        flops += 2 * count * depth * outs
    return pl.pallas_call(
        functools.partial(products_kernel, kinds, base is not None),
        grid=(outs // tile,),
        in_specs=specs,
        out_specs=pl.BlockSpec((count, tile), lambda n: (0, n)),
        out_shape=jax.ShapeDtypeStruct((count, outs), BF16),
        compiler_params=pltpu.CompilerParams(vmem_limit_bytes=VMEM),
        cost_estimate=pl.CostEstimate(
            flops=flops, bytes_accessed=flops // 512, transcendentals=0
        ),
        name=name,
    )(*arrays)


def heads_split(array, heads):
    if heads == 1:
        return [array]
    lane = lax.broadcasted_iota(jnp.int32, array.shape, 1)
    return [jnp.where(lane // HDIM == h, array, jnp.zeros((), array.dtype)) for h in range(heads)]


def near_mask():
    key = lax.broadcasted_iota(jnp.int32, (CLEN, CLEN), 0)
    query = lax.broadcasted_iota(jnp.int32, (CLEN, CLEN), 1)
    return key <= query


def over_far(base, count, big, step):
    per = big // CLEN
    full = count // per

    @pl.loop(0, full)
    def _(i):
        step(pl.multiple_of(base + i * big, CLEN), big)

    @pl.loop(full * per, count)
    def _(i):
        step(pl.multiple_of(base + i * CLEN, CLEN), CLEN)


def attend_kernel(
    big, group_ref, far_ref, item_ref, q_ref, ko_ref, vo_ref, kp_ref, vt_s, o_ref, ot_ref,
    lse_ref, m_s, l_s, acc_s,
):
    heads = q_ref.shape[1] // HDIM
    item = item_ref[pl.program_id(1)]
    base = group_ref[item] * PLEN

    queries = heads_split(q_ref[...] * BF16(HDIM**-0.5), heads)
    mask = near_mask()
    keys = ko_ref[...]
    values = vo_ref[...].T
    spans = [slice(h * HDIM, (h + 1) * HDIM) for h in range(heads)]
    scores = [dot(keys, queries[h], NT) for h in range(heads)]
    for h in range(heads):
        s = jnp.where(mask, scores[h], -1e30)
        m = jnp.max(s, axis=0, keepdims=True)
        p = jnp.exp(s - m)
        m_s[h] = m
        l_s[h] = jnp.sum(p, axis=0, keepdims=True)
        acc_s[h] = dot(values[spans[h]], p.astype(BF16), NN)

    def step(first, size):
        k = kp_ref[pl.ds(first, size), :]
        scores = [dot(k, queries[h], NT) for h in range(heads)]
        for h in range(heads):
            old = m_s[h]
            m = jnp.maximum(old, jnp.max(scores[h], axis=0, keepdims=True))
            p = jnp.exp(scores[h] - m)
            a = jnp.exp(old - m)
            m_s[h] = m
            l_s[h] = l_s[h] * a + jnp.sum(p, axis=0, keepdims=True)
            acc_s[h] = acc_s[h] * a + dot(vt_s[spans[h], pl.ds(first, size)], p.astype(BF16), NN)

    over_far(base, far_ref[item], big, step)
    for h in range(heads):
        ot_ref[spans[h], :] = acc_s[h] * (1.0 / l_s[h])
        lse_ref[0, h : h + 1, :] = m_s[h] + jnp.log(l_s[h])
    o_ref[...] = ot_ref[...].T.astype(BF16)


def turn_kernel(k_ref, v_ref, kt_ref, vt_ref):
    kt_ref[...] = k_ref[...].T
    vt_ref[...] = v_ref[...].T


def turn_prompts(qkv, width):
    wide = min(4 * HDIM, width)
    (_, k, v), (_, ka, va) = split_columns(qkv, width)
    block = lambda at: pl.BlockSpec((CLEN, wide), lambda h, i: (i, at + h))
    turned = pl.BlockSpec((wide, CLEN), lambda h, i: (h, i))
    return pl.pallas_call(
        turn_kernel,
        grid=(width // wide, GPR * PLEN // CLEN),
        in_specs=[block(ka), block(va)],
        out_specs=[turned, turned],
        out_shape=[jax.ShapeDtypeStruct((width, GPR * PLEN), BF16)] * 2,
        compiler_params=pltpu.CompilerParams(vmem_limit_bytes=VMEM),
        name="turn_prompts",
    )(k, v)


def turned_back(values, tables):
    width = values.shape[1]
    cosine, first, second = (ref[...] for ref in tables)
    wide = 2 * HDIM
    if width < wide:
        values = jnp.concatenate([values, values], axis=1)
    parts = [
        rotated(values[:, c : c + wide], cosine, -first, -second)
        for c in range(0, values.shape[1], wide)
    ]
    out = parts[0] if len(parts) == 1 else jnp.concatenate(parts, axis=1)
    return out[:, :width].astype(BF16)


def attend_back_kernel(big, first_piece, prompt_items, prompt_count, *refs):
    group_ref, far_ref, item_ref = refs[:3]
    q_ref, ko_ref, vo_ref, do_ref, ot_ref, lse_ref, kp_ref, vp_ref, kt_s = refs[3:12]
    tables = refs[12:15]
    before = () if first_piece else refs[15:17]
    dq_ref, dk_ref, dv_ref, dk_s, dv_s, dq_s, near_k, near_v = refs[15 + len(before) :]
    width = q_ref.shape[1]
    heads = width // HDIM
    turn = pl.program_id(1)
    item = item_ref[turn]
    base = group_ref[item] * PLEN

    @pl.when(turn == 0)
    def _():
        if first_piece:
            dk_s[...] = jnp.zeros_like(dk_s)
            dv_s[...] = jnp.zeros_like(dv_s)
        else:
            dk_s[...] = before[0][...]
            dv_s[...] = before[1][...]

    do = do_ref[...]
    queries = heads_split(q_ref[...] * BF16(HDIM**-0.5), heads)
    grads = heads_split(do, heads)
    query_cat = jnp.concatenate(queries, axis=0)
    grad_cat = jnp.concatenate(grads, axis=0)
    spans = [slice(h * HDIM, (h + 1) * HDIM) for h in range(heads)]
    product = ot_ref[...] * do.astype(F32).T
    center = [jnp.sum(product[span], axis=0, keepdims=True) for span in spans]
    lse = [lse_ref[0, h : h + 1, :] for h in range(heads)]
    mask = near_mask()

    def piece(k, v, kt, near):
        chance, grad_scores = [], []
        scores = [dot(k, queries[h], NT) for h in range(heads)]
        grad_chance = [dot(v, grads[h], NT) for h in range(heads)]
        for h in range(heads):
            p = jnp.exp(scores[h] - lse[h])
            if near:
                p = jnp.where(mask, p, 0.0)
            grad_scores.append((p * (grad_chance[h] - center[h])).astype(BF16))
            chance.append(p.astype(BF16))
        for h in range(heads):
            step = dot(kt(spans[h]), grad_scores[h], NN)
            if near:
                dq_s[spans[h], :] = step
            else:
                dq_s[spans[h], :] += step
        return (
            dot(jnp.concatenate(grad_scores, axis=1), query_cat, NN),
            dot(jnp.concatenate(chance, axis=1), grad_cat, NN),
        )

    own = ko_ref[...]
    own_t = own.T
    near_k[...], near_v[...] = piece(own, vo_ref[...], lambda span: own_t[span], True)

    @pl.when(turn < prompt_count)
    def _():
        rows = pl.ds(pl.multiple_of(item * CLEN, CLEN), CLEN)
        dk_s[rows, :] += near_k[...]
        dv_s[rows, :] += near_v[...]

    @pl.when(turn >= prompt_count)
    def _():
        dk_ref[...] = turned_back(near_k[...], tables)
        dv_ref[...] = near_v[...].astype(BF16)

    def step(first, size):
        rows = pl.ds(first, size)
        k_step, v_step = piece(
            kp_ref[rows, :], vp_ref[rows, :], lambda span: kt_s[span, rows], False
        )
        dk_s[rows, :] += k_step
        dv_s[rows, :] += v_step

    over_far(base, far_ref[item], big, step)
    dq_ref[...] = turned_back((dq_s[...] * (HDIM**-0.5)).T, tables)


def finish_kernel(dk_ref, dv_ref, cos_ref, first_ref, second_ref, ok_ref, ov_ref):
    ok_ref[...] = turned_back(dk_ref[...], (cos_ref, first_ref, second_ref))
    ov_ref[...] = dv_ref[...].astype(BF16)


def finish_prompts(dk, dv, tables):
    rows, width = dk.shape
    wide = min(4 * HDIM, width)
    block = pl.BlockSpec((CLEN, wide), lambda h, i: (i, h))
    table = pl.BlockSpec((CLEN, 2 * HDIM), lambda h, i: (i % (PLEN // CLEN), 0))
    return pl.pallas_call(
        finish_kernel,
        grid=(width // wide, rows // CLEN),
        in_specs=[block, block, table, table, table],
        out_specs=[block, block],
        out_shape=[jax.ShapeDtypeStruct((rows, width), BF16)] * 2,
        compiler_params=pltpu.CompilerParams(vmem_limit_bytes=VMEM),
        name="finish_prompts",
    )(dk, dv, *tables)


def split_columns(qkv, width):
    wide = min(4 * HDIM, width)
    if wide % 128 == 0:
        return (qkv, qkv, qkv), tuple(t * width // wide for t in range(3))
    return tuple(qkv[:, t * width : (t + 1) * width] for t in range(3)), (0, 0, 0)


def attention_specs(width):
    wide = min(4 * HDIM, width)
    heads = wide // HDIM
    return (
        wide,
        heads,
        lambda at: pl.BlockSpec((CLEN, wide), lambda h, i, g, f, items: (items[i], at + h)),
        pl.BlockSpec((CLEN, wide), lambda h, i, *_: (i, h)),
        pl.BlockSpec((wide, CLEN), lambda h, i, *_: (h, i)),
        lambda at: pl.BlockSpec((GPR * PLEN, wide), lambda h, i, *_: (0, at + h)),
        pl.BlockSpec((1, heads, CLEN), lambda h, i, *_: (h, 0, i)),
    )


def attend(qkv, turned_v, width, group, far, items):
    rows = items.shape[0] * CLEN
    wide, heads, picked, block, turned, prompts, stats = attention_specs(width)
    (q, k, v), (qa, ka, va) = split_columns(qkv, width)
    pairs = rows * (PLEN + CLEN) * width // HDIM
    return pl.pallas_call(
        functools.partial(attend_kernel, 1024),
        grid_spec=pltpu.PrefetchScalarGridSpec(
            num_scalar_prefetch=3,
            grid=(width // wide, rows // CLEN),
            in_specs=[
                picked(qa), picked(ka), picked(va), prompts(ka),
                pl.BlockSpec((wide, GPR * PLEN), lambda h, i, *_: (h, 0)),
            ],
            out_specs=[block, turned, stats],
            scratch_shapes=[
                pltpu.VMEM((heads, 1, CLEN), F32),
                pltpu.VMEM((heads, 1, CLEN), F32),
                pltpu.VMEM((heads, HDIM, CLEN), F32),
            ],
        ),
        out_shape=[
            jax.ShapeDtypeStruct((rows, width), BF16),
            jax.ShapeDtypeStruct((width, rows), F32),
            jax.ShapeDtypeStruct((width // wide, heads, rows), F32),
        ],
        compiler_params=pltpu.CompilerParams(vmem_limit_bytes=VMEM),
        cost_estimate=pl.CostEstimate(
            flops=4 * pairs * 256, bytes_accessed=rows * width * 12, transcendentals=pairs
        ),
        name="attend",
    )(group, far, items, q, k, v, k, turned_v)


def attend_back(
    qkv, turned_k, width, grad, turned_out, lse, tables, group, far, items, prompt_count, before
):
    rows = items.shape[0] * CLEN
    wide, heads, picked, block, turned, prompts, stats = attention_specs(width)
    (q, k, v), (qa, ka, va) = split_columns(qkv, width)
    table = pl.BlockSpec((CLEN, 2 * HDIM), lambda h, i, g, f, items: (f[items[i]], 0))
    total = pl.BlockSpec((GPR * PLEN, wide), lambda h, i, *_: (0, h))
    late = pl.BlockSpec((CLEN, wide), lambda h, i, *_: (jnp.maximum(i - prompt_count, 0), h))
    pairs = rows * (PLEN + CLEN) * width // HDIM
    first = not before
    late_rows = rows - prompt_count * CLEN
    return pl.pallas_call(
        functools.partial(attend_back_kernel, 1024, first, GPR * PLEN // CLEN, prompt_count),
        grid_spec=pltpu.PrefetchScalarGridSpec(
            num_scalar_prefetch=3,
            grid=(width // wide, rows // CLEN),
            in_specs=[
                picked(qa), picked(ka), picked(va), picked(0), turned, stats, prompts(ka),
                prompts(va), pl.BlockSpec((wide, GPR * PLEN), lambda h, i, *_: (h, 0)), table, table,
                table,
            ]
            + [total] * len(before),
            out_specs=[block, late, late, total, total],
            scratch_shapes=[
                pltpu.VMEM((wide, CLEN), F32),
                pltpu.VMEM((CLEN, wide), F32),
                pltpu.VMEM((CLEN, wide), F32),
            ],
        ),
        out_shape=[jax.ShapeDtypeStruct((rows, width), BF16)]
        + [jax.ShapeDtypeStruct((late_rows, width), BF16)] * 2
        + [jax.ShapeDtypeStruct((GPR * PLEN, width), F32)] * 2,
        input_output_aliases={} if first else {15: 3, 16: 4},
        compiler_params=pltpu.CompilerParams(vmem_limit_bytes=VMEM),
        cost_estimate=pl.CostEstimate(
            flops=8 * pairs * 256, bytes_accessed=rows * width * 24, transcendentals=pairs
        ),
        name="attend_back",
    )(group, far, items, q, k, v, grad, turned_out, lse, k, v, turned_k, *tables, *before)


def tie(*trees):
    return lax.optimization_barrier(trees)


COUNT = 128


def begin_kernel(names, flag_ref, *refs):
    refs = dict(zip(names, refs))
    outer = flag_ref[0] == 1
    out_ref = refs["out"]

    @pl.when(outer)
    def _():
        out_ref[...] = refs["next"][...] if "next" in refs else jnp.zeros_like(out_ref)

    @pl.when(flag_ref[0] == 0)
    def _():
        if "part" not in refs:
            out_ref[...] = jnp.zeros_like(out_ref)
            return
        total = (
            refs["part"][...].astype(F32)
            + refs["swapped"][...].astype(F32)
            + refs["crossed"][...].astype(F32)
        )
        if "tokens" in refs:
            total = total + refs["tokens"][...].astype(F32) + refs["bias"][...]
        out_ref[...] = total.astype(BF16)


def middle_kernel(names, flag_ref, *refs):
    refs = dict(zip(names, refs))
    outer = flag_ref[0] == 1
    swap_ref = refs["swap"]

    @pl.when(outer)
    def _():
        swap_ref[...] = refs["near"][...] if "near" in refs else jnp.zeros_like(swap_ref)

    @pl.when(flag_ref[0] == 0)
    def _():
        swap_ref[...] = refs["crossed"][...] if "crossed" in refs else jnp.zeros_like(swap_ref)

    if "far" in refs:
        refs["cross"][...] = (
            refs["far"][...].astype(F32) + refs["swapped"][...].astype(F32)
        ).astype(BF16)


def line_call(kernel, flags, rows, width, ins, outs, name):
    steps = rows // COUNT

    def spec(shape, first, who):
        if shape[0] == 1:
            return pl.BlockSpec(shape, lambda i, flag: (0, 0))

        def index(i, flag):
            needed = {"all": 1, "outer": flag[0], "inner": 1 - flag[0]}[who]
            return (first(flag[1], steps) + i * needed, 0)

        return pl.BlockSpec((COUNT, width), index)

    return pl.pallas_call(
        functools.partial(kernel, [i[0] for i in ins] + outs),
        grid_spec=pltpu.PrefetchScalarGridSpec(
            num_scalar_prefetch=1,
            grid=(steps,),
            in_specs=[spec(array.shape, first, who) for _, array, first, who in ins],
            out_specs=[pl.BlockSpec((COUNT, width), lambda i, flag: (i, 0)) for _ in outs],
        ),
        out_shape=[jax.ShapeDtypeStruct((rows, width), BF16) for _ in outs],
        compiler_params=pltpu.CompilerParams(vmem_limit_bytes=VMEM),
        name=name,
    )(flags, *[i[1] for i in ins])


def total_specs(half, width):
    outer = lambda flag: flag[0]
    inner = lambda flag: 1 - flag[0]

    def spec(part, who):
        return pl.BlockSpec((COUNT, width), lambda p, i, flag: (i * who(flag) * (p == part), 0))

    return [spec(0, outer), spec(0, inner), spec(1, outer), spec(1, inner)]


def total_of(flag_ref, refs, keep):
    part = pl.program_id(0)
    for at, ref in enumerate(refs):
        right = (part == at // 2) & (flag_ref[0] == 1 - at % 2)

        @pl.when(right)
        def _(ref=ref):
            keep(ref[...])


def rows_of(block, half):
    steps = half // COUNT

    def index(p, i, flag):
        return ((2 * block + (flag[1] + p) % 2) * steps + i, 0)

    return index


def place_kernel(flag_ref, a, b, c, d, *rest):
    out_ref = rest[-1]

    def keep(value):
        out_ref[...] = value

    total_of(flag_ref, (a, b, c, d), keep)


def place_total(flags, four, block, rows, before):
    half, width = four[0].shape
    return pl.pallas_call(
        place_kernel,
        grid_spec=pltpu.PrefetchScalarGridSpec(
            num_scalar_prefetch=1,
            grid=(2, half // COUNT),
            in_specs=total_specs(half, width)
            + [pl.BlockSpec(memory_space=pl.ANY)] * (before is not None),
            out_specs=pl.BlockSpec((COUNT, width), rows_of(block, half)),
        ),
        out_shape=jax.ShapeDtypeStruct((rows, width), BF16),
        input_output_aliases={} if before is None else {5: 0},
        compiler_params=pltpu.CompilerParams(vmem_limit_bytes=VMEM),
        name="place_total",
    )(flags, *four, *(() if before is None else (before,)))


def norm_back_kernel(flag_ref, a, b, c, d, x_ref, cot_ref, gain_ref, *rest):
    out_ref, gain_sum, shift_sum, held = rest[-4:]

    @pl.when((pl.program_id(0) == 0) & (pl.program_id(1) == 0))
    def _():
        gain_sum[...] = jnp.zeros_like(gain_sum)
        shift_sum[...] = jnp.zeros_like(shift_sum)

    def keep(value):
        held[...] = value.astype(F32)

    total_of(flag_ref, (a, b, c, d), keep)
    x = x_ref[...].astype(F32)
    center = x - jnp.mean(x, axis=-1, keepdims=True)
    inverse = lax.rsqrt(jnp.mean(center * center, axis=-1, keepdims=True) + 1e-05)
    normed = center * inverse
    total = held[...]
    gain_sum[...] += jnp.sum(total * normed, axis=0, keepdims=True)
    shift_sum[...] += jnp.sum(total, axis=0, keepdims=True)
    scaled = total * gain_ref[...]
    grad = scaled - jnp.mean(scaled, axis=-1, keepdims=True)
    grad = inverse * (grad - normed * jnp.mean(scaled * normed, axis=-1, keepdims=True))
    out_ref[...] = cot_ref[...].astype(F32) + grad


def norm_back(flags, four, block, tokens, cotangent, gain, before):
    half, width = four[0].shape
    row = pl.BlockSpec((1, width), lambda p, i, flag: (0, 0))
    whole = pl.BlockSpec((COUNT, width), rows_of(block, half))
    return pl.pallas_call(
        norm_back_kernel,
        grid_spec=pltpu.PrefetchScalarGridSpec(
            num_scalar_prefetch=1,
            grid=(2, half // COUNT),
            in_specs=total_specs(half, width)
            + [whole, whole, row]
            + [pl.BlockSpec(memory_space=pl.ANY)] * (before is not None),
            out_specs=[whole, row, row],
            scratch_shapes=[pltpu.VMEM((COUNT, width), F32)],
        ),
        out_shape=[
            jax.ShapeDtypeStruct(tokens.shape, F32),
            jax.ShapeDtypeStruct((1, width), F32),
            jax.ShapeDtypeStruct((1, width), F32),
        ],
        input_output_aliases={} if before is None else {8: 0},
        compiler_params=pltpu.CompilerParams(vmem_limit_bytes=VMEM),
        name="norm_back",
    )(flags, *four, tokens, cotangent, gain, *(() if before is None else (before,)))


class Line:
    def __init__(self, flags, tokens, bias):
        self.flags, self.tokens, self.bias = flags, tokens, bias
        self.part = self.near = None
        self.block = -1

    def begin(self, part, with_input):
        zero = lambda side, steps: 0
        near = lambda side, steps: side * steps
        ins = []
        if self.part is not None:
            ins += [
                ("part", self.part, near, "inner"),
                ("swapped", self.swapped, zero, "inner"),
                ("crossed", self.crossed, zero, "inner"),
            ]
            if self.with_input:
                block = self.block
                ins += [
                    ("tokens", self.tokens, lambda side, steps: (2 * block + side) * steps, "inner"),
                    ("bias", self.bias, zero, "all"),
                ]
        if part is not None:
            ins.append(("next", part, lambda side, steps: (1 - side) * steps, "outer"))
        shape = (self.part if part is None else part).shape
        (out,) = line_call(
            begin_kernel, self.flags, shape[0] // 2, shape[1], ins, ["out"], "line_begin"
        )
        had = self.part is not None
        self.part, self.with_input = part, with_input
        self.block += 1
        self.near = out if had else None
        return out, self.near

    def middle(self, swapped, crossed):
        self.first, self.other = swapped, crossed
        ins = []
        if self.part is not None:
            ins += [
                ("near", self.part, lambda side, steps: side * steps, "outer"),
                ("far", self.part, lambda side, steps: (1 - side) * steps, "inner"),
                ("swapped", swapped, lambda side, steps: 0, "inner"),
            ]
        if crossed is not None:
            ins.append(("crossed", crossed, lambda side, steps: 0, "inner"))
        if self.part is None:
            return crossed, None
        return tuple(
            line_call(
                middle_kernel, self.flags, *swapped.shape, ins, ["swap", "cross"], "line_middle"
            )
        )

    def end(self, swapped, crossed):
        self.swapped, self.crossed = swapped, crossed
        if self.near is None:
            return None
        return self.first, self.near, swapped, self.other


def send(swap, cross):
    outer, middle = [(0, 1), (3, 2), (1, 0), (2, 3)], [(1, 2), (2, 1)]
    return (
        None if swap is None else lax.ppermute(swap, "tp", outer),
        None if cross is None else lax.ppermute(cross, "tp", middle),
    )


def body(
    tokens, cotangent, membership, ln_gain, ln_bias, w_query, b_query, w_key, b_key, w_value,
    b_value, w_dense, b_dense, w_fc1, b_fc1, w_fc2, b_fc2,
):
    rows, width = tokens.shape
    ctx_count = lax.axis_size("ctx")
    ctx_index = lax.axis_index("ctx")
    local = w_query.shape[1]
    share = local // ctx_count
    mine = 3 * share
    block = min(BLOCK, rows // 2)
    blocks = rows // block

    def mixed(query, key, value):
        lead = query.shape[:-1]
        stacked = jnp.stack(
            [a.reshape(*lead, ctx_count, share) for a in (query, key, value)], axis=-2
        )
        return stacked.reshape(*lead, 3 * local)

    gather = functools.partial(lax.all_gather, axis_name=("dp", "ctx"), tiled=True)
    qkv_weight = gather(mixed(w_query, w_key, w_value), axis=0)
    expand_weight = gather(w_fc1, axis=0)
    shrink_weight = gather(w_fc2, axis=1)
    dense_weight = gather(w_dense, axis=1)
    qkv_bias = mixed(b_query, b_key, b_value).astype(F32)[None]

    per_prompt = PLEN // CLEN
    prompt_items = GPR * per_prompt
    own_items = rows // CLEN
    items = jnp.arange(own_items * ctx_count, dtype=jnp.int32)
    far = jnp.where(items < prompt_items, items % per_prompt, per_prompt)
    group = jnp.concatenate([items[:prompt_items] // per_prompt, membership[0]])
    own_spots = lax.dynamic_slice_in_dim(far, ctx_index * own_items, own_items)
    tables = rotary_tables()
    per_block = block // CLEN
    item_table = items.reshape(ctx_count, blocks, per_block)
    piece_items = [item_table[:, b].reshape(-1) for b in range(blocks)]
    prompt_count = ctx_count // 2 * per_block

    gain = ln_gain.astype(F32)
    shift = ln_bias.astype(F32)
    hidden, qkv = qkv_project(
        tokens, gain[None], shift[None], qkv_weight, qkv_bias, tables, own_spots, share
    )

    def exchange(parts):
        if ctx_count == 2:
            low = ctx_index == 0
            away = jnp.where(low, parts[1], parts[0])
            stay = jnp.where(low, parts[0], parts[1])
            came = lax.ppermute(away, "ctx", [(0, 1), (1, 0)])
            return [jnp.where(low, stay, came), jnp.where(low, came, stay)]
        came = lax.all_to_all(jnp.stack(parts), "ctx", split_axis=0, concat_axis=0, tiled=True)
        return [came[c] for c in range(ctx_count)]

    def swap_whole(array):
        swapped = lax.all_to_all(array, "ctx", split_axis=0, concat_axis=0, tiled=True)
        return swapped.reshape(-1, array.shape[-1])

    qkv_all = swap_whole(qkv)
    cut = lambda array, i: array[i * block : (i + 1) * block]

    expand_lin, activated = row_call(
        expand_kernel, "expand", 256, rows, (hidden, expand_weight, b_fc1.astype(F32)[None]),
        (
            jax.ShapeDtypeStruct((rows, expand_weight.shape[1]), F32),
            jax.ShapeDtypeStruct((rows, expand_weight.shape[1]), BF16),
        ),
        2 * rows * width * expand_weight.shape[1],
    )
    mlp_out, grad_expand, expand_sum, cot_sum = row_call(
        shrink_kernel, "shrink", 256, rows, (activated, cotangent, expand_lin, shrink_weight),
        (
            jax.ShapeDtypeStruct((rows, width), BF16),
            jax.ShapeDtypeStruct(activated.shape, BF16),
            jax.ShapeDtypeStruct((1, activated.shape[1]), F32),
            jax.ShapeDtypeStruct((1, width), F32),
        ),
        4 * rows * width * expand_weight.shape[1],
    )
    _, cot_late = tie(hidden, cotangent)
    grad_att = jnp.stack(
        [
            dot_back(cot_late, dense_weight[c * share : (c + 1) * share]).astype(BF16)
            for c in range(ctx_count)
        ]
    )
    grad_all = swap_whole(grad_att)
    qkv_all, mlp_out, grad_att = tie(qkv_all, mlp_out, grad_att)
    turned_k, turned_v = turn_prompts(qkv_all, share)

    place = lax.axis_index("tp")
    flags = jnp.stack([((place == 0) | (place == 3)).astype(jnp.int32), place // 2])
    gain_row = gain[None]

    env = {}

    def forward(b):
        def run(qkv_in, turned_in):
            return attend(qkv_in, turned_in, share, group, far, piece_items[b])

        def keep(out):
            o, env["turned", b], env["lse", b] = out
            env["attended", b] = exchange([cut(o, c) for c in range(ctx_count)])

        return run, (qkv_all, turned_v), keep

    def out_part(b):
        def run(mlp, weight, *heads_out):
            pairs = [(part, 0, weight, c) for c, part in enumerate(heads_out)]
            return products(block, width, (mlp, b), pairs, "out_part")

        def keep(out):
            env["part", b] = out

        return run, (mlp_out, dense_weight, *env["attended", b]), keep

    def backward(b):
        before = () if b == 0 else env["totals"]

        def run(qkv_in, turned_in, grad_in, turned, lse, *before):
            return attend_back(
                qkv_in, turned_in, share, grad_in, turned, lse, tables, group, far, piece_items[b],
                prompt_count, before,
            )

        def keep(out):
            env["dq", b], env["dk", b], env["dv", b] = out[:3]
            env["totals"] = out[3:]

        return run, (qkv_all, turned_k, grad_all, env["turned", b], env["lse", b], *before), keep

    def finish():
        def run(dk, dv):
            return finish_prompts(dk, dv, tables)

        def keep(out):
            env["prompt_grads"] = [array.reshape(ctx_count // 2, rows, share) for array in out]

        return run, env["totals"], keep

    def give_back(b):
        def run(prompts, dq, dk, dv):
            parts = []
            for c in range(ctx_count):
                at = c - ctx_count // 2
                near = slice(b * block, (b + 1) * block)
                key = prompts[0][c, near] if at < 0 else cut(dk, at)
                value = prompts[1][c, near] if at < 0 else cut(dv, at)
                parts.append(jnp.concatenate([cut(dq, c), key, value], axis=1))
            return jnp.concatenate(exchange(parts), axis=1)

        def keep(out):
            env["grad_qkv", b] = out

        return run, (env["prompt_grads"], env["dq", b], env["dk", b], env["dv", b]), keep

    def grad_part(b):
        def run(grad_exp, exp_weight, grad, weight):
            pairs = [(grad_exp, b, exp_weight, None), (grad, 0, weight, None)]
            return products(block, width, None, pairs, "grad_part")

        def keep(out):
            env["part", blocks + b] = out

        return run, (grad_expand, expand_weight, env["grad_qkv", b], qkv_weight), keep

    def weight_grad(name, left, right, axis):
        def run(left, right):
            return transpose_dot(left, right).astype(BF16)

        def keep(out):
            env[name] = lax.psum_scatter(
                out, ("dp", "ctx"), scatter_dimension=axis, tiled=True
            ).astype(F32)

        return run, (left, right), keep

    def put_out(b):
        def run(four, before):
            return place_total(flags, four, b, rows, before)

        def keep(out):
            env["layer_out"] = out

        return run, (env["total", b], env.get("layer_out")), keep

    def put_grad(b):
        def run(four, tokens_in, cot_in, before):
            return norm_back(flags, four, b, tokens_in, cot_in, gain_row, before)

        def keep(out):
            env["grad_tokens"], env["gain", b], env["shift", b] = out

        return run, (env["total", blocks + b], tokens, cotangent, env.get("grad_tokens")), keep

    def all_attended():
        return jnp.concatenate(
            [
                jnp.concatenate([env["attended", b][c] for b in range(blocks)], axis=0)
                for c in range(ctx_count)
            ],
            axis=1,
        )

    def all_grad_qkv():
        return jnp.concatenate([env["grad_qkv", b] for b in range(blocks)], axis=0)

    ticks = 4 * blocks + 2
    plan = [[] for _ in range(ticks + 8)]
    spot = 2 * blocks - 2
    for b in range(blocks):
        if b >= 2:
            plan[b - 2].append(functools.partial(forward, b))
        if b >= 1:
            plan[b - 1].append(functools.partial(out_part, b))
        plan[blocks - 2 + b].append(functools.partial(backward, b))
        plan[2 * b + 4].append(functools.partial(put_out, b))
        plan[spot + 1 + 2 * b].append(functools.partial(grad_part, b))
        plan[2 * blocks + 2 * b + 4].append(functools.partial(put_grad, b))
    after = [[] for _ in plan]
    after[spot - 1].append(finish)
    for b in range(blocks):
        plan[spot + 2 * b].append(functools.partial(give_back, b))
    plan[spot].append(lambda: weight_grad("dense", all_attended(), cotangent, 1))
    plan[spot].append(lambda: weight_grad("fc2", activated, cotangent, 1))
    plan[spot + 3].append(lambda: weight_grad("fc1", hidden, grad_expand, 0))
    plan[spot + 2 * blocks].append(lambda: weight_grad("qkv", hidden, all_grad_qkv(), 0))

    def perform(make):
        run, ins, keep = make()
        keep(run(*ins))

    for b in range(min(2, blocks)):
        perform(functools.partial(forward, b))
    perform(functools.partial(out_part, 0))

    line = Line(flags, tokens, (b_dense.astype(F32) + b_fc2.astype(F32))[None])
    arrived = (None, None)
    for t in range(ticks):
        b, second = divmod(t, 2)
        if second:
            operands = line.middle(*arrived)
        else:
            if t > 0:
                total = line.end(*arrived)
                if total is not None:
                    env["total", b - 2] = total
            operands = line.begin(env.get(("part", b)), b < blocks)
        stages = [s for s in (plan[t], after[t]) if s]
        sent = None
        for n, stage in enumerate(stages):
            work = [make() for make in stage]
            operands, ins = tie(operands, [w[1] for w in work])
            if sent is None:
                sent = send(*operands)
            outs = [w[0](*i) for w, i in zip(work, ins)]
            if n == len(stages) - 1:
                arrived, outs = tie(sent, outs)
            for w, out in zip(work, outs):
                w[2](out)
        if not stages:
            arrived = send(*operands)
    env["total", 2 * blocks - 1] = line.end(*arrived)
    for late in plan[ticks:]:
        for make in late:
            perform(make)

    layer_out, grad_tokens = env["layer_out"], env["grad_tokens"]
    small = (
        sum(env["gain", b][0] for b in range(blocks)),
        sum(env["shift", b][0] for b in range(blocks)),
        jnp.sum(all_grad_qkv().astype(F32), axis=0),
        expand_sum[0],
        cot_sum[0],
    )
    sizes = [array.shape[0] for array in small]
    packed = lax.psum(jnp.concatenate(small), ("dp", "ctx"))
    ends = [sum(sizes[: i + 1]) for i in range(len(sizes))]
    gain_sum, shift_sum, qkv_sum, expand_total, out_sum = (
        packed[end - size : end] for end, size in zip(ends, sizes)
    )

    def unmixed(array):
        lead = array.shape[:-1]
        parts = array.reshape(*lead, ctx_count, 3, share)
        return tuple(parts[..., t, :].reshape(*lead, local) for t in range(3))

    grad_query, grad_key, grad_value = unmixed(env["qkv"])
    sum_query, sum_key, sum_value = unmixed(qkv_sum)
    return (
        layer_out, grad_tokens, gain_sum, shift_sum, grad_query, sum_query, grad_key, sum_key,
        grad_value, sum_value, env["dense"], out_sum, env["fc1"], expand_total, env["fc2"], out_sum,
    )


def solution(mesh):
    rows = P(("dp", "ctx"), None)
    down, across = P(("dp", "ctx"), "tp"), P("tp", ("dp", "ctx"))
    wide = P("tp")
    ins = (
        rows, rows, P("dp", None), P(), P(), down, wide, down, wide, down, wide, across, P(), down,
        wide, across, P(),
    )
    outs = (
        rows, rows, P(), P(), down, wide, down, wide, down, wide, across, P(), down, wide, across,
        P(),
    )
    return jax.shard_map(body, mesh=mesh, in_specs=ins, out_specs=outs, check_vma=False)
```

time: 2460 us -> 1640 us (0.67)
  waiting for transfers between devices: 1350 us -> 299 us
  Pallas kernels: 360 us -> 884 us
  matrix products: 434 us -> 154 us
  other arithmetic: 162 us -> 84.6 us
  starting transfers between devices: 29.3 us -> 97.4 us
    psum x1 -> x0, waiting for transfers between devices: 1110 us -> none  [tp_sum(): total = lax.psum(part, 'tp').astype(F32)]
    pallas_call x1 -> x41, Pallas kernels: 199 us -> 712 us  [the longest x4 231 us: attend_back(): pl.pallas_call(functools.partial(attend_back_kernel, 1024, first, GPR * P...]
    all_to_all x4 -> x2, waiting for transfers between devices: 221 us -> 0.01 us  [swap_whole(): lax.all_to_all(array, 'ctx', split_axis=0, concat_axis=0, tiled=True)]
    ppermute x0 -> x42, waiting for transfers between devices: none -> 203 us  [the longest x18 146 us: send(): lax.ppermute(swap, 'tp', outer)]
    dot_general x10 -> x2, matrix products: 178 us -> 19.8 us  [dot_back(): return jnp.einsum('rb,ab->ra', left, right, preferred_element_type=F32)]
    dot_general x9 -> x0, matrix products: 119 us -> none  [the longest x4 53.3 us: body(): jnp.dot(cut(activated, i), shrink_weight, preferred_element_type=F32)]
    reduce_sum x5 -> x1, other arithmetic: 113 us -> 6.32 us  [body(): jnp.sum(all_grad_qkv().astype(F32), axis=0)]
    ppermute x0 -> x42, starting transfers between devices: none -> 83.1 us  [the longest x18 50.4 us: send(): lax.ppermute(swap, 'tp', outer)]
  transfers between devices with their start and end apart: 13 -> 52, of which waited for: 4 -> 16; matrix products, arithmetic and copies ran while one was open for 22% -> 16% of each run, Pallas kernels for 15% -> 51%
where the time goes in v2:
time: 1640 us; the launch traced here: 1630 us
  Pallas kernels  884 us (54%)
  waiting for transfers between devices  299 us (18%)
  matrix products  154 us (9%)
  starting transfers between devices  97.4 us (6%)
  other arithmetic  84.6 us (5%)
  local copies, waits for them, and re-layouts  69.6 us (4%)
  blocking collectives  23 us (1%)
    pallas_call x4, Pallas kernels, attend_back(): pl.pallas_call(functools.partial(attend_back_kernel, 1024, first, GPR * P...  231 us
    pallas_call x2, Pallas kernels, row_call(): pl.pallas_call(kernel, grid=(rows // count,), in_specs=[spec(a.shape) for...  150 us
    ppermute x18, waiting for transfers between devices, send(): lax.ppermute(swap, 'tp', outer)  146 us
    dot_general x4, matrix products, transpose_dot(): return jnp.einsum('ra,rb->ab', left, right, preferred_element_type=F32)  134 us
    pallas_call x8, Pallas kernels, products(): pl.pallas_call(functools.partial(products_kernel, kinds, base is not None...  129 us
    pallas_call x4, Pallas kernels, attend(): pl.pallas_call(functools.partial(attend_kernel, 1024), grid_spec=pltpu.Pr...  126 us
    pallas_call x17, Pallas kernels, line_call(): pl.pallas_call(functools.partial(kernel, [i[0] for i in ins] + outs), gri...  89.2 us
    ppermute x8, waiting for transfers between devices, exchange(): came = lax.ppermute(away, 'ctx', [(0, 1), (1, 0)])  57.4 us
  transfers between devices with their start and end apart: 52, of which 16 were waited for; matrix products, arithmetic and copies ran while one was open for 16% of the time, Pallas kernels for 51%

profile of v2, /device:TPU:0, one launch (start us, length us, event | category | flops | bytes accessed | tf_op | source)
XLA Modules:
  0.0 1626.9 jit_solution(18393070877215001381)
XLA Ops:
  60.2 45.9 %qkv_project.1 = (bf16[4096,2048]{1,0:T(8,128)(2,1)}, bf16[2,4096,768]{2,1,0:T(8,128)(2,1)}) custom-call(s32[16]{0:T(128)} %dynamic_slice.3.where_ref, bf16[4096,2048]{1,0:T(8,128)(2,1)} %x_ref.6, f32[1,2048]{1,0:T(1,128)} %bitcast.80, f32[1,2048]{1,0:T(1,128)} %bitcast.92, bf16[2048,1536]{1,0:T(8,128)(2,1)} %all-gather.5.cloned.1.call-done.weight_ref.refs_3_, ...), custom_call_target="tpu_custom_call" | custom-call | flops 25769803776 | bytes 46137344 | tf_op jit(solution)/shard_map/qkv_project/pallas_call | solution.py:109
  136.8 32.1 %all-gather.7.cloned.1.call-done.weight_ref.refs_1_ = bf16[2048,2048]{1,0:T(8,128)(2,1)} async-done(((bf16[256,2048]{1,0:T(8,128)(2,1)}), bf16[2048,2048]{1,0:T(8,128)(2,1)}) %all-gather.7.cloned.1.call-update) | async-done | bytes 8388624 | tf_op jit(solution)/shard_map/all_gather | solution.py:814
  168.9 51.2 %expand.1 = (f32[4096,2048]{1,0:T(8,128)}, bf16[4096,2048]{1,0:T(8,128)(2,1)}) custom-call(bf16[4096,2048]{1,0:T(8,128)(2,1)} %get-tuple-element.609.hidden_ref, bf16[2048,2048]{1,0:T(8,128)(2,1)} %all-gather.7.cloned.1.call-done.weight_ref.refs_1_, f32[1,2048]{1,0:T(1,128)} %bitcast.91), custom_call_target="tpu_custom_call" | custom-call | flops 34359738368 | bytes 75505664 | tf_op jit(solution)/shard_map/expand/pallas_call | solution.py:176
  220.0 38.6 %all-gather.9.cloned.1.call-done.weight_ref = bf16[2048,2048]{1,0:T(8,128)(2,1)} async-done(((bf16[2048,256]{1,0:T(8,128)(2,1)}), bf16[2048,2048]{1,0:T(8,128)(2,1)}) %all-gather.9.cloned.1.call-update) | async-done | bytes 8388624 | tf_op jit(solution)/shard_map/all_gather | solution.py:815
  258.7 98.8 %shrink.1 = (bf16[4096,2048]{1,0:T(8,128)(2,1)}, bf16[4096,2048]{1,0:T(8,128)(2,1)}, f32[1,2048]{1,0:T(1,128)}, f32[1,2048]{1,0:T(1,128)}) custom-call(bf16[4096,2048]{1,0:T(8,128)(2,1)} %get-tuple-element.483.act_ref, bf16[4096,2048]{1,0:T(8,128)(2,1)} %cot_ref.6, f32[4096,2048]{1,0:T(8,128)} %get-tuple-element.334.lin_ref, ...), custom_call_target="tpu_custom_call" | custom-call | flops 68719476736 | bytes 109068288 | tf_op jit(solution)/shard_map/shrink/pallas_call | solution.py:176
  368.3 28.2 %attend.4 = (bf16[2048,256]{1,0:T(8,128)(2,1)}, f32[256,2048]{1,0:T(8,128)}, f32[1,4,2048]{2,1,0:T(4,128)}) custom-call(s32[32]{0:T(128)} %pad_add_fusion.1.group_ref.refs_0_, s32[32]{0:T(128)} %copy-done.82, s32[8]{0:T(128)} %reshape_squeeze.38.item_ref.refs_2_, ...), custom_call_target="tpu_custom_call" | custom-call | flops 19327352832 | bytes 6291456 | tf_op jit(solution)/shard_map/attend/pallas_call | solution.py:469
  398.1 34.9 %attend.5 = (bf16[2048,256]{1,0:T(8,128)(2,1)}, f32[256,2048]{1,0:T(8,128)}, f32[1,4,2048]{2,1,0:T(4,128)}) custom-call(s32[32]{0:T(128)} %pad_add_fusion.1.group_ref.refs_0_, s32[32]{0:T(128)} %copy-done.82, s32[8]{0:T(128)} %reshape_squeeze.39.item_ref.refs_2_, ...), custom_call_target="tpu_custom_call" | custom-call | flops 19327352832 | bytes 6291456 | tf_op jit(solution)/shard_map/attend/pallas_call | solution.py:469
  461.0 28.0 %attend.6 = (bf16[2048,256]{1,0:T(8,128)(2,1)}, f32[256,2048]{1,0:T(8,128)}, f32[1,4,2048]{2,1,0:T(4,128)}) custom-call(s32[32]{0:T(128)} %pad_add_fusion.1.group_ref.refs_0_, s32[32]{0:T(128)} %copy-done.82, s32[8]{0:T(128)} %reshape_squeeze.40.item_ref.refs_2_, ...), custom_call_target="tpu_custom_call" | custom-call | flops 19327352832 | bytes 6291456 | tf_op jit(solution)/shard_map/attend/pallas_call | solution.py:469
  532.4 35.0 %attend.7 = (bf16[2048,256]{1,0:T(8,128)(2,1)}, f32[256,2048]{1,0:T(8,128)}, f32[1,4,2048]{2,1,0:T(4,128)}) custom-call(s32[32]{0:T(128)} %pad_add_fusion.1.group_ref.refs_0_, s32[32]{0:T(128)} %copy-done.82, s32[8]{0:T(128)} %reshape_squeeze.41.item_ref.refs_2_, ...), custom_call_target="tpu_custom_call" | custom-call | flops 19327352832 | bytes 6291456 | tf_op jit(solution)/shard_map/attend/pallas_call | solution.py:469
  586.2 49.9 %attend_back.4 = (bf16[2048,256]{1,0:T(8,128)(2,1)}, bf16[1024,256]{1,0:T(8,128)(2,1)}, bf16[1024,256]{1,0:T(8,128)(2,1)}, f32[4096,256]{1,0:T(8,128)}, f32[4096,256]{1,0:T(8,128)}) custom-call(s32[32]{0:T(128)} %pad_add_fusion.1.group_ref.refs_0_, s32[32]{0:T(128)} %copy-done.82, s32[8]{0:T(128)} %reshape_squeeze.38.item_ref.refs_2_, ...), custom_call_target="tpu_custom_call" | custom-call | flops 38654705664 | bytes 12582912 | tf_op jit(solution)/shard_map/attend_back/pallas_call | solution.py:510
  644.8 27.0 %maximum_maximum_fusion = bf16[4096,512]{1,0:T(8,128)(2,1)} fusion(bf16[1024,256]{1,0:T(8,128)(2,1)S(1)} %copy-done.34, bf16[1024,256]{1,0:T(8,128)(2,1)S(1)} %copy-done.26, bf16[1024,256]{1,0:T(8,128)(2,1)S(1)} %copy-done.24, bf16[1024,256]{1,0:T(8,128)(2,1)S(1)} %copy-done.22, bf16[1024,256]{1,0:T(8,128)(2,1)} %get-tuple-element.387.refs_1_, ...), kind=kLoop, calls=%fused_computation.9 | loop fusion | flops 33554432 | bytes 8388608 | tf_op jit(solution)/shard_map/concatenate | solution.py:990
  682.9 64.4 %attend_back.5 = (bf16[2048,256]{1,0:T(8,128)(2,1)}, bf16[1024,256]{1,0:T(8,128)(2,1)}, bf16[1024,256]{1,0:T(8,128)(2,1)}, f32[4096,256]{1,0:T(8,128)}, f32[4096,256]{1,0:T(8,128)}) custom-call(s32[32]{0:T(128)} %pad_add_fusion.1.group_ref.refs_0_, s32[32]{0:T(128)} %copy-done.82, ...), custom_call_target="tpu_custom_call", output_to_operand_aliasing={{3}: (15, {}), {4}: (16, {})} | custom-call | flops 38654705664 | bytes 12582912 | tf_op jit(solution)/shard_map/attend_back/pallas_call | solution.py:510
  766.4 52.3 %attend_back.6 = (bf16[2048,256]{1,0:T(8,128)(2,1)}, bf16[1024,256]{1,0:T(8,128)(2,1)}, bf16[1024,256]{1,0:T(8,128)(2,1)}, f32[4096,256]{1,0:T(8,128)}, f32[4096,256]{1,0:T(8,128)}) custom-call(s32[32]{0:T(128)} %pad_add_fusion.1.group_ref.refs_0_, s32[32]{0:T(128)} %copy-done.82, ...), custom_call_target="tpu_custom_call", output_to_operand_aliasing={{3}: (15, {}), {4}: (16, {})} | custom-call | flops 38654705664 | bytes 12582912 | tf_op jit(solution)/shard_map/attend_back/pallas_call | solution.py:510
  829.9 64.3 %attend_back.7 = (bf16[2048,256]{1,0:T(8,128)(2,1)}, bf16[1024,256]{1,0:T(8,128)(2,1)}, bf16[1024,256]{1,0:T(8,128)(2,1)}, f32[4096,256]{1,0:T(8,128)}, f32[4096,256]{1,0:T(8,128)}) custom-call(s32[32]{0:T(128)} %pad_add_fusion.1.group_ref.refs_0_, s32[32]{0:T(128)} %copy-done.82, ...), custom_call_target="tpu_custom_call", output_to_operand_aliasing={{3}: (15, {}), {4}: (16, {})} | custom-call | flops 38654705664 | bytes 12582912 | tf_op jit(solution)/shard_map/attend_back/pallas_call | solution.py:510
  924.9 43.3 %convolution_convert_fusion.2 = bf16[2048,2048]{1,0:T(8,128)(2,1)} fusion(bf16[4096,2048]{1,0:T(8,128)(2,1)} %get-tuple-element.483.act_ref, bf16[4096,2048]{1,0:T(8,128)(2,1)} %cot_ref.6), kind=kOutput, calls=%fused_computation.3 | convolution fusion | flops 34363932672 | bytes 41943040 | tf_op jit(solution)/shard_map/ra,rb->ab/dot_general | solution.py:28
  1003.4 24.0 %grad_part.4.refs_5_.refs_0_.refs_1_ = bf16[1024,2048]{1,0:T(8,128)(2,1)} custom-call(bf16[4096,2048]{1,0:T(8,128)(2,1)} %get-tuple-element.589.refs_0_, bf16[2048,2048]{1,0:T(8,128)(2,1)} %all-gather.7.cloned.1.call-done.weight_ref.refs_1_, bf16[1024,1536]{1,0:T(8,128)(2,1)} %pad_maximum_fusion.1.refs_2_, ...), custom_call_target="tpu_custom_call" | custom-call | flops 15032385536 | bytes 29360128 | tf_op jit(solution)/shard_map/grad_part/pallas_call | solution.py:226
  1070.9 38.1 %collective-permute-done.22 = bf16[1024,768]{1,0:T(8,128)(2,1)} collective-permute-done((bf16[1024,768]{1,0:T(8,128)(2,1)}, bf16[1024,768]{1,0:T(8,128)(2,1)}, u32[]{:S(2)}, u32[]{:S(2)}) %collective-permute-start.22) | collective-permute-done | bytes 1572896 | tf_op jit(solution)/shard_map/ppermute | solution.py:843
  1128.4 43.3 %convolution_convert_fusion.1 = bf16[2048,2048]{1,0:T(8,128)(2,1)} fusion(bf16[4096,2048]{1,0:T(8,128)(2,1)} %get-tuple-element.609.hidden_ref, bf16[4096,2048]{1,0:T(8,128)(2,1)} %get-tuple-element.589.refs_0_), kind=kOutput, calls=%fused_computation.2 | convolution fusion | flops 34363932672 | bytes 41943040 | tf_op jit(solution)/shard_map/ra,rb->ab/dot_general | solution.py:28
  1171.7 23.5 %grad_part.5.refs_3_.refs_0_.refs_1_ = bf16[1024,2048]{1,0:T(8,128)(2,1)} custom-call(bf16[4096,2048]{1,0:T(8,128)(2,1)} %get-tuple-element.589.refs_0_, bf16[2048,2048]{1,0:T(8,128)(2,1)} %all-gather.7.cloned.1.call-done.weight_ref.refs_1_, bf16[1024,1536]{1,0:T(8,128)(2,1)} %pad_maximum_fusion.2.refs_2_, ...), custom_call_target="tpu_custom_call" | custom-call | flops 15032385536 | bytes 29360128 | tf_op jit(solution)/shard_map/grad_part/pallas_call | solution.py:226
  1254.9 24.0 %grad_part.6.refs_3_.refs_0_.refs_1_ = bf16[1024,2048]{1,0:T(8,128)(2,1)} custom-call(bf16[4096,2048]{1,0:T(8,128)(2,1)} %get-tuple-element.589.refs_0_, bf16[2048,2048]{1,0:T(8,128)(2,1)} %all-gather.7.cloned.1.call-done.weight_ref.refs_1_, bf16[1024,1536]{1,0:T(8,128)(2,1)} %pad_maximum_fusion.3.refs_2_, ...), custom_call_target="tpu_custom_call" | custom-call | flops 15032385536 | bytes 29360128 | tf_op jit(solution)/shard_map/grad_part/pallas_call | solution.py:226
  1353.9 23.7 %grad_part.7.refs_3_.refs_0_.refs_1_ = bf16[1024,2048]{1,0:T(8,128)(2,1)} custom-call(bf16[4096,2048]{1,0:T(8,128)(2,1)} %get-tuple-element.589.refs_0_, bf16[2048,2048]{1,0:T(8,128)(2,1)} %all-gather.7.cloned.1.call-done.weight_ref.refs_1_, bf16[1024,1536]{1,0:T(8,128)(2,1)} %copy-done.4, bf16[2048,1536]{1,0:T(8,128)(2,1)} %all-gather.5.cloned.1.call-done.weight_ref.refs_3_), custom_call_target="tpu_custom_call" | custom-call | flops 15032385536 | bytes 29360128 | tf_op jit(solution)/shard_map/grad_part/pallas_call | solution.py:226
  1408.5 34.1 %convolution_convert_fusion = bf16[2048,1536]{1,0:T(8,128)(2,1)} fusion(bf16[4096,2048]{1,0:T(8,128)(2,1)} %get-tuple-element.609.hidden_ref, bf16[4096,1536]{1,0:T(8,128)(2,1)} %constant_dynamic-update-slice_fusion), kind=kOutput, calls=%fused_computation.1 | convolution fusion | flops 25772949504 | bytes 35651584 | tf_op jit(solution)/shard_map/ra,rb->ab/dot_general | solution.py:28
  1452.4 41.7 %collective-permute-done.37.refs_1_.c = bf16[512,2048]{1,0:T(8,128)(2,1)S(1)} collective-permute-done((bf16[512,2048]{1,0:T(8,128)(2,1)}, bf16[512,2048]{1,0:T(8,128)(2,1)S(1)}, u32[]{:S(2)}, u32[]{:S(2)}) %collective-permute-start.37) | collective-permute-done | bytes 2097184 | tf_op jit(solution)/shard_map/ppermute | solution.py:787
  1521.4 27.0 %collective-permute-done.39.a = bf16[512,2048]{1,0:T(8,128)(2,1)S(1)} collective-permute-done((bf16[512,2048]{1,0:T(8,128)(2,1)}, bf16[512,2048]{1,0:T(8,128)(2,1)S(1)}, u32[]{:S(2)}, u32[]{:S(2)}) %collective-permute-start.39) | collective-permute-done | bytes 2097184 | tf_op jit(solution)/shard_map/ppermute | solution.py:787
  (400 shorter events, 638.0 us)
Async XLA Ops:
  11.8 102.7 %all-gather.11.cloned.1.call-start = ((), (), s32[]{:S(2)}) async-start(), calls=%async_computation.9 | async-start | bytes 2359296 | tf_op jit(solution)/shard_map/all_gather | solution.py:816
  12.6 156.3 %all-gather.7.cloned.1.call-start = ((), (), s32[]{:S(2)}) async-start(), calls=%async_computation.7 | async-start | bytes 9437184 | tf_op jit(solution)/shard_map/all_gather | solution.py:814
  13.3 245.3 %all-gather.9.cloned.1.call-start = ((), (), s32[]{:S(2)}) async-start(), calls=%async_computation.8 | async-start | bytes 9437184 | tf_op jit(solution)/shard_map/all_gather | solution.py:815
  106.2 251.3 %all-to-all-start = ((bf16[2,4096,768]{2,1,0:T(8,128)(2,1)}), bf16[2,4096,768]{2,1,0:T(8,128)(2,1)}, u32[]{:S(2)}, u32[]{:S(2)}) async-start(bf16[2,4096,768]{2,1,0:T(8,128)(2,1)} %get-tuple-element.331), calls=%async_computation | async-start | bytes 25165824 | tf_op jit(solution)/shard_map/all_to_all | solution.py:849
  518.0 64.1 %all-to-all-start.1 = ((bf16[2,4096,256]{2,1,0:T(8,128)(2,1)}), bf16[2,4096,256]{2,1,0:T(8,128)(2,1)}, u32[]{:S(2)}, u32[]{:S(2)}) async-start(bf16[2,4096,256]{2,1,0:T(8,128)(2,1)} %pad_maximum_fusion), calls=%async_computation.1 | async-start | bytes 8388608 | tf_op jit(solution)/shard_map/all_to_all | solution.py:849
  523.6 1026.6 %reduce-scatter.7.cloned.1.call-start = ((), (), s32[]{:S(2)}) async-start(), calls=%async_computation.11 | async-start | bytes 2359296 | tf_op jit(solution)/shard_map/reduce_scatter | solution.py:965
  582.1 89.7 %collective-permute-start.7 = (bf16[512,2048]{1,0:T(8,128)(2,1)}, bf16[512,2048]{1,0:T(8,128)(2,1)S(1)}, u32[]{:S(2)}, u32[]{:S(2)}) collective-permute-start(bf16[512,2048]{1,0:T(8,128)(2,1)} %line_begin.10.b), channel_id=1, source_target_pairs={{0,1},{3,2},{1,0},{2,3},{4,5},{7,6},{5,4},{6,7},{8,9},{11,10},{9,8... | collective-permute-start | bytes 6291464 | tf_op jit(solution)/shard_map/ppermute | solution.py:787
  585.5 86.3 %collective-permute-start.8 = (bf16[512,2048]{1,0:T(8,128)(2,1)}, bf16[512,2048]{1,0:T(8,128)(2,1)S(1)}, u32[]{:S(2)}, u32[]{:S(2)}) collective-permute-start(bf16[512,2048]{1,0:T(8,128)(2,1)} %line_begin.10.b), channel_id=1, source_target_pairs={{1,2},{2,1},{5,6},{6,5},{9,10},{10,9},{13,14},{14,13},{17,18},{18,... | collective-permute-start | bytes 6291464 | tf_op jit(solution)/shard_map/ppermute | solution.py:788
  679.2 68.2 %collective-permute-start.9 = (bf16[512,2048]{1,0:T(8,128)(2,1)}, bf16[512,2048]{1,0:T(8,128)(2,1)S(1)}, u32[]{:S(2)}, u32[]{:S(2)}) collective-permute-start(bf16[512,2048]{1,0:T(8,128)(2,1)} %get-tuple-element.400), channel_id=1, source_target_pairs={{0,1},{3,2},{1,0},{2,3},{4,5},{7,6},{5,4},{6,7},{8,9},{11,10},{9,8... | collective-permute-start | bytes 6291464 | tf_op jit(solution)/shard_map/ppermute | solution.py:787
  682.1 65.2 %collective-permute-start.10 = (bf16[512,2048]{1,0:T(8,128)(2,1)}, bf16[512,2048]{1,0:T(8,128)(2,1)S(1)}, u32[]{:S(2)}, u32[]{:S(2)}) collective-permute-start(bf16[512,2048]{1,0:T(8,128)(2,1)} %get-tuple-element.401), channel_id=1, source_target_pairs={{1,2},{2,1},{5,6},{6,5},{9,10},{10,9},{13,14},{14,13},{17,18},{18,... | collective-permute-start | bytes 6291464 | tf_op jit(solution)/shard_map/ppermute | solution.py:788
  754.5 64.3 %collective-permute-start.11 = (bf16[512,2048]{1,0:T(8,128)(2,1)}, bf16[512,2048]{1,0:T(8,128)(2,1)S(1)}, u32[]{:S(2)}, u32[]{:S(2)}) collective-permute-start(bf16[512,2048]{1,0:T(8,128)(2,1)} %line_begin.11.b), channel_id=1, source_target_pairs={{0,1},{3,2},{1,0},{2,3},{4,5},{7,6},{5,4},{6,7},{8,9},{11,10},{9,8... | collective-permute-start | bytes 6291464 | tf_op jit(solution)/shard_map/ppermute | solution.py:787
  757.7 61.0 %collective-permute-start.12 = (bf16[512,2048]{1,0:T(8,128)(2,1)}, bf16[512,2048]{1,0:T(8,128)(2,1)S(1)}, u32[]{:S(2)}, u32[]{:S(2)}) collective-permute-start(bf16[512,2048]{1,0:T(8,128)(2,1)} %line_begin.11.b), channel_id=1, source_target_pairs={{1,2},{2,1},{5,6},{6,5},{9,10},{10,9},{13,14},{14,13},{17,18},{18,... | collective-permute-start | bytes 6291464 | tf_op jit(solution)/shard_map/ppermute | solution.py:788
  826.3 81.2 %collective-permute-start.13 = (bf16[512,2048]{1,0:T(8,128)(2,1)}, bf16[512,2048]{1,0:T(8,128)(2,1)S(1)}, u32[]{:S(2)}, u32[]{:S(2)}) collective-permute-start(bf16[512,2048]{1,0:T(8,128)(2,1)} %get-tuple-element.446), channel_id=1, source_target_pairs={{0,1},{3,2},{1,0},{2,3},{4,5},{7,6},{5,4},{6,7},{8,9},{11,10},{9,8... | collective-permute-start | bytes 6291464 | tf_op jit(solution)/shard_map/ppermute | solution.py:787
  829.1 78.3 %collective-permute-start.14 = (bf16[512,2048]{1,0:T(8,128)(2,1)}, bf16[512,2048]{1,0:T(8,128)(2,1)S(1)}, u32[]{:S(2)}, u32[]{:S(2)}) collective-permute-start(bf16[512,2048]{1,0:T(8,128)(2,1)} %get-tuple-element.447), channel_id=1, source_target_pairs={{1,2},{2,1},{5,6},{6,5},{9,10},{10,9},{13,14},{14,13},{17,18},{18,... | collective-permute-start | bytes 6291464 | tf_op jit(solution)/shard_map/ppermute | solution.py:788
  917.9 72.0 %collective-permute-start.17 = (bf16[1024,768]{1,0:T(8,128)(2,1)}, bf16[1024,768]{1,0:T(8,128)(2,1)}, u32[]{:S(2)}, u32[]{:S(2)}) collective-permute-start(bf16[1024,768]{1,0:T(8,128)(2,1)} %broadcast_select_fusion.14), channel_id=1, source_target_pairs={{0,4},{4,0},{1,5},{5,1},{2,6},{6,2},{3,7},{7,3},{8,12},{12,8},{9,1... | collective-permute-start | bytes 4718600 | tf_op jit(solution)/shard_map/ppermute | solution.py:843
  919.6 75.1 %collective-permute-start.15 = (bf16[512,2048]{1,0:T(8,128)(2,1)S(1)}, bf16[512,2048]{1,0:T(8,128)(2,1)}, u32[]{:S(2)}, u32[]{:S(2)}) collective-permute-start(bf16[512,2048]{1,0:T(8,128)(2,1)S(1)} %copy-done.5), channel_id=1, source_target_pairs={{0,1},{3,2},{1,0},{2,3},{4,5},{7,6},{5,4},{6,7},{8,9},{11,10},{9,8... | collective-permute-start | bytes 6291464 | tf_op jit(solution)/shard_map/ppermute | solution.py:787
  922.8 71.8 %collective-permute-start.16 = (bf16[512,2048]{1,0:T(8,128)(2,1)S(1)}, bf16[512,2048]{1,0:T(8,128)(2,1)}, u32[]{:S(2)}, u32[]{:S(2)}) collective-permute-start(bf16[512,2048]{1,0:T(8,128)(2,1)S(1)} %copy-done.5), channel_id=1, source_target_pairs={{1,2},{2,1},{5,6},{6,5},{9,10},{10,9},{13,14},{14,13},{17,18},{18,... | collective-permute-start | bytes 6291464 | tf_op jit(solution)/shard_map/ppermute | solution.py:788
  994.7 557.2 %reduce-scatter.11.cloned.1.call-start = ((), (), s32[]{:S(2)}) async-start(), calls=%async_computation.13 | async-start | bytes 9437184 | tf_op jit(solution)/shard_map/reduce_scatter | solution.py:965
  995.3 565.7 %reduce-scatter.9.cloned.1.call-start = ((), (), s32[]{:S(2)}) async-start(), calls=%async_computation.12 | async-start | bytes 9437184 | tf_op jit(solution)/shard_map/reduce_scatter | solution.py:965
  1057.9 55.4 %collective-permute-start.20 = (bf16[512,2048]{1,0:T(8,128)(2,1)S(1)}, bf16[512,2048]{1,0:T(8,128)(2,1)S(1)}, u32[]{:S(2)}, u32[]{:S(2)}) collective-permute-start(bf16[512,2048]{1,0:T(8,128)(2,1)S(1)} %copy-done.6), channel_id=1, source_target_pairs={{0,1},{3,2},{1,0},{2,3},{4,5},{7,6},{5,4},{6,7},{8,9},{11,10},{9,8... | collective-permute-start | bytes 6291464 | tf_op jit(solution)/shard_map/ppermute | solution.py:787
  1121.5 73.8 %collective-permute-start.23 = (bf16[512,2048]{1,0:T(8,128)(2,1)}, bf16[512,2048]{1,0:T(8,128)(2,1)S(1)}, u32[]{:S(2)}, u32[]{:S(2)}) collective-permute-start(bf16[512,2048]{1,0:T(8,128)(2,1)} %get-tuple-element.521), channel_id=1, source_target_pairs={{0,1},{3,2},{1,0},{2,3},{4,5},{7,6},{5,4},{6,7},{8,9},{11,10},{9,8... | collective-permute-start | bytes 6291464 | tf_op jit(solution)/shard_map/ppermute | solution.py:787
  1126.4 68.9 %collective-permute-start.24 = (bf16[512,2048]{1,0:T(8,128)(2,1)}, bf16[512,2048]{1,0:T(8,128)(2,1)}, u32[]{:S(2)}, u32[]{:S(2)}) collective-permute-start(bf16[512,2048]{1,0:T(8,128)(2,1)} %get-tuple-element.522), channel_id=1, source_target_pairs={{1,2},{2,1},{5,6},{6,5},{9,10},{10,9},{13,14},{14,13},{17,18},{18,... | collective-permute-start | bytes 6291464 | tf_op jit(solution)/shard_map/ppermute | solution.py:788
  1209.9 404.7 %reduce-scatter.5.cloned.1.call-start = ((), (), s32[]{:S(2)}) async-start(), calls=%async_computation.10 | async-start | bytes 7077888 | tf_op jit(solution)/shard_map/reduce_scatter | solution.py:965
  1388.0 54.6 %collective-permute-start.35 = (bf16[512,2048]{1,0:T(8,128)(2,1)}, bf16[512,2048]{1,0:T(8,128)(2,1)S(1)}, u32[]{:S(2)}, u32[]{:S(2)}) collective-permute-start(bf16[512,2048]{1,0:T(8,128)(2,1)} %line_begin.16.b), channel_id=1, source_target_pairs={{0,1},{3,2},{1,0},{2,3},{4,5},{7,6},{5,4},{6,7},{8,9},{11,10},{9,8... | collective-permute-start | bytes 6291464 | tf_op jit(solution)/shard_map/ppermute | solution.py:787
  (111 other events, 1796.0 us)
Sparse Core Ops, SparseCore 0:
  12.0 48.2 all-gather.4
  62.1 28.1 all-gather.10
  92.2 76.6 all-gather.6
  170.6 87.9 all-gather.8
  994.8 40.1 reduce-scatter.6
  1038.7 89.2 reduce-scatter.10
  1210.0 70.7 reduce-scatter.8
  1442.8 60.7 reduce-scatter.4

commit v3 on v2

--- a/solution.py
+++ b/solution.py
@@ -20,6 +20,10 @@
 NN = (((1,), (0,)), ((), ()))
 
 
+def cost(bytes_accessed, flops=0):
+    return pl.CostEstimate(flops=flops, bytes_accessed=bytes_accessed, transcendentals=0)
+
+
 def dot(left, right, dims):
     return lax.dot_general(left, right, dims, preferred_element_type=F32)
 
@@ -40,9 +44,11 @@
 
 def gelu_parts(v):
     scale = (2.0 / jnp.pi) ** 0.5
-    t = jnp.tanh(scale * (v + 0.044715 * v * v * v))
-    value = 0.5 * v * (1.0 + t)
-    slope = 0.5 * (1.0 + t) + 0.5 * v * (1.0 - t * t) * (scale * (1.0 + 3 * 0.044715 * v * v))
+    square = v * v
+    t = jnp.tanh(v * (scale + (scale * 0.044715) * square))
+    half = 0.5 * v
+    value = half + half * t
+    slope = (0.5 + 0.5 * t) + (half - half * t * t) * (scale + (scale * 3 * 0.044715) * square)
     return value, slope
 
 
@@ -72,18 +78,33 @@
     )
 
 
+def ahead(count, first, second):
+    held = first(0)
+    for i in range(count):
+        following = first(i + 1) if i + 1 < count else None
+        second(i, held)
+        held = following
+
+
+def norm_kernel(x_ref, gain_ref, shift_ref, out_ref):
+    x = x_ref[...].astype(F32)
+    out_ref[...] = norm_apply(x, gain_ref[...], shift_ref[...]).astype(BF16)
+
+
 def qkv_kernel(
-    share, where_ref, x_ref, gain_ref, shift_ref, weight_ref, bias_ref, cos_ref, first_ref,
-    second_ref, hidden_ref, out_ref,
+    share, where_ref, hidden_ref, weight_ref, bias_ref, cos_ref, first_ref, second_ref, out_ref
 ):
-    x = x_ref[...].astype(F32)
-    hidden = norm_apply(x, gain_ref[...], shift_ref[...]).astype(BF16)
-    hidden_ref[...] = hidden
+    hidden = hidden_ref[...]
     cosine, first, second = cos_ref[...], first_ref[...], second_ref[...]
     lane = lax.broadcasted_iota(jnp.int32, (1, 2 * HDIM), 1)
     member_width = out_ref.shape[2]
-    for begin in range(0, weight_ref.shape[1], 512):
-        lin = dot(hidden, weight_ref[:, begin : begin + 512], NN) + bias_ref[:, begin : begin + 512]
+
+    def linear(i):
+        at = slice(i * 512, (i + 1) * 512)
+        return dot(hidden, weight_ref[:, at], NN) + bias_ref[:, at]
+
+    def turn(i, lin):
+        begin = i * 512
         for column in range(0, 512, 2 * HDIM):
             part = lin[:, column : column + 2 * HDIM]
             turns = [((begin + column + off) // share) % 3 < 2 for off in (0, HDIM)]
@@ -94,14 +115,16 @@
                     turned = jnp.where(keep, turned, part)
                 part = turned
             part = part.astype(BF16)
-            for off in range(0, 2 * HDIM, min(2 * HDIM, share)):
-                size = min(2 * HDIM, share)
+            size = min(2 * HDIM, share)
+            for off in range(0, 2 * HDIM, size):
                 member, place = divmod(begin + column + off, member_width)
                 out_ref[member, :, place : place + size] = part[:, off : off + size]
 
-
-def qkv_project(x, gain, shift, weight, bias, tables, spots, share):
-    rows, width = x.shape
+    ahead(weight_ref.shape[1] // 512, linear, turn)
+
+
+def qkv_project(hidden, weight, bias, tables, spots, share):
+    rows, width = hidden.shape
     outs = weight.shape[1]
     count = 256
     whole = lambda shape: pl.BlockSpec(shape, lambda i, *_: (0, 0))
@@ -113,58 +136,95 @@
             grid=(rows // count,),
             in_specs=[
                 pl.BlockSpec((count, width), lambda i, *_: (i, 0)),
-                whole((1, width)),
-                whole((1, width)),
                 whole((width, outs)),
                 whole((1, outs)),
                 table,
                 table,
                 table,
             ],
-            out_specs=[
-                pl.BlockSpec((count, width), lambda i, *_: (i, 0)),
-                pl.BlockSpec((outs // (3 * share), count, 3 * share), lambda i, *_: (0, i, 0)),
-            ],
-        ),
-        out_shape=[
-            jax.ShapeDtypeStruct((rows, width), BF16),
-            jax.ShapeDtypeStruct((outs // (3 * share), rows, 3 * share), BF16),
-        ],
+            out_specs=pl.BlockSpec(
+                (outs // (3 * share), count, 3 * share), lambda i, *_: (0, i, 0)
+            ),
+        ),
+        out_shape=jax.ShapeDtypeStruct((outs // (3 * share), rows, 3 * share), BF16),
         compiler_params=pltpu.CompilerParams(vmem_limit_bytes=VMEM),
         cost_estimate=pl.CostEstimate(
             flops=2 * rows * width * outs, bytes_accessed=2 * rows * (2 * width + outs),
             transcendentals=0,
         ),
         name="qkv_project",
-    )(spots, x, gain, shift, weight, bias, *tables)
-
-
-def expand_kernel(hidden_ref, weight_ref, bias_ref, lin_ref, out_ref):
+    )(spots, hidden, weight, bias, *tables)
+
+
+def expand_kernel(hidden_ref, weight_ref, bias_ref, slope_ref, out_ref):
     hidden = hidden_ref[...]
-    for begin in range(0, weight_ref.shape[1], 512):
-        at = slice(begin, begin + 512)
-        lin = dot(hidden, weight_ref[:, at], NN) + bias_ref[:, at]
-        lin_ref[:, at] = lin
-        out_ref[:, at] = gelu_parts(lin)[0].astype(BF16)
-
-
-def shrink_kernel(act_ref, cot_ref, lin_ref, weight_ref, out_ref, grad_ref, sum_ref, cot_sum_ref):
+
+    def linear(i):
+        at = slice(i * 512, (i + 1) * 512)
+        return dot(hidden, weight_ref[:, at], NN) + bias_ref[:, at]
+
+    def keep(i, lin):
+        at = slice(i * 512, (i + 1) * 512)
+        value, slope = gelu_parts(lin)
+        out_ref[:, at] = value.astype(BF16)
+        slope_ref[:, at] = slope.astype(BF16)
+
+    ahead(weight_ref.shape[1] // 512, linear, keep)
+
+
+def shrink_kernel(act_ref, weight_ref, out_ref):
+    out_ref[...] = dot(act_ref[...], weight_ref[...], NN).astype(BF16)
+
+
+def slope_kernel(cot_ref, slope_ref, weight_ref, grad_ref, sum_ref, cot_sum_ref):
     @pl.when(pl.program_id(0) == 0)
     def _():
         sum_ref[...] = jnp.zeros_like(sum_ref)
         cot_sum_ref[...] = jnp.zeros_like(cot_sum_ref)
 
-    act, cot = act_ref[...], cot_ref[...]
-    for begin in range(0, weight_ref.shape[0], 512):
-        at = slice(begin, begin + 512)
-        slope = gelu_parts(lin_ref[:, at])[1]
-        grad = (slope * dot(cot, weight_ref[at, :], NT)).astype(BF16)
+    cot = cot_ref[...]
+    cot_sum_ref[...] += jnp.sum(cot.astype(F32), axis=0, keepdims=True)
+
+    def back(i):
+        return dot(cot, weight_ref[i * 512 : (i + 1) * 512, :], NT)
+
+    def keep(i, grad):
+        at = slice(i * 512, (i + 1) * 512)
+        grad = (slope_ref[:, at].astype(F32) * grad).astype(BF16)
         grad_ref[:, at] = grad
         sum_ref[:, at] += jnp.sum(grad.astype(F32), axis=0, keepdims=True)
-    for begin in range(0, weight_ref.shape[1], 512):
-        at = slice(begin, begin + 512)
-        out_ref[:, at] = dot(act, weight_ref[:, at], NN).astype(BF16)
-        cot_sum_ref[:, at] += jnp.sum(cot_ref[:, at].astype(F32), axis=0, keepdims=True)
+
+    ahead(weight_ref.shape[0] // 512, back, keep)
+
+
+def grad_attended_kernel(cot_ref, weight_ref, out_ref):
+    cot = cot_ref[...]
+    share = out_ref.shape[2]
+    whole = dot(cot, weight_ref[...], NT).astype(BF16)
+    for c in range(out_ref.shape[0]):
+        out_ref[c] = whole[:, c * share : (c + 1) * share]
+
+
+def grad_attended(cotangent, weight, share):
+    rows, width = cotangent.shape
+    local = weight.shape[0]
+    count = 512
+    return pl.pallas_call(
+        grad_attended_kernel,
+        grid=(rows // count,),
+        in_specs=[
+            pl.BlockSpec((count, width), lambda i: (i, 0)),
+            pl.BlockSpec((local, width), lambda i: (0, 0)),
+        ],
+        out_specs=pl.BlockSpec((local // share, count, share), lambda i: (0, i, 0)),
+        out_shape=jax.ShapeDtypeStruct((local // share, rows, share), BF16),
+        compiler_params=pltpu.CompilerParams(vmem_limit_bytes=VMEM),
+        cost_estimate=pl.CostEstimate(
+            flops=2 * rows * width * local, bytes_accessed=2 * rows * (width + local),
+            transcendentals=0,
+        ),
+        name="grad_attended",
+    )(cotangent, weight)
 
 
 def row_call(kernel, name, count, rows, in_arrays, outs, flops):
@@ -304,25 +364,25 @@
     o_ref[...] = ot_ref[...].T.astype(BF16)
 
 
-def turn_kernel(k_ref, v_ref, kt_ref, vt_ref):
-    kt_ref[...] = k_ref[...].T
-    vt_ref[...] = v_ref[...].T
-
-
-def turn_prompts(qkv, width):
+def turn_kernel(in_ref, out_ref):
+    for begin in range(0, in_ref.shape[0], CLEN):
+        out_ref[:, begin : begin + CLEN] = in_ref[begin : begin + CLEN, :].T
+
+
+def turn_prompts(qkv, width, which):
     wide = min(4 * HDIM, width)
-    (_, k, v), (_, ka, va) = split_columns(qkv, width)
-    block = lambda at: pl.BlockSpec((CLEN, wide), lambda h, i: (i, at + h))
-    turned = pl.BlockSpec((wide, CLEN), lambda h, i: (h, i))
+    arrays, ats = split_columns(qkv, width)
+    count = PLEN // 2
     return pl.pallas_call(
         turn_kernel,
-        grid=(width // wide, GPR * PLEN // CLEN),
-        in_specs=[block(ka), block(va)],
-        out_specs=[turned, turned],
-        out_shape=[jax.ShapeDtypeStruct((width, GPR * PLEN), BF16)] * 2,
+        grid=(width // wide, GPR * PLEN // count),
+        in_specs=[pl.BlockSpec((count, wide), lambda h, i: (i, ats[which] + h))],
+        out_specs=pl.BlockSpec((wide, count), lambda h, i: (h, i)),
+        out_shape=jax.ShapeDtypeStruct((width, GPR * PLEN), BF16),
         compiler_params=pltpu.CompilerParams(vmem_limit_bytes=VMEM),
+        cost_estimate=cost(width * GPR * PLEN * 8),
         name="turn_prompts",
-    )(k, v)
+    )(arrays[which])
 
 
 def turned_back(values, tables):
@@ -427,15 +487,17 @@
 def finish_prompts(dk, dv, tables):
     rows, width = dk.shape
     wide = min(4 * HDIM, width)
-    block = pl.BlockSpec((CLEN, wide), lambda h, i: (i, h))
-    table = pl.BlockSpec((CLEN, 2 * HDIM), lambda h, i: (i % (PLEN // CLEN), 0))
+    count = PLEN // 2
+    block = pl.BlockSpec((count, wide), lambda h, i: (i, h))
+    table = pl.BlockSpec((count, 2 * HDIM), lambda h, i: (i % (PLEN // count), 0))
     return pl.pallas_call(
         finish_kernel,
-        grid=(width // wide, rows // CLEN),
+        grid=(width // wide, rows // count),
         in_specs=[block, block, table, table, table],
         out_specs=[block, block],
         out_shape=[jax.ShapeDtypeStruct((rows, width), BF16)] * 2,
         compiler_params=pltpu.CompilerParams(vmem_limit_bytes=VMEM),
+        cost_estimate=cost(rows * width * 30),
         name="finish_prompts",
     )(dk, dv, *tables)
 
@@ -541,7 +603,7 @@
     return lax.optimization_barrier(trees)
 
 
-COUNT = 128
+COUNT = 256
 
 
 def begin_kernel(names, flag_ref, *refs):
@@ -610,22 +672,25 @@
         ),
         out_shape=[jax.ShapeDtypeStruct((rows, width), BF16) for _ in outs],
         compiler_params=pltpu.CompilerParams(vmem_limit_bytes=VMEM),
+        cost_estimate=cost(rows * width * 16),
         name=name,
     )(flags, *[i[1] for i in ins])
 
 
-def total_specs(half, width):
+def total_specs(half, width, begin):
     outer = lambda flag: flag[0]
     inner = lambda flag: 1 - flag[0]
 
     def spec(part, who):
-        return pl.BlockSpec((COUNT, width), lambda p, i, flag: (i * who(flag) * (p == part), 0))
+        return pl.BlockSpec(
+            (COUNT, width), lambda p, i, flag: (i * who(flag) * (p + begin == part), 0)
+        )
 
     return [spec(0, outer), spec(0, inner), spec(1, outer), spec(1, inner)]
 
 
-def total_of(flag_ref, refs, keep):
-    part = pl.program_id(0)
+def total_of(flag_ref, refs, keep, begin):
+    part = pl.program_id(0) + begin
     for at, ref in enumerate(refs):
         right = (part == at // 2) & (flag_ref[0] == 1 - at % 2)
 
@@ -634,11 +699,11 @@
             keep(ref[...])
 
 
-def rows_of(block, half):
+def rows_of(block, half, begin):
     steps = half // COUNT
 
     def index(p, i, flag):
-        return ((2 * block + (flag[1] + p) % 2) * steps + i, 0)
+        return ((2 * block + (flag[1] + p + begin) % 2) * steps + i, 0)
 
     return index
 
@@ -649,7 +714,7 @@
     def keep(value):
         out_ref[...] = value
 
-    total_of(flag_ref, (a, b, c, d), keep)
+    total_of(flag_ref, (a, b, c, d), keep, 0)
 
 
 def place_total(flags, four, block, rows, before):
@@ -659,71 +724,104 @@
         grid_spec=pltpu.PrefetchScalarGridSpec(
             num_scalar_prefetch=1,
             grid=(2, half // COUNT),
-            in_specs=total_specs(half, width)
+            in_specs=total_specs(half, width, 0)
             + [pl.BlockSpec(memory_space=pl.ANY)] * (before is not None),
-            out_specs=pl.BlockSpec((COUNT, width), rows_of(block, half)),
+            out_specs=pl.BlockSpec((COUNT, width), rows_of(block, half, 0)),
         ),
         out_shape=jax.ShapeDtypeStruct((rows, width), BF16),
         input_output_aliases={} if before is None else {5: 0},
         compiler_params=pltpu.CompilerParams(vmem_limit_bytes=VMEM),
+        cost_estimate=cost(half * width * 24),
         name="place_total",
     )(flags, *four, *(() if before is None else (before,)))
 
 
-def norm_back_kernel(flag_ref, a, b, c, d, x_ref, cot_ref, gain_ref, *rest):
-    out_ref, gain_sum, shift_sum, held = rest[-4:]
-
-    @pl.when((pl.program_id(0) == 0) & (pl.program_id(1) == 0))
+def normed_rows(x_ref):
+    x = x_ref[...].astype(F32)
+    center = x - jnp.mean(x, axis=-1, keepdims=True)
+    inverse = lax.rsqrt(jnp.mean(center * center, axis=-1, keepdims=True) + 1e-05)
+    return center * inverse, inverse
+
+
+def norm_back_kernel(begin, flag_ref, a, b, c, d, x_ref, cot_ref, gain_ref, *rest):
+    out_ref, held = rest[-2:]
+
+    def keep(value):
+        held[...] = value.astype(F32) * gain_ref[...]
+
+    total_of(flag_ref, (a, b, c, d), keep, begin)
+    normed, inverse = normed_rows(x_ref)
+    scaled = held[...]
+    grad = scaled - jnp.mean(scaled, axis=-1, keepdims=True)
+    grad = inverse * (grad - normed * jnp.mean(scaled * normed, axis=-1, keepdims=True))
+    out_ref[...] = cot_ref[...].astype(F32) + grad
+
+
+def norm_back(flags, four, block, tokens, cotangent, gain, before, begin, count):
+    half, width = four[0].shape
+    row = pl.BlockSpec((1, width), lambda p, i, flag: (0, 0))
+    whole = pl.BlockSpec((COUNT, width), rows_of(block, half, begin))
+    return pl.pallas_call(
+        functools.partial(norm_back_kernel, begin),
+        grid_spec=pltpu.PrefetchScalarGridSpec(
+            num_scalar_prefetch=1,
+            grid=(count, half // COUNT),
+            in_specs=total_specs(half, width, begin)
+            + [whole, whole, row]
+            + [pl.BlockSpec(memory_space=pl.ANY)] * (before is not None),
+            out_specs=whole,
+            scratch_shapes=[pltpu.VMEM((COUNT, width), F32)],
+        ),
+        out_shape=jax.ShapeDtypeStruct(tokens.shape, F32),
+        input_output_aliases={} if before is None else {8: 0},
+        compiler_params=pltpu.CompilerParams(vmem_limit_bytes=VMEM),
+        cost_estimate=cost(half * width * 24 * count),
+        name="norm_back",
+    )(flags, *four, tokens, cotangent, gain, *(() if before is None else (before,)))
+
+
+def norm_sums_kernel(flag_ref, total_ref, x_ref, gain_sum, shift_sum):
+    @pl.when(pl.program_id(0) == 0)
     def _():
         gain_sum[...] = jnp.zeros_like(gain_sum)
         shift_sum[...] = jnp.zeros_like(shift_sum)
 
-    def keep(value):
-        held[...] = value.astype(F32)
-
-    total_of(flag_ref, (a, b, c, d), keep)
-    x = x_ref[...].astype(F32)
-    center = x - jnp.mean(x, axis=-1, keepdims=True)
-    inverse = lax.rsqrt(jnp.mean(center * center, axis=-1, keepdims=True) + 1e-05)
-    normed = center * inverse
-    total = held[...]
-    gain_sum[...] += jnp.sum(total * normed, axis=0, keepdims=True)
-    shift_sum[...] += jnp.sum(total, axis=0, keepdims=True)
-    scaled = total * gain_ref[...]
-    grad = scaled - jnp.mean(scaled, axis=-1, keepdims=True)
-    grad = inverse * (grad - normed * jnp.mean(scaled * normed, axis=-1, keepdims=True))
-    out_ref[...] = cot_ref[...].astype(F32) + grad
-
-
-def norm_back(flags, four, block, tokens, cotangent, gain, before):
-    half, width = four[0].shape
-    row = pl.BlockSpec((1, width), lambda p, i, flag: (0, 0))
-    whole = pl.BlockSpec((COUNT, width), rows_of(block, half))
+    @pl.when(flag_ref[0] == 0)
+    def _():
+        total = total_ref[...].astype(F32)
+        gain_sum[...] += jnp.sum(total * normed_rows(x_ref)[0], axis=0, keepdims=True)
+        shift_sum[...] += jnp.sum(total, axis=0, keepdims=True)
+
+
+def norm_sums(flags, near, block, tokens):
+    half, width = near.shape
+    steps = half // COUNT
+    row = pl.BlockSpec((1, width), lambda i, flag: (0, 0))
     return pl.pallas_call(
-        norm_back_kernel,
+        norm_sums_kernel,
         grid_spec=pltpu.PrefetchScalarGridSpec(
             num_scalar_prefetch=1,
-            grid=(2, half // COUNT),
-            in_specs=total_specs(half, width)
-            + [whole, whole, row]
-            + [pl.BlockSpec(memory_space=pl.ANY)] * (before is not None),
-            out_specs=[whole, row, row],
-            scratch_shapes=[pltpu.VMEM((COUNT, width), F32)],
-        ),
-        out_shape=[
-            jax.ShapeDtypeStruct(tokens.shape, F32),
-            jax.ShapeDtypeStruct((1, width), F32),
-            jax.ShapeDtypeStruct((1, width), F32),
-        ],
-        input_output_aliases={} if before is None else {8: 0},
+            grid=(steps,),
+            in_specs=[
+                pl.BlockSpec((COUNT, width), lambda i, flag: (i * (1 - flag[0]), 0)),
+                pl.BlockSpec(
+                    (COUNT, width),
+                    lambda i, flag: ((2 * block + flag[1]) * steps + i * (1 - flag[0]), 0),
+                ),
+            ],
+            out_specs=[row, row],
+        ),
+        out_shape=[jax.ShapeDtypeStruct((1, width), F32)] * 2,
         compiler_params=pltpu.CompilerParams(vmem_limit_bytes=VMEM),
-        name="norm_back",
-    )(flags, *four, tokens, cotangent, gain, *(() if before is None else (before,)))
+        cost_estimate=cost(half * width * 10),
+        name="norm_sums",
+    )(flags, near, tokens)
 
 
 class Line:
     def __init__(self, flags, tokens, bias):
         self.flags, self.tokens, self.bias = flags, tokens, bias
+        self.outer = flags[0] == 1
         self.part = self.near = None
         self.block = -1
 
@@ -812,8 +910,6 @@
     gather = functools.partial(lax.all_gather, axis_name=("dp", "ctx"), tiled=True)
     qkv_weight = gather(mixed(w_query, w_key, w_value), axis=0)
     expand_weight = gather(w_fc1, axis=0)
-    shrink_weight = gather(w_fc2, axis=1)
-    dense_weight = gather(w_dense, axis=1)
     qkv_bias = mixed(b_query, b_key, b_value).astype(F32)[None]
 
     per_prompt = PLEN // CLEN
@@ -831,55 +927,57 @@
 
     gain = ln_gain.astype(F32)
     shift = ln_bias.astype(F32)
-    hidden, qkv = qkv_project(
-        tokens, gain[None], shift[None], qkv_weight, qkv_bias, tables, own_spots, share
+    (hidden,) = row_call(
+        norm_kernel, "norm", 256, rows, (tokens, gain[None], shift[None]),
+        (jax.ShapeDtypeStruct((rows, width), BF16),), 0,
     )
-
-    def exchange(parts):
+    hidden, tables, qkv_weight, fc2_shard = tie(hidden, tables, qkv_weight, w_fc2)
+    shrink_weight = gather(fc2_shard, axis=1)
+    qkv = qkv_project(hidden, qkv_weight, qkv_bias, tables, own_spots, share)
+
+    def start_exchange(parts):
         if ctx_count == 2:
             low = ctx_index == 0
             away = jnp.where(low, parts[1], parts[0])
             stay = jnp.where(low, parts[0], parts[1])
-            came = lax.ppermute(away, "ctx", [(0, 1), (1, 0)])
+            return stay, lax.ppermute(away, "ctx", [(0, 1), (1, 0)])
+        return (lax.all_to_all(jnp.stack(parts), "ctx", split_axis=0, concat_axis=0, tiled=True),)
+
+    def end_exchange(came):
+        if ctx_count == 2:
+            low = ctx_index == 0
+            stay, came = came
             return [jnp.where(low, stay, came), jnp.where(low, came, stay)]
-        came = lax.all_to_all(jnp.stack(parts), "ctx", split_axis=0, concat_axis=0, tiled=True)
-        return [came[c] for c in range(ctx_count)]
+        return [came[0][c] for c in range(ctx_count)]
 
     def swap_whole(array):
         swapped = lax.all_to_all(array, "ctx", split_axis=0, concat_axis=0, tiled=True)
         return swapped.reshape(-1, array.shape[-1])
 
+    qkv, hidden = tie(qkv, hidden)
     qkv_all = swap_whole(qkv)
     cut = lambda array, i: array[i * block : (i + 1) * block]
 
-    expand_lin, activated = row_call(
+    gelu_slope, activated = row_call(
         expand_kernel, "expand", 256, rows, (hidden, expand_weight, b_fc1.astype(F32)[None]),
         (
-            jax.ShapeDtypeStruct((rows, expand_weight.shape[1]), F32),
+            jax.ShapeDtypeStruct((rows, expand_weight.shape[1]), BF16),
             jax.ShapeDtypeStruct((rows, expand_weight.shape[1]), BF16),
         ),
         2 * rows * width * expand_weight.shape[1],
     )
-    mlp_out, grad_expand, expand_sum, cot_sum = row_call(
-        shrink_kernel, "shrink", 256, rows, (activated, cotangent, expand_lin, shrink_weight),
-        (
-            jax.ShapeDtypeStruct((rows, width), BF16),
-            jax.ShapeDtypeStruct(activated.shape, BF16),
-            jax.ShapeDtypeStruct((1, activated.shape[1]), F32),
-            jax.ShapeDtypeStruct((1, width), F32),
-        ),
-        4 * rows * width * expand_weight.shape[1],
+    activated, dense_shard = tie(activated, w_dense)
+    dense_weight = gather(dense_shard, axis=1)
+    (mlp_out,) = row_call(
+        shrink_kernel, "shrink", 256, rows, (activated, shrink_weight),
+        (jax.ShapeDtypeStruct((rows, width), BF16),),
+        2 * rows * width * expand_weight.shape[1],
     )
-    _, cot_late = tie(hidden, cotangent)
-    grad_att = jnp.stack(
-        [
-            dot_back(cot_late, dense_weight[c * share : (c + 1) * share]).astype(BF16)
-            for c in range(ctx_count)
-        ]
-    )
+    mlp_out, cot_late = tie(mlp_out, cotangent)
+    grad_att = grad_attended(cot_late, dense_weight, share)
+    qkv_all, mlp_out, grad_att = tie(qkv_all, mlp_out, grad_att)
     grad_all = swap_whole(grad_att)
-    qkv_all, mlp_out, grad_att = tie(qkv_all, mlp_out, grad_att)
-    turned_k, turned_v = turn_prompts(qkv_all, share)
+    turned_v = turn_prompts(qkv_all, share, 2)
 
     place = lax.axis_index("tp")
     flags = jnp.stack([((place == 0) | (place == 3)).astype(jnp.int32), place // 2])
@@ -889,11 +987,15 @@
 
     def forward(b):
         def run(qkv_in, turned_in):
-            return attend(qkv_in, turned_in, share, group, far, piece_items[b])
-
-        def keep(out):
-            o, env["turned", b], env["lse", b] = out
-            env["attended", b] = exchange([cut(o, c) for c in range(ctx_count)])
+            o, turned, lse = attend(qkv_in, turned_in, share, group, far, piece_items[b])
+            return start_exchange([cut(o, c) for c in range(ctx_count)]), turned, lse
+
+        def keep(out):
+            came, env["turned", b], env["lse", b] = out
+            env["attended", b] = end_exchange(came)
+            for c, part in enumerate(env["attended", b]):
+                before = env.get(("whole", c), jnp.zeros((rows, share), BF16))
+                env["whole", c] = lax.dynamic_update_slice(before, part, (b * block, 0))
 
         return run, (qkv_all, turned_v), keep
 
@@ -906,6 +1008,32 @@
             env["part", b] = out
 
         return run, (mlp_out, dense_weight, *env["attended", b]), keep
+
+    def slope():
+        def run(cot, gelu_slope, weight):
+            return row_call(
+                slope_kernel, "slope", 256, rows, (cot, gelu_slope, weight),
+                (
+                    jax.ShapeDtypeStruct(gelu_slope.shape, BF16),
+                    jax.ShapeDtypeStruct((1, gelu_slope.shape[1]), F32),
+                    jax.ShapeDtypeStruct((1, width), F32),
+                ),
+                2 * rows * width * gelu_slope.shape[1],
+            )
+
+        def keep(out):
+            env["grad_expand"], env["expand_sum"], env["cot_sum"] = out
+
+        return run, (cotangent, gelu_slope, shrink_weight), keep
+
+    def turn_keys():
+        def run(qkv_in):
+            return turn_prompts(qkv_in, share, 1)
+
+        def keep(out):
+            env["turned_k"] = out
+
+        return run, (qkv_all,), keep
 
     def backward(b):
         before = () if b == 0 else env["totals"]
@@ -920,7 +1048,8 @@
             env["dq", b], env["dk", b], env["dv", b] = out[:3]
             env["totals"] = out[3:]
 
-        return run, (qkv_all, turned_k, grad_all, env["turned", b], env["lse", b], *before), keep
+        ins = (qkv_all, env["turned_k"], grad_all, env["turned", b], env["lse", b], *before)
+        return run, ins, keep
 
     def finish():
         def run(dk, dv):
@@ -940,29 +1069,35 @@
                 key = prompts[0][c, near] if at < 0 else cut(dk, at)
                 value = prompts[1][c, near] if at < 0 else cut(dv, at)
                 parts.append(jnp.concatenate([cut(dq, c), key, value], axis=1))
-            return jnp.concatenate(exchange(parts), axis=1)
-
-        def keep(out):
-            env["grad_qkv", b] = out
+            return start_exchange(parts)
+
+        def keep(out):
+            env["sent_back", b] = out
 
         return run, (env["prompt_grads"], env["dq", b], env["dk", b], env["dv", b]), keep
 
     def grad_part(b):
-        def run(grad_exp, exp_weight, grad, weight):
+        def run(grad_exp, exp_weight, came, weight):
+            grad = jnp.concatenate(end_exchange(came), axis=1)
             pairs = [(grad_exp, b, exp_weight, None), (grad, 0, weight, None)]
-            return products(block, width, None, pairs, "grad_part")
-
-        def keep(out):
-            env["part", blocks + b] = out
-
-        return run, (grad_expand, expand_weight, env["grad_qkv", b], qkv_weight), keep
-
-    def weight_grad(name, left, right, axis):
+            part = products(block, width, None, pairs, "grad_part")
+            return part, grad, jnp.sum(grad.astype(F32), axis=0)
+
+        def keep(out):
+            env["part", blocks + b], grad, env["qkv_sum", b] = out
+            before = env.get("all_qkv", jnp.zeros((rows, 3 * local), BF16))
+            env["all_qkv"] = lax.dynamic_update_slice(before, grad, (b * block, 0))
+
+        return run, (env["grad_expand"], expand_weight, env["sent_back", b], qkv_weight), keep
+
+    def weight_grad(name, left, right, axis, part, parts):
         def run(left, right):
+            cut_out = lambda a: a[:, part * a.shape[1] // parts : (part + 1) * a.shape[1] // parts]
+            left, right = (cut_out(left), right) if axis else (left, cut_out(right))
             return transpose_dot(left, right).astype(BF16)
 
         def keep(out):
-            env[name] = lax.psum_scatter(
+            env[name, part] = lax.psum_scatter(
                 out, ("dp", "ctx"), scatter_dimension=axis, tiled=True
             ).astype(F32)
 
@@ -977,54 +1112,91 @@
 
         return run, (env["total", b], env.get("layer_out")), keep
 
-    def put_grad(b):
+    def put_grad(b, begin, count):
         def run(four, tokens_in, cot_in, before):
-            return norm_back(flags, four, b, tokens_in, cot_in, gain_row, before)
-
-        def keep(out):
-            env["grad_tokens"], env["gain", b], env["shift", b] = out
-
-        return run, (env["total", blocks + b], tokens, cotangent, env.get("grad_tokens")), keep
+            return norm_back(flags, four, b, tokens_in, cot_in, gain_row, before, begin, count)
+
+        def keep(out):
+            env["grad_tokens"] = out
+
+        total = env["total", blocks + b]
+        return run, (total, tokens, cotangent, env.get("grad_tokens")), keep
+
+    def sums(b):
+        def run(near, tokens_in):
+            return norm_sums(flags, near, b, tokens_in)
+
+        def keep(out):
+            env["gain", b], env["shift", b] = out
+
+        return run, (line.near, tokens), keep
+
+    def add_all(name, axes, pieces):
+        def run(arrays):
+            return lax.psum(jnp.concatenate(arrays), axes)
+
+        def keep(out):
+            env[name] = out
+
+        return run, (pieces(),), keep
+
+    def share_sums():
+        def run(parts):
+            own = jnp.concatenate([sum(part) for part in parts])
+            both = own + lax.ppermute(own, "tp", [(1, 2), (2, 1)])
+            return jnp.where(line.outer, lax.ppermute(both, "tp", [(1, 0), (2, 3)]), both)
+
+        def keep(out):
+            env["norm_sums"] = out
+
+        parts = [[env[name, b] for b in range(blocks)] for name in ("gain", "shift")]
+        return run, (parts,), keep
+
+    def all_pieces():
+        total = sum(env["qkv_sum", b] for b in range(blocks))
+        return [env["norm_sums"].reshape(-1), total, env["expand_sum"][0], env["cot_sum"][0]]
 
     def all_attended():
-        return jnp.concatenate(
-            [
-                jnp.concatenate([env["attended", b][c] for b in range(blocks)], axis=0)
-                for c in range(ctx_count)
-            ],
-            axis=1,
-        )
-
-    def all_grad_qkv():
-        return jnp.concatenate([env["grad_qkv", b] for b in range(blocks)], axis=0)
+        return jnp.concatenate([env["whole", c] for c in range(ctx_count)], axis=1)
 
     ticks = 4 * blocks + 2
     plan = [[] for _ in range(ticks + 8)]
-    spot = 2 * blocks - 2
+    after = [[] for _ in plan]
+    turn = 2 * blocks
+    last = blocks - 1
+    add = lambda slot, make, *args: plan[slot].append(functools.partial(make, *args))
     for b in range(blocks):
-        if b >= 2:
-            plan[b - 2].append(functools.partial(forward, b))
-        if b >= 1:
-            plan[b - 1].append(functools.partial(out_part, b))
-        plan[blocks - 2 + b].append(functools.partial(backward, b))
-        plan[2 * b + 4].append(functools.partial(put_out, b))
-        plan[spot + 1 + 2 * b].append(functools.partial(grad_part, b))
-        plan[2 * blocks + 2 * b + 4].append(functools.partial(put_grad, b))
-    after = [[] for _ in plan]
-    after[spot - 1].append(finish)
-    for b in range(blocks):
-        plan[spot + 2 * b].append(functools.partial(give_back, b))
-    plan[spot].append(lambda: weight_grad("dense", all_attended(), cotangent, 1))
-    plan[spot].append(lambda: weight_grad("fc2", activated, cotangent, 1))
-    plan[spot + 3].append(lambda: weight_grad("fc1", hidden, grad_expand, 0))
-    plan[spot + 2 * blocks].append(lambda: weight_grad("qkv", hidden, all_grad_qkv(), 0))
+        if b:
+            add(b - 1, forward, b)
+            add(b, out_part, b)
+            add(turn + 2 * (b - 1), give_back, b)
+        add(last + b, backward, b)
+        if b:
+            add(turn - 1 + 2 * b, grad_part, b)
+        add(turn + 1 + 2 * b, put_out, b)
+        add(turn + 2 * b + 2, sums, b)
+        if b < last:
+            add(turn + 2 * b + 4 + b % 2, put_grad, b, 0, 2)
+    add(0, turn_keys)
+    after[turn - 2].append(finish)
+    add(turn - 1, give_back, 0)
+    add(turn - 1, slope)
+    after[turn - 1].append(functools.partial(grad_part, 0))
+    add(turn, lambda: weight_grad("fc2", activated, cotangent, 1, 0, 1))
+    add(turn + 2, lambda: weight_grad("fc1", hidden, env["grad_expand"], 0, 0, 2))
+    add(turn + 4, lambda: weight_grad("fc1", hidden, env["grad_expand"], 0, 1, 2))
+    add(2 * turn - 2, lambda: weight_grad("qkv", hidden, env["all_qkv"], 0, 0, 1))
+    add(2 * turn - 1, lambda: weight_grad("dense", all_attended(), cotangent, 1, 0, 1))
+    add(ticks - 1, share_sums)
+    after[ticks - 1].append(functools.partial(add_all, "total", ("dp", "ctx"), all_pieces))
+    add(ticks - 1, put_grad, last, 0, 1)
+    add(ticks, put_grad, last, 1, 1)
 
     def perform(make):
         run, ins, keep = make()
         keep(run(*ins))
 
-    for b in range(min(2, blocks)):
-        perform(functools.partial(forward, b))
+    perform(functools.partial(forward, 0))
     perform(functools.partial(out_part, 0))
 
     line = Line(flags, tokens, (b_dense.astype(F32) + b_fc2.astype(F32))[None])
@@ -1039,6 +1211,8 @@
                 if total is not None:
                     env["total", b - 2] = total
             operands = line.begin(env.get(("part", b)), b < blocks)
+        if t == ticks - 1:
+            env["total", 2 * blocks - 1] = (line.first, line.near, line.first, line.near)
         stages = [s for s in (plan[t], after[t]) if s]
         sent = None
         for n, stage in enumerate(stages):
@@ -1059,18 +1233,9 @@
             perform(make)
 
     layer_out, grad_tokens = env["layer_out"], env["grad_tokens"]
-    small = (
-        sum(env["gain", b][0] for b in range(blocks)),
-        sum(env["shift", b][0] for b in range(blocks)),
-        jnp.sum(all_grad_qkv().astype(F32), axis=0),
-        expand_sum[0],
-        cot_sum[0],
-    )
-    sizes = [array.shape[0] for array in small]
-    packed = lax.psum(jnp.concatenate(small), ("dp", "ctx"))
-    ends = [sum(sizes[: i + 1]) for i in range(len(sizes))]
-    gain_sum, shift_sum, qkv_sum, expand_total, out_sum = (
-        packed[end - size : end] for end, size in zip(ends, sizes)
+    sizes = (width, width, 3 * local, w_fc1.shape[1])
+    gain_sum, shift_sum, qkv_sum, expand_total, out_sum = jnp.split(
+        env["total"], [sum(sizes[: i + 1]) for i in range(len(sizes))]
     )
 
     def unmixed(array):
@@ -1078,11 +1243,12 @@
         parts = array.reshape(*lead, ctx_count, 3, share)
         return tuple(parts[..., t, :].reshape(*lead, local) for t in range(3))
 
-    grad_query, grad_key, grad_value = unmixed(env["qkv"])
+    grad_query, grad_key, grad_value = unmixed(env["qkv", 0])
     sum_query, sum_key, sum_value = unmixed(qkv_sum)
     return (
         layer_out, grad_tokens, gain_sum, shift_sum, grad_query, sum_query, grad_key, sum_key,
-        grad_value, sum_value, env["dense"], out_sum, env["fc1"], expand_total, env["fc2"], out_sum,
+        grad_value, sum_value, env["dense", 0], out_sum,
+        jnp.concatenate([env["fc1", 0], env["fc1", 1]], axis=1), expand_total, env["fc2", 0], out_sum,
     )
 
 

time: 1640 us -> 1460 us (0.89)
  waiting for transfers between devices: 299 us -> 141 us
  other arithmetic: 84.6 us -> 61.6 us
    ppermute x18, waiting for transfers between devices: 146 us -> 32.3 us  [send(): lax.ppermute(swap, 'tp', outer)]
    all_to_all x2, waiting for transfers between devices: 0.01 us -> 23.2 us  [swap_whole(): lax.all_to_all(array, 'ctx', split_axis=0, concat_axis=0, tiled=True)]
    ppermute x8 -> x10, waiting for transfers between devices: 57.4 us -> 36 us  [the longest x8 18.3 us: start_exchange(): return (stay, lax.ppermute(away, 'ctx', [(0, 1), (1, 0)]))]
    pallas_call x2 -> x4, Pallas kernels: 150 us -> 170 us  [row_call(): pl.pallas_call(kernel, grid=(rows // count,), in_specs=[spec(a.shape) for...]
    dot_general x2 -> x0, matrix products: 19.8 us -> none  [dot_back(): return jnp.einsum('rb,ab->ra', left, right, preferred_element_type=F32)]
    all_gather x1, waiting for transfers between devices: 32.1 us -> 12.5 us  [body(): expand_weight = gather(w_fc1, axis=0)]
    pallas_call x6 -> x13, Pallas kernels: 80.4 us -> 99.1 us  [the longest x5 55.4 us: norm_back(): pl.pallas_call(functools.partial(norm_back_kernel, begin), grid_spec=pltp...]
    concatenate x5 -> x8, other arithmetic: 33.2 us -> 15.3 us  [the longest x4 7.61 us: run(): grad = jnp.concatenate(end_exchange(came), axis=1)]
  transfers between devices with their start and end apart: 52 -> 55, of which waited for: 16 -> 12; matrix products, arithmetic and copies ran while one was open for 16% -> 16% of each run, Pallas kernels for 51% -> 57%
where the time goes in v3:
time: 1460 us; the launch traced here: 1450 us
  Pallas kernels  898 us (62%)
  waiting for transfers between devices  141 us (10%)
  matrix products  138 us (9%)
  starting transfers between devices  101 us (7%)
  local copies, waits for them, and re-layouts  69.6 us (5%)
  other arithmetic  61.6 us (4%)
  blocking collectives  25.3 us (2%)
  between operations  15.4 us (1%)
    pallas_call x4, Pallas kernels, attend_back(): pl.pallas_call(functools.partial(attend_back_kernel, 1024, first, GPR * P...  230 us
    pallas_call x4, Pallas kernels, row_call(): pl.pallas_call(kernel, grid=(rows // count,), in_specs=[spec(a.shape) for...  170 us
    dot_general x5, matrix products, transpose_dot(): return jnp.einsum('ra,rb->ab', left, right, preferred_element_type=F32)  138 us
    pallas_call x8, Pallas kernels, products(): pl.pallas_call(functools.partial(products_kernel, kinds, base is not None...  129 us
    pallas_call x4, Pallas kernels, attend(): pl.pallas_call(functools.partial(attend_kernel, 1024), grid_spec=pltpu.Pr...  126 us
    pallas_call x17, Pallas kernels, line_call(): pl.pallas_call(functools.partial(kernel, [i[0] for i in ins] + outs), gri...  80.5 us
    pallas_call x5, Pallas kernels, norm_back(): pl.pallas_call(functools.partial(norm_back_kernel, begin), grid_spec=pltp...  55.4 us
    ppermute x18, starting transfers between devices, send(): lax.ppermute(swap, 'tp', outer)  49.3 us
  transfers between devices with their start and end apart: 55, of which 12 were waited for; matrix products, arithmetic and copies ran while one was open for 16% of the time, Pallas kernels for 57%

profile of v3, /device:TPU:0, one launch (start us, length us, event | category | flops | bytes accessed | tf_op | source)
XLA Modules:
  0.0 1449.9 jit_solution(16203907368390070969)
XLA Ops:
  62.1 36.8 %qkv_project.1 = bf16[2,4096,768]{2,1,0:T(8,128)(2,1)} custom-call(s32[16]{0:T(128)} %dynamic_slice.3.where_ref, bf16[4096,2048]{1,0:T(8,128)(2,1)} %norm.1.hidden_ref, bf16[2048,1536]{1,0:T(8,128)(2,1)} %all-gather.5.cloned.1.call-done.weight_ref.refs_3_, f32[1,1536]{1,0:T(1,128)} %reshape.163.bias_ref, f32[2304,128]{1,0:T(8,128)} %concatenate.69.cos_ref.refs_12_, ...), custom_call_target="tpu_custom_call" | custom-call | flops 25769803776 | bytes 46137344 | tf_op jit(solution)/shard_map/qkv_project/pallas_call | solution.py:132
  120.4 60.7 %expand.1 = (bf16[4096,2048]{1,0:T(8,128)(2,1)}, bf16[4096,2048]{1,0:T(8,128)(2,1)}) custom-call(bf16[4096,2048]{1,0:T(8,128)(2,1)} %norm.1.hidden_ref, bf16[2048,2048]{1,0:T(8,128)(2,1)} %all-gather.7.cloned.1.call-done.weight_ref.refs_1_, f32[1,2048]{1,0:T(1,128)} %bitcast.89), custom_call_target="tpu_custom_call" | custom-call | flops 34359738368 | bytes 58728448 | tf_op jit(solution)/shard_map/expand/pallas_call | solution.py:236
  182.3 28.7 %all-gather.9.cloned.1.call-done.weight_ref = bf16[2048,2048]{1,0:T(8,128)(2,1)} async-done(((bf16[2048,256]{1,0:T(8,128)(2,1)}), bf16[2048,2048]{1,0:T(8,128)(2,1)}) %all-gather.9.cloned.1.call-update) | async-done | bytes 8388624 | tf_op jit(solution)/shard_map/all_gather | solution.py:935
  211.0 42.2 %shrink.1.refs_0_ = bf16[4096,2048]{1,0:T(8,128)(2,1)} custom-call(bf16[4096,2048]{1,0:T(8,128)(2,1)} %get-tuple-element.585.act_ref, bf16[2048,2048]{1,0:T(8,128)(2,1)} %all-gather.9.cloned.1.call-done.weight_ref), custom_call_target="tpu_custom_call" | custom-call | flops 34359738368 | bytes 41943040 | tf_op jit(solution)/shard_map/shrink/pallas_call | solution.py:236
  268.4 23.2 %all-to-all-done = bf16[2,4096,768]{2,1,0:T(8,128)(2,1)} async-done(((bf16[2,4096,768]{2,1,0:T(8,128)(2,1)}), bf16[2,4096,768]{2,1,0:T(8,128)(2,1)}, u32[]{:S(2)}, u32[]{:S(2)}) %all-to-all-start) | async-done | bytes 12582944 | tf_op jit(solution)/shard_map/all_to_all | solution.py:954
  295.7 27.9 %attend.4 = (bf16[2048,256]{1,0:T(8,128)(2,1)}, f32[256,2048]{1,0:T(8,128)}, f32[1,4,2048]{2,1,0:T(4,128)}) custom-call(s32[32]{0:T(128)} %pad_add_fusion.1.group_ref.refs_0_, s32[32]{0:T(128)} %copy-done.70, s32[8]{0:T(128)} %reshape_squeeze.38.item_ref.refs_2_, ...), custom_call_target="tpu_custom_call" | custom-call | flops 19327352832 | bytes 6291456 | tf_op jit(solution)/shard_map/attend/pallas_call | solution.py:531
  352.8 34.9 %attend.5 = (bf16[2048,256]{1,0:T(8,128)(2,1)}, f32[256,2048]{1,0:T(8,128)}, f32[1,4,2048]{2,1,0:T(4,128)}) custom-call(s32[32]{0:T(128)} %pad_add_fusion.1.group_ref.refs_0_, s32[32]{0:T(128)} %copy-done.70, s32[8]{0:T(128)} %reshape_squeeze.39.item_ref.refs_2_, ...), custom_call_target="tpu_custom_call" | custom-call | flops 19327352832 | bytes 6291456 | tf_op jit(solution)/shard_map/attend/pallas_call | solution.py:531
  413.0 28.0 %attend.6 = (bf16[2048,256]{1,0:T(8,128)(2,1)}, f32[256,2048]{1,0:T(8,128)}, f32[1,4,2048]{2,1,0:T(4,128)}) custom-call(s32[32]{0:T(128)} %pad_add_fusion.1.group_ref.refs_0_, s32[32]{0:T(128)} %copy-done.70, s32[8]{0:T(128)} %reshape_squeeze.40.item_ref.refs_2_, ...), custom_call_target="tpu_custom_call" | custom-call | flops 19327352832 | bytes 6291456 | tf_op jit(solution)/shard_map/attend/pallas_call | solution.py:531
  471.8 34.9 %attend.7 = (bf16[2048,256]{1,0:T(8,128)(2,1)}, f32[256,2048]{1,0:T(8,128)}, f32[1,4,2048]{2,1,0:T(4,128)}) custom-call(s32[32]{0:T(128)} %pad_add_fusion.1.group_ref.refs_0_, s32[32]{0:T(128)} %copy-done.70, s32[8]{0:T(128)} %reshape_squeeze.41.item_ref.refs_2_, ...), custom_call_target="tpu_custom_call" | custom-call | flops 19327352832 | bytes 6291456 | tf_op jit(solution)/shard_map/attend/pallas_call | solution.py:531
  536.7 49.9 %attend_back.4 = (bf16[2048,256]{1,0:T(8,128)(2,1)}, bf16[1024,256]{1,0:T(8,128)(2,1)}, bf16[1024,256]{1,0:T(8,128)(2,1)}, f32[4096,256]{1,0:T(8,128)}, f32[4096,256]{1,0:T(8,128)}) custom-call(s32[32]{0:T(128)} %pad_add_fusion.1.group_ref.refs_0_, s32[32]{0:T(128)} %copy-done.70, s32[8]{0:T(128)} %reshape_squeeze.38.item_ref.refs_2_, ...), custom_call_target="tpu_custom_call" | custom-call | flops 38654705664 | bytes 12582912 | tf_op jit(solution)/shard_map/attend_back/pallas_call | solution.py:572
  598.3 64.0 %attend_back.5 = (bf16[2048,256]{1,0:T(8,128)(2,1)}, bf16[1024,256]{1,0:T(8,128)(2,1)}, bf16[1024,256]{1,0:T(8,128)(2,1)}, f32[4096,256]{1,0:T(8,128)}, f32[4096,256]{1,0:T(8,128)}) custom-call(s32[32]{0:T(128)} %pad_add_fusion.1.group_ref.refs_0_, s32[32]{0:T(128)} %copy-done.70, ...), custom_call_target="tpu_custom_call", output_to_operand_aliasing={{3}: (15, {}), {4}: (16, {})} | custom-call | flops 38654705664 | bytes 12582912 | tf_op jit(solution)/shard_map/attend_back/pallas_call | solution.py:572
  673.3 52.2 %attend_back.6 = (bf16[2048,256]{1,0:T(8,128)(2,1)}, bf16[1024,256]{1,0:T(8,128)(2,1)}, bf16[1024,256]{1,0:T(8,128)(2,1)}, f32[4096,256]{1,0:T(8,128)}, f32[4096,256]{1,0:T(8,128)}) custom-call(s32[32]{0:T(128)} %pad_add_fusion.1.group_ref.refs_0_, s32[32]{0:T(128)} %copy-done.70, ...), custom_call_target="tpu_custom_call", output_to_operand_aliasing={{3}: (15, {}), {4}: (16, {})} | custom-call | flops 38654705664 | bytes 12582912 | tf_op jit(solution)/shard_map/attend_back/pallas_call | solution.py:572
  736.6 63.9 %attend_back.7 = (bf16[2048,256]{1,0:T(8,128)(2,1)}, bf16[1024,256]{1,0:T(8,128)(2,1)}, bf16[1024,256]{1,0:T(8,128)(2,1)}, f32[4096,256]{1,0:T(8,128)}, f32[4096,256]{1,0:T(8,128)}) custom-call(s32[32]{0:T(128)} %pad_add_fusion.1.group_ref.refs_0_, s32[32]{0:T(128)} %copy-done.70, ...), custom_call_target="tpu_custom_call", output_to_operand_aliasing={{3}: (15, {}), {4}: (16, {})} | custom-call | flops 38654705664 | bytes 12582912 | tf_op jit(solution)/shard_map/attend_back/pallas_call | solution.py:572
  826.1 46.1 %slope.1 = (bf16[4096,2048]{1,0:T(8,128)(2,1)}, f32[1,2048]{1,0:T(1,128)}, f32[1,2048]{1,0:T(1,128)}) custom-call(bf16[4096,2048]{1,0:T(8,128)(2,1)} %cot_ref.7, bf16[4096,2048]{1,0:T(8,128)(2,1)} %get-tuple-element.559.slope_ref, bf16[2048,2048]{1,0:T(8,128)(2,1)} %all-gather.9.cloned.1.call-done.weight_ref), custom_call_target="tpu_custom_call" | custom-call | flops 34359738368 | bytes 58736640 | tf_op jit(solution)/shard_map/slope/pallas_call | solution.py:236
  876.8 23.6 %grad_part.4.refs_5_.refs_0_.refs_1_ = bf16[1024,2048]{1,0:T(8,128)(2,1)} custom-call(bf16[4096,2048]{1,0:T(8,128)(2,1)} %get-tuple-element.681.refs_0_, bf16[2048,2048]{1,0:T(8,128)(2,1)} %all-gather.7.cloned.1.call-done.weight_ref.refs_1_, bf16[1024,1536]{1,0:T(8,128)(2,1)} %pad_maximum_fusion.1.refs_2_, ...), custom_call_target="tpu_custom_call" | custom-call | flops 15032385536 | bytes 29360128 | tf_op jit(solution)/shard_map/grad_part/pallas_call | solution.py:286
  917.1 43.3 %convolution_convert_fusion.1 = bf16[2048,2048]{1,0:T(8,128)(2,1)} fusion(bf16[4096,2048]{1,0:T(8,128)(2,1)} %get-tuple-element.585.act_ref, bf16[4096,2048]{1,0:T(8,128)(2,1)} %cot_ref.7), kind=kOutput, calls=%fused_computation.5 | convolution fusion | flops 34363932672 | bytes 41943040 | tf_op jit(solution)/shard_map/ra,rb->ab/dot_general | solution.py:32
  992.9 23.8 %grad_part.5.refs_3_.refs_0_.refs_1_ = bf16[1024,2048]{1,0:T(8,128)(2,1)} custom-call(bf16[4096,2048]{1,0:T(8,128)(2,1)} %get-tuple-element.681.refs_0_, bf16[2048,2048]{1,0:T(8,128)(2,1)} %all-gather.7.cloned.1.call-done.weight_ref.refs_1_, bf16[1024,1536]{1,0:T(8,128)(2,1)} %pad_maximum_fusion.2.refs_2_, ...), custom_call_target="tpu_custom_call" | custom-call | flops 15032385536 | bytes 29360128 | tf_op jit(solution)/shard_map/grad_part/pallas_call | solution.py:286
  1035.9 23.7 %fusion.4 = bf16[2048,1024]{1,0:T(8,128)(2,1)} fusion(bf16[4096,2048]{1,0:T(8,128)(2,1)} %norm.1.hidden_ref, bf16[4096,2048]{1,0:T(8,128)(2,1)} %get-tuple-element.681.refs_0_), kind=kOutput, calls=%fused_computation.11 | convolution fusion | flops 17181966336 | bytes 29360128 | tf_op jit(solution)/shard_map/ra,rb->ab/dot_general | solution.py:32
  1092.6 24.0 %grad_part.6.refs_3_.refs_0_.refs_1_ = bf16[1024,2048]{1,0:T(8,128)(2,1)} custom-call(bf16[4096,2048]{1,0:T(8,128)(2,1)} %get-tuple-element.681.refs_0_, bf16[2048,2048]{1,0:T(8,128)(2,1)} %all-gather.7.cloned.1.call-done.weight_ref.refs_1_, bf16[1024,1536]{1,0:T(8,128)(2,1)} %pad_maximum_fusion.3.refs_2_, ...), custom_call_target="tpu_custom_call" | custom-call | flops 15032385536 | bytes 29360128 | tf_op jit(solution)/shard_map/grad_part/pallas_call | solution.py:286
  1132.0 23.8 %fusion.7 = bf16[2048,1024]{1,0:T(8,128)(2,1)} fusion(bf16[4096,2048]{1,0:T(8,128)(2,1)} %norm.1.hidden_ref, bf16[4096,2048]{1,0:T(8,128)(2,1)} %get-tuple-element.681.refs_0_), kind=kOutput, calls=%fused_computation.12 | convolution fusion | flops 17181966336 | bytes 29360128 | tf_op jit(solution)/shard_map/ra,rb->ab/dot_general | solution.py:32
  1187.8 24.4 %grad_part.7.refs_3_.refs_0_.refs_1_ = bf16[1024,2048]{1,0:T(8,128)(2,1)} custom-call(bf16[4096,2048]{1,0:T(8,128)(2,1)} %get-tuple-element.681.refs_0_, bf16[2048,2048]{1,0:T(8,128)(2,1)} %all-gather.7.cloned.1.call-done.weight_ref.refs_1_, bf16[1024,1536]{1,0:T(8,128)(2,1)} %pad_maximum_fusion.4.refs_2_, ...), custom_call_target="tpu_custom_call" | custom-call | flops 15032385536 | bytes 29360128 | tf_op jit(solution)/shard_map/grad_part/pallas_call | solution.py:286
  1234.4 34.0 %convolution_convert_fusion = bf16[2048,1536]{1,0:T(8,128)(2,1)} fusion(bf16[4096,2048]{1,0:T(8,128)(2,1)} %norm.1.hidden_ref, bf16[4096,1536]{1,0:T(8,128)(2,1)} %constant_dynamic-update-slice_fusion.6), kind=kOutput, calls=%fused_computation.4 | convolution fusion | flops 25772949504 | bytes 35651584 | tf_op jit(solution)/shard_map/ra,rb->ab/dot_general | solution.py:32
  1340.7 24.1 %collective-permute-done.39.a.c = bf16[512,2048]{1,0:T(8,128)(2,1)S(1)} collective-permute-done((bf16[512,2048]{1,0:T(8,128)(2,1)}, bf16[512,2048]{1,0:T(8,128)(2,1)S(1)}, u32[]{:S(2)}, u32[]{:S(2)}) %collective-permute-start.39) | collective-permute-done | bytes 2097184 | tf_op jit(solution)/shard_map/ppermute | solution.py:885
  1401.4 25.3 %psum.7 = f32[9728]{0:T(1024)S(1)} all-reduce(f32[9728]{0:T(1024)S(1)} %pad_maximum_fusion.14), channel_id=1, replica_groups=mesh['dp'=4,'ctx'=2,'tp'=4] {'dp','ctx'}, use_global_device_ids=true, to_apply=%region_4.5 | all-reduce | flops 9728 | bytes 77824 | tf_op jit(solution)/shard_map/psum | solution.py:1136
  (396 shorter events, 571.1 us)
Async XLA Ops:
  7.2 53.0 %all-gather.5.cloned.1.call-start = ((), (), s32[]{:S(2)}) async-start(), calls=%async_computation.7 | async-start | bytes 7077888 | tf_op jit(solution)/shard_map/all_gather | solution.py:911
  11.8 108.6 %all-gather.7.cloned.1.call-start = ((), (), s32[]{:S(2)}) async-start(), calls=%async_computation.8 | async-start | bytes 9437184 | tf_op jit(solution)/shard_map/all_gather | solution.py:912
  12.5 198.4 %all-gather.9.cloned.1.call-start = ((), (), s32[]{:S(2)}) async-start(), calls=%async_computation.9 | async-start | bytes 9437184 | tf_op jit(solution)/shard_map/all_gather | solution.py:935
  98.9 192.7 %all-to-all-start = ((bf16[2,4096,768]{2,1,0:T(8,128)(2,1)}), bf16[2,4096,768]{2,1,0:T(8,128)(2,1)}, u32[]{:S(2)}, u32[]{:S(2)}) async-start(bf16[2,4096,768]{2,1,0:T(8,128)(2,1)} %qkv_project.1), calls=%async_computation | async-start | bytes 25165824 | tf_op jit(solution)/shard_map/all_to_all | solution.py:954
  107.3 146.0 %all-gather.11.cloned.1.call-start = ((), (), s32[]{:S(2)}) async-start(), calls=%async_computation.10 | async-start | bytes 2359296 | tf_op jit(solution)/shard_map/all_gather | solution.py:970
  351.4 51.6 %collective-permute-start.1 = (bf16[512,2048]{1,0:T(8,128)(2,1)}, bf16[512,2048]{1,0:T(8,128)(2,1)}, u32[]{:S(2)}, u32[]{:S(2)}) collective-permute-start(bf16[512,2048]{1,0:T(8,128)(2,1)} %line_begin.9), channel_id=1, source_target_pairs={{0,1},{3,2},{1,0},{2,3},{4,5},{7,6},{5,4},{6,7},{8,9},{11,10},{9,8... | collective-permute-start | bytes 6291464 | tf_op jit(solution)/shard_map/ppermute | solution.py:885
  444.1 82.4 %all-to-all-start.1 = ((bf16[2,4096,256]{2,1,0:T(8,128)(2,1)}), bf16[2,4096,256]{2,1,0:T(8,128)(2,1)}, u32[]{:S(2)}, u32[]{:S(2)}) async-start(bf16[2,4096,256]{2,1,0:T(8,128)(2,1)} %grad_attended.1), calls=%async_computation.1 | async-start | bytes 8388608 | tf_op jit(solution)/shard_map/all_to_all | solution.py:954
  449.8 917.6 %reduce-scatter.14.cloned.1.call-start = ((), (), s32[]{:S(2)}) async-start(), calls=%async_computation.15 | async-start | bytes 9437184 | tf_op jit(solution)/shard_map/reduce_scatter | solution.py:1100
  465.4 53.3 %collective-permute-start.6 = (bf16[512,2048]{1,0:T(8,128)(2,1)S(1)}, bf16[512,2048]{1,0:T(8,128)(2,1)S(1)}, u32[]{:S(2)}, u32[]{:S(2)}) collective-permute-start(bf16[512,2048]{1,0:T(8,128)(2,1)S(1)} %copy-done.20), channel_id=1, source_target_pairs={{0,1},{3,2},{1,0},{2,3},{4,5},{7,6},{5,4},{6,7},{8,9},{11,10},{9,8... | collective-permute-start | bytes 6291464 | tf_op jit(solution)/shard_map/ppermute | solution.py:885
  526.5 60.0 %collective-permute-start.9 = (bf16[512,2048]{1,0:T(8,128)(2,1)}, bf16[512,2048]{1,0:T(8,128)(2,1)S(1)}, u32[]{:S(2)}, u32[]{:S(2)}) collective-permute-start(bf16[512,2048]{1,0:T(8,128)(2,1)} %get-tuple-element.465), channel_id=1, source_target_pairs={{0,1},{3,2},{1,0},{2,3},{4,5},{7,6},{5,4},{6,7},{8,9},{11,10},{9,8... | collective-permute-start | bytes 6291464 | tf_op jit(solution)/shard_map/ppermute | solution.py:885
  527.3 59.2 %collective-permute-start.10 = (bf16[512,2048]{1,0:T(8,128)(2,1)}, bf16[512,2048]{1,0:T(8,128)(2,1)S(1)}, u32[]{:S(2)}, u32[]{:S(2)}) collective-permute-start(bf16[512,2048]{1,0:T(8,128)(2,1)} %get-tuple-element.466), channel_id=1, source_target_pairs={{1,2},{2,1},{5,6},{6,5},{9,10},{10,9},{13,14},{14,13},{17,18},{18,... | collective-permute-start | bytes 6291464 | tf_op jit(solution)/shard_map/ppermute | solution.py:886
  593.2 69.1 %collective-permute-start.11 = (bf16[512,2048]{1,0:T(8,128)(2,1)}, bf16[512,2048]{1,0:T(8,128)(2,1)S(1)}, u32[]{:S(2)}, u32[]{:S(2)}) collective-permute-start(bf16[512,2048]{1,0:T(8,128)(2,1)} %line_begin.11.b), channel_id=1, source_target_pairs={{0,1},{3,2},{1,0},{2,3},{4,5},{7,6},{5,4},{6,7},{8,9},{11,10},{9,8... | collective-permute-start | bytes 6291464 | tf_op jit(solution)/shard_map/ppermute | solution.py:885
  597.5 64.8 %collective-permute-start.12 = (bf16[512,2048]{1,0:T(8,128)(2,1)}, bf16[512,2048]{1,0:T(8,128)(2,1)S(1)}, u32[]{:S(2)}, u32[]{:S(2)}) collective-permute-start(bf16[512,2048]{1,0:T(8,128)(2,1)} %line_begin.11.b), channel_id=1, source_target_pairs={{1,2},{2,1},{5,6},{6,5},{9,10},{10,9},{13,14},{14,13},{17,18},{18,... | collective-permute-start | bytes 6291464 | tf_op jit(solution)/shard_map/ppermute | solution.py:886
  669.4 56.1 %collective-permute-start.13 = (bf16[512,2048]{1,0:T(8,128)(2,1)}, bf16[512,2048]{1,0:T(8,128)(2,1)S(1)}, u32[]{:S(2)}, u32[]{:S(2)}) collective-permute-start(bf16[512,2048]{1,0:T(8,128)(2,1)} %get-tuple-element.511), channel_id=1, source_target_pairs={{0,1},{3,2},{1,0},{2,3},{4,5},{7,6},{5,4},{6,7},{8,9},{11,10},{9,8... | collective-permute-start | bytes 6291464 | tf_op jit(solution)/shard_map/ppermute | solution.py:885
  672.3 53.3 %collective-permute-start.14 = (bf16[512,2048]{1,0:T(8,128)(2,1)}, bf16[512,2048]{1,0:T(8,128)(2,1)S(1)}, u32[]{:S(2)}, u32[]{:S(2)}) collective-permute-start(bf16[512,2048]{1,0:T(8,128)(2,1)} %get-tuple-element.512), channel_id=1, source_target_pairs={{1,2},{2,1},{5,6},{6,5},{9,10},{10,9},{13,14},{14,13},{17,18},{18,... | collective-permute-start | bytes 6291464 | tf_op jit(solution)/shard_map/ppermute | solution.py:886
  732.2 76.9 %collective-permute-start.15 = (bf16[512,2048]{1,0:T(8,128)(2,1)}, bf16[512,2048]{1,0:T(8,128)(2,1)S(1)}, u32[]{:S(2)}, u32[]{:S(2)}) collective-permute-start(bf16[512,2048]{1,0:T(8,128)(2,1)} %line_begin.12.b), channel_id=1, source_target_pairs={{0,1},{3,2},{1,0},{2,3},{4,5},{7,6},{5,4},{6,7},{8,9},{11,10},{9,8... | collective-permute-start | bytes 6291464 | tf_op jit(solution)/shard_map/ppermute | solution.py:885
  735.3 73.8 %collective-permute-start.16 = (bf16[512,2048]{1,0:T(8,128)(2,1)}, bf16[512,2048]{1,0:T(8,128)(2,1)S(1)}, u32[]{:S(2)}, u32[]{:S(2)}) collective-permute-start(bf16[512,2048]{1,0:T(8,128)(2,1)} %line_begin.12.b), channel_id=1, source_target_pairs={{1,2},{2,1},{5,6},{6,5},{9,10},{10,9},{13,14},{14,13},{17,18},{18,... | collective-permute-start | bytes 6291464 | tf_op jit(solution)/shard_map/ppermute | solution.py:886
  822.3 78.1 %collective-permute-start.17 = (bf16[512,2048]{1,0:T(8,128)(2,1)}, bf16[512,2048]{1,0:T(8,128)(2,1)S(1)}, u32[]{:S(2)}, u32[]{:S(2)}) collective-permute-start(bf16[512,2048]{1,0:T(8,128)(2,1)} %get-tuple-element.556), channel_id=1, source_target_pairs={{0,1},{3,2},{1,0},{2,3},{4,5},{7,6},{5,4},{6,7},{8,9},{11,10},{9,8... | collective-permute-start | bytes 6291464 | tf_op jit(solution)/shard_map/ppermute | solution.py:885
  825.1 75.3 %collective-permute-start.18 = (bf16[512,2048]{1,0:T(8,128)(2,1)}, bf16[512,2048]{1,0:T(8,128)(2,1)S(1)}, u32[]{:S(2)}, u32[]{:S(2)}) collective-permute-start(bf16[512,2048]{1,0:T(8,128)(2,1)} %get-tuple-element.557), channel_id=1, source_target_pairs={{1,2},{2,1},{5,6},{6,5},{9,10},{10,9},{13,14},{14,13},{17,18},{18,... | collective-permute-start | bytes 6291464 | tf_op jit(solution)/shard_map/ppermute | solution.py:886
  960.4 411.5 %reduce-scatter.10.cloned.1.call-start = ((), (), s32[]{:S(2)}) async-start(), calls=%async_computation.13 | async-start | bytes 4718592 | tf_op jit(solution)/shard_map/reduce_scatter | solution.py:1100
  1081.0 291.0 %reduce-scatter.12.cloned.1.call-start = ((), (), s32[]{:S(2)}) async-start(), calls=%async_computation.14 | async-start | bytes 4718592 | tf_op jit(solution)/shard_map/reduce_scatter | solution.py:1100
  1183.8 242.9 %reduce-scatter.8.cloned.1.call-start = ((), (), s32[]{:S(2)}) async-start(), calls=%async_computation.12 | async-start | bytes 2359296 | tf_op jit(solution)/shard_map/reduce_scatter | solution.py:1100
  1313.4 124.3 %reduce-scatter.6.cloned.1.call-start = ((), (), s32[]{:S(2)}) async-start(), calls=%async_computation.11 | async-start | bytes 7077888 | tf_op jit(solution)/shard_map/reduce_scatter | solution.py:1100
  1364.8 63.7 %collective-permute-start.41 = (bf16[512,2048]{1,0:T(8,128)(2,1)}, bf16[512,2048]{1,0:T(8,128)(2,1)}, u32[]{:S(2)}, u32[]{:S(2)}) collective-permute-start(bf16[512,2048]{1,0:T(8,128)(2,1)} %collective-permute-done.40.d), channel_id=1, source_target_pairs={{0,1},{3,2},{1,0},{2,3},{4,5},{7,6},{5,4},{6,7},{8,9},{11,10},{9,8... | collective-permute-start | bytes 6291464 | tf_op jit(solution)/shard_map/ppermute | solution.py:885
  (102 other events, 2040.7 us)
Sparse Core Ops, SparseCore 0:
  11.9 48.2 all-gather.4
  62.1 58.2 all-gather.6
  122.3 88.6 all-gather.8
  212.7 36.2 all-gather.10
  960.5 75.3 reduce-scatter.13
  1081.1 54.7 reduce-scatter.9
  1183.9 50.4 reduce-scatter.11
  1313.5 43.1 reduce-scatter.7
  1360.1 62.8 reduce-scatter.5

commit v4 on v3

--- a/solution.py
+++ b/solution.py
@@ -736,8 +736,8 @@
     )(flags, *four, *(() if before is None else (before,)))
 
 
-def normed_rows(x_ref):
-    x = x_ref[...].astype(F32)
+def normed_rows(tokens):
+    x = tokens.astype(F32)
     center = x - jnp.mean(x, axis=-1, keepdims=True)
     inverse = lax.rsqrt(jnp.mean(center * center, axis=-1, keepdims=True) + 1e-05)
     return center * inverse, inverse
@@ -747,11 +747,11 @@
     out_ref, held = rest[-2:]
 
     def keep(value):
-        held[...] = value.astype(F32) * gain_ref[...]
+        held[...] = value
 
     total_of(flag_ref, (a, b, c, d), keep, begin)
-    normed, inverse = normed_rows(x_ref)
-    scaled = held[...]
+    normed, inverse = normed_rows(x_ref[...])
+    scaled = held[...].astype(F32) * gain_ref[...]
     grad = scaled - jnp.mean(scaled, axis=-1, keepdims=True)
     grad = inverse * (grad - normed * jnp.mean(scaled * normed, axis=-1, keepdims=True))
     out_ref[...] = cot_ref[...].astype(F32) + grad
@@ -770,7 +770,7 @@
             + [whole, whole, row]
             + [pl.BlockSpec(memory_space=pl.ANY)] * (before is not None),
             out_specs=whole,
-            scratch_shapes=[pltpu.VMEM((COUNT, width), F32)],
+            scratch_shapes=[pltpu.VMEM((COUNT, width), BF16)],
         ),
         out_shape=jax.ShapeDtypeStruct(tokens.shape, F32),
         input_output_aliases={} if before is None else {8: 0},
@@ -789,7 +789,7 @@
     @pl.when(flag_ref[0] == 0)
     def _():
         total = total_ref[...].astype(F32)
-        gain_sum[...] += jnp.sum(total * normed_rows(x_ref)[0], axis=0, keepdims=True)
+        gain_sum[...] += jnp.sum(total * normed_rows(x_ref[...])[0], axis=0, keepdims=True)
         shift_sum[...] += jnp.sum(total, axis=0, keepdims=True)
 
 
@@ -1175,7 +1175,7 @@
             add(turn - 1 + 2 * b, grad_part, b)
         add(turn + 1 + 2 * b, put_out, b)
         add(turn + 2 * b + 2, sums, b)
-        if b < last:
+        if b < last - 1:
             add(turn + 2 * b + 4 + b % 2, put_grad, b, 0, 2)
     add(0, turn_keys)
     after[turn - 2].append(finish)
@@ -1187,8 +1187,9 @@
     add(turn + 4, lambda: weight_grad("fc1", hidden, env["grad_expand"], 0, 1, 2))
     add(2 * turn - 2, lambda: weight_grad("qkv", hidden, env["all_qkv"], 0, 0, 1))
     add(2 * turn - 1, lambda: weight_grad("dense", all_attended(), cotangent, 1, 0, 1))
-    add(ticks - 1, share_sums)
-    after[ticks - 1].append(functools.partial(add_all, "total", ("dp", "ctx"), all_pieces))
+    after[ticks - 2].append(share_sums)
+    after[ticks - 2].append(functools.partial(put_grad, last - 1, 0, 2))
+    add(ticks - 1, add_all, "total", ("dp", "ctx"), all_pieces)
     add(ticks - 1, put_grad, last, 0, 1)
     add(ticks, put_grad, last, 1, 1)
 

time: 1460 us -> 1450 us (level)
  waiting for transfers between devices: 141 us -> 120 us
    ppermute x18, waiting for transfers between devices: 32.3 us -> 8.52 us  [send(): lax.ppermute(swap, 'tp', outer)]
  transfers between devices with their start and end apart: 55 -> 55, of which waited for: 12 -> 11; matrix products, arithmetic and copies ran while one was open for 16% -> 16% of each run, Pallas kernels for 57% -> 57%
where the time goes in v4:
time: 1450 us; the launch traced here: 1440 us
  Pallas kernels  897 us (62%)
  matrix products  138 us (10%)
  waiting for transfers between devices  120 us (8%)
  starting transfers between devices  110 us (8%)
  local copies, waits for them, and re-layouts  69.4 us (5%)
  other arithmetic  62.7 us (4%)
  blocking collectives  26.5 us (2%)
  between operations  15.3 us (1%)
    pallas_call x4, Pallas kernels, attend_back(): pl.pallas_call(functools.partial(attend_back_kernel, 1024, first, GPR * P...  230 us
    pallas_call x4, Pallas kernels, row_call(): pl.pallas_call(kernel, grid=(rows // count,), in_specs=[spec(a.shape) for...  170 us
    dot_general x5, matrix products, transpose_dot(): return jnp.einsum('ra,rb->ab', left, right, preferred_element_type=F32)  138 us
    pallas_call x8, Pallas kernels, products(): pl.pallas_call(functools.partial(products_kernel, kinds, base is not None...  129 us
    pallas_call x4, Pallas kernels, attend(): pl.pallas_call(functools.partial(attend_kernel, 1024), grid_spec=pltpu.Pr...  126 us
    pallas_call x17, Pallas kernels, line_call(): pl.pallas_call(functools.partial(kernel, [i[0] for i in ins] + outs), gri...  80.7 us
    ppermute x18, starting transfers between devices, send(): lax.ppermute(swap, 'tp', outer)  58.9 us
    pallas_call x5, Pallas kernels, norm_back(): pl.pallas_call(functools.partial(norm_back_kernel, begin), grid_spec=pltp...  55.2 us
  transfers between devices with their start and end apart: 55, of which 11 were waited for; matrix products, arithmetic and copies ran while one was open for 16% of the time, Pallas kernels for 57%

profile of v4, /device:TPU:0, one launch (start us, length us, event | category | flops | bytes accessed | tf_op | source)
XLA Modules:
  0.0 1438.8 jit_solution(14719327178395468175)
XLA Ops:
  32.3 20.9 %norm.1.hidden_ref = bf16[4096,2048]{1,0:T(8,128)(2,1)} custom-call(bf16[4096,2048]{1,0:T(8,128)(2,1)} %x_ref.11, f32[1,2048]{1,0:T(1,128)} %bitcast.74, f32[1,2048]{1,0:T(1,128)} %bitcast.86), custom_call_target="tpu_custom_call" | custom-call | bytes 33570816 | tf_op jit(solution)/shard_map/norm/pallas_call | solution.py:236
  62.1 36.8 %qkv_project.1 = bf16[2,4096,768]{2,1,0:T(8,128)(2,1)} custom-call(s32[16]{0:T(128)} %dynamic_slice.3.where_ref, bf16[4096,2048]{1,0:T(8,128)(2,1)} %norm.1.hidden_ref, bf16[2048,1536]{1,0:T(8,128)(2,1)} %all-gather.5.cloned.1.call-done.weight_ref.refs_3_, f32[1,1536]{1,0:T(1,128)} %reshape.163.bias_ref, f32[2304,128]{1,0:T(8,128)} %concatenate.69.cos_ref.refs_12_, ...), custom_call_target="tpu_custom_call" | custom-call | flops 25769803776 | bytes 46137344 | tf_op jit(solution)/shard_map/qkv_project/pallas_call | solution.py:132
  120.4 60.7 %expand.1 = (bf16[4096,2048]{1,0:T(8,128)(2,1)}, bf16[4096,2048]{1,0:T(8,128)(2,1)}) custom-call(bf16[4096,2048]{1,0:T(8,128)(2,1)} %norm.1.hidden_ref, bf16[2048,2048]{1,0:T(8,128)(2,1)} %all-gather.7.cloned.1.call-done.weight_ref.refs_1_, f32[1,2048]{1,0:T(1,128)} %bitcast.89), custom_call_target="tpu_custom_call" | custom-call | flops 34359738368 | bytes 58728448 | tf_op jit(solution)/shard_map/expand/pallas_call | solution.py:236
  182.3 28.7 %all-gather.9.cloned.1.call-done.weight_ref = bf16[2048,2048]{1,0:T(8,128)(2,1)} async-done(((bf16[2048,256]{1,0:T(8,128)(2,1)}), bf16[2048,2048]{1,0:T(8,128)(2,1)}) %all-gather.9.cloned.1.call-update) | async-done | bytes 8388624 | tf_op jit(solution)/shard_map/all_gather | solution.py:935
  211.0 42.2 %shrink.1.refs_0_ = bf16[4096,2048]{1,0:T(8,128)(2,1)} custom-call(bf16[4096,2048]{1,0:T(8,128)(2,1)} %get-tuple-element.585.act_ref, bf16[2048,2048]{1,0:T(8,128)(2,1)} %all-gather.9.cloned.1.call-done.weight_ref), custom_call_target="tpu_custom_call" | custom-call | flops 34359738368 | bytes 41943040 | tf_op jit(solution)/shard_map/shrink/pallas_call | solution.py:236
  268.3 23.2 %all-to-all-done = bf16[2,4096,768]{2,1,0:T(8,128)(2,1)} async-done(((bf16[2,4096,768]{2,1,0:T(8,128)(2,1)}), bf16[2,4096,768]{2,1,0:T(8,128)(2,1)}, u32[]{:S(2)}, u32[]{:S(2)}) %all-to-all-start) | async-done | bytes 12582944 | tf_op jit(solution)/shard_map/all_to_all | solution.py:954
  295.7 27.9 %attend.4 = (bf16[2048,256]{1,0:T(8,128)(2,1)}, f32[256,2048]{1,0:T(8,128)}, f32[1,4,2048]{2,1,0:T(4,128)}) custom-call(s32[32]{0:T(128)} %pad_add_fusion.1.group_ref.refs_0_, s32[32]{0:T(128)} %copy-done.68, s32[8]{0:T(128)} %reshape_squeeze.38.item_ref.refs_2_, ...), custom_call_target="tpu_custom_call" | custom-call | flops 19327352832 | bytes 6291456 | tf_op jit(solution)/shard_map/attend/pallas_call | solution.py:531
  352.9 35.0 %attend.5 = (bf16[2048,256]{1,0:T(8,128)(2,1)}, f32[256,2048]{1,0:T(8,128)}, f32[1,4,2048]{2,1,0:T(4,128)}) custom-call(s32[32]{0:T(128)} %pad_add_fusion.1.group_ref.refs_0_, s32[32]{0:T(128)} %copy-done.68, s32[8]{0:T(128)} %reshape_squeeze.39.item_ref.refs_2_, ...), custom_call_target="tpu_custom_call" | custom-call | flops 19327352832 | bytes 6291456 | tf_op jit(solution)/shard_map/attend/pallas_call | solution.py:531
  413.3 28.0 %attend.6 = (bf16[2048,256]{1,0:T(8,128)(2,1)}, f32[256,2048]{1,0:T(8,128)}, f32[1,4,2048]{2,1,0:T(4,128)}) custom-call(s32[32]{0:T(128)} %pad_add_fusion.1.group_ref.refs_0_, s32[32]{0:T(128)} %copy-done.68, s32[8]{0:T(128)} %reshape_squeeze.40.item_ref.refs_2_, ...), custom_call_target="tpu_custom_call" | custom-call | flops 19327352832 | bytes 6291456 | tf_op jit(solution)/shard_map/attend/pallas_call | solution.py:531
  472.1 34.9 %attend.7 = (bf16[2048,256]{1,0:T(8,128)(2,1)}, f32[256,2048]{1,0:T(8,128)}, f32[1,4,2048]{2,1,0:T(4,128)}) custom-call(s32[32]{0:T(128)} %pad_add_fusion.1.group_ref.refs_0_, s32[32]{0:T(128)} %copy-done.68, s32[8]{0:T(128)} %reshape_squeeze.41.item_ref.refs_2_, ...), custom_call_target="tpu_custom_call" | custom-call | flops 19327352832 | bytes 6291456 | tf_op jit(solution)/shard_map/attend/pallas_call | solution.py:531
  536.9 49.9 %attend_back.4 = (bf16[2048,256]{1,0:T(8,128)(2,1)}, bf16[1024,256]{1,0:T(8,128)(2,1)}, bf16[1024,256]{1,0:T(8,128)(2,1)}, f32[4096,256]{1,0:T(8,128)}, f32[4096,256]{1,0:T(8,128)}) custom-call(s32[32]{0:T(128)} %pad_add_fusion.1.group_ref.refs_0_, s32[32]{0:T(128)} %copy-done.68, s32[8]{0:T(128)} %reshape_squeeze.38.item_ref.refs_2_, ...), custom_call_target="tpu_custom_call" | custom-call | flops 38654705664 | bytes 12582912 | tf_op jit(solution)/shard_map/attend_back/pallas_call | solution.py:572
  598.6 64.0 %attend_back.5 = (bf16[2048,256]{1,0:T(8,128)(2,1)}, bf16[1024,256]{1,0:T(8,128)(2,1)}, bf16[1024,256]{1,0:T(8,128)(2,1)}, f32[4096,256]{1,0:T(8,128)}, f32[4096,256]{1,0:T(8,128)}) custom-call(s32[32]{0:T(128)} %pad_add_fusion.1.group_ref.refs_0_, s32[32]{0:T(128)} %copy-done.68, ...), custom_call_target="tpu_custom_call", output_to_operand_aliasing={{3}: (15, {}), {4}: (16, {})} | custom-call | flops 38654705664 | bytes 12582912 | tf_op jit(solution)/shard_map/attend_back/pallas_call | solution.py:572
  673.5 52.2 %attend_back.6 = (bf16[2048,256]{1,0:T(8,128)(2,1)}, bf16[1024,256]{1,0:T(8,128)(2,1)}, bf16[1024,256]{1,0:T(8,128)(2,1)}, f32[4096,256]{1,0:T(8,128)}, f32[4096,256]{1,0:T(8,128)}) custom-call(s32[32]{0:T(128)} %pad_add_fusion.1.group_ref.refs_0_, s32[32]{0:T(128)} %copy-done.68, ...), custom_call_target="tpu_custom_call", output_to_operand_aliasing={{3}: (15, {}), {4}: (16, {})} | custom-call | flops 38654705664 | bytes 12582912 | tf_op jit(solution)/shard_map/attend_back/pallas_call | solution.py:572
  736.6 64.0 %attend_back.7 = (bf16[2048,256]{1,0:T(8,128)(2,1)}, bf16[1024,256]{1,0:T(8,128)(2,1)}, bf16[1024,256]{1,0:T(8,128)(2,1)}, f32[4096,256]{1,0:T(8,128)}, f32[4096,256]{1,0:T(8,128)}) custom-call(s32[32]{0:T(128)} %pad_add_fusion.1.group_ref.refs_0_, s32[32]{0:T(128)} %copy-done.68, ...), custom_call_target="tpu_custom_call", output_to_operand_aliasing={{3}: (15, {}), {4}: (16, {})} | custom-call | flops 38654705664 | bytes 12582912 | tf_op jit(solution)/shard_map/attend_back/pallas_call | solution.py:572
  826.3 46.1 %slope.1 = (bf16[4096,2048]{1,0:T(8,128)(2,1)}, f32[1,2048]{1,0:T(1,128)}, f32[1,2048]{1,0:T(1,128)}) custom-call(bf16[4096,2048]{1,0:T(8,128)(2,1)} %cot_ref.7, bf16[4096,2048]{1,0:T(8,128)(2,1)} %get-tuple-element.559.slope_ref, bf16[2048,2048]{1,0:T(8,128)(2,1)} %all-gather.9.cloned.1.call-done.weight_ref), custom_call_target="tpu_custom_call" | custom-call | flops 34359738368 | bytes 58736640 | tf_op jit(solution)/shard_map/slope/pallas_call | solution.py:236
  877.0 23.6 %grad_part.4.refs_5_.refs_0_.refs_1_ = bf16[1024,2048]{1,0:T(8,128)(2,1)} custom-call(bf16[4096,2048]{1,0:T(8,128)(2,1)} %get-tuple-element.681.refs_0_, bf16[2048,2048]{1,0:T(8,128)(2,1)} %all-gather.7.cloned.1.call-done.weight_ref.refs_1_, bf16[1024,1536]{1,0:T(8,128)(2,1)} %pad_maximum_fusion.1.refs_2_, ...), custom_call_target="tpu_custom_call" | custom-call | flops 15032385536 | bytes 29360128 | tf_op jit(solution)/shard_map/grad_part/pallas_call | solution.py:286
  917.4 43.3 %convolution_convert_fusion.1 = bf16[2048,2048]{1,0:T(8,128)(2,1)} fusion(bf16[4096,2048]{1,0:T(8,128)(2,1)} %get-tuple-element.585.act_ref, bf16[4096,2048]{1,0:T(8,128)(2,1)} %cot_ref.7), kind=kOutput, calls=%fused_computation.5 | convolution fusion | flops 34363932672 | bytes 41943040 | tf_op jit(solution)/shard_map/ra,rb->ab/dot_general | solution.py:32
  993.1 23.8 %grad_part.5.refs_3_.refs_0_.refs_1_ = bf16[1024,2048]{1,0:T(8,128)(2,1)} custom-call(bf16[4096,2048]{1,0:T(8,128)(2,1)} %get-tuple-element.681.refs_0_, bf16[2048,2048]{1,0:T(8,128)(2,1)} %all-gather.7.cloned.1.call-done.weight_ref.refs_1_, bf16[1024,1536]{1,0:T(8,128)(2,1)} %pad_maximum_fusion.2.refs_2_, ...), custom_call_target="tpu_custom_call" | custom-call | flops 15032385536 | bytes 29360128 | tf_op jit(solution)/shard_map/grad_part/pallas_call | solution.py:286
  1036.3 23.7 %fusion.4 = bf16[2048,1024]{1,0:T(8,128)(2,1)} fusion(bf16[4096,2048]{1,0:T(8,128)(2,1)} %norm.1.hidden_ref, bf16[4096,2048]{1,0:T(8,128)(2,1)} %get-tuple-element.681.refs_0_), kind=kOutput, calls=%fused_computation.11 | convolution fusion | flops 17181966336 | bytes 29360128 | tf_op jit(solution)/shard_map/ra,rb->ab/dot_general | solution.py:32
  1093.1 23.8 %grad_part.6.refs_3_.refs_0_.refs_1_ = bf16[1024,2048]{1,0:T(8,128)(2,1)} custom-call(bf16[4096,2048]{1,0:T(8,128)(2,1)} %get-tuple-element.681.refs_0_, bf16[2048,2048]{1,0:T(8,128)(2,1)} %all-gather.7.cloned.1.call-done.weight_ref.refs_1_, bf16[1024,1536]{1,0:T(8,128)(2,1)} %pad_maximum_fusion.3.refs_2_, ...), custom_call_target="tpu_custom_call" | custom-call | flops 15032385536 | bytes 29360128 | tf_op jit(solution)/shard_map/grad_part/pallas_call | solution.py:286
  1132.3 23.8 %fusion.7 = bf16[2048,1024]{1,0:T(8,128)(2,1)} fusion(bf16[4096,2048]{1,0:T(8,128)(2,1)} %norm.1.hidden_ref, bf16[4096,2048]{1,0:T(8,128)(2,1)} %get-tuple-element.681.refs_0_), kind=kOutput, calls=%fused_computation.12 | convolution fusion | flops 17181966336 | bytes 29360128 | tf_op jit(solution)/shard_map/ra,rb->ab/dot_general | solution.py:32
  1188.1 24.4 %grad_part.7.refs_3_.refs_0_.refs_1_ = bf16[1024,2048]{1,0:T(8,128)(2,1)} custom-call(bf16[4096,2048]{1,0:T(8,128)(2,1)} %get-tuple-element.681.refs_0_, bf16[2048,2048]{1,0:T(8,128)(2,1)} %all-gather.7.cloned.1.call-done.weight_ref.refs_1_, bf16[1024,1536]{1,0:T(8,128)(2,1)} %pad_maximum_fusion.4.refs_2_, ...), custom_call_target="tpu_custom_call" | custom-call | flops 15032385536 | bytes 29360128 | tf_op jit(solution)/shard_map/grad_part/pallas_call | solution.py:286
  1234.7 34.0 %convolution_convert_fusion = bf16[2048,1536]{1,0:T(8,128)(2,1)} fusion(bf16[4096,2048]{1,0:T(8,128)(2,1)} %norm.1.hidden_ref, bf16[4096,1536]{1,0:T(8,128)(2,1)} %constant_dynamic-update-slice_fusion.6), kind=kOutput, calls=%fused_computation.4 | convolution fusion | flops 25772949504 | bytes 35651584 | tf_op jit(solution)/shard_map/ra,rb->ab/dot_general | solution.py:32
  1389.1 26.5 %psum.7 = f32[9728]{0:T(1024)S(1)} all-reduce(f32[9728]{0:T(1024)S(1)} %pad_maximum_fusion.14), channel_id=1, replica_groups=mesh['dp'=4,'ctx'=2,'tp'=4] {'dp','ctx'}, use_global_device_ids=true, to_apply=%region_4.5 | all-reduce | flops 9728 | bytes 77824 | tf_op jit(solution)/shard_map/psum | solution.py:1136
  (392 shorter events, 562.2 us)
Async XLA Ops:
  7.2 53.0 %all-gather.5.cloned.1.call-start = ((), (), s32[]{:S(2)}) async-start(), calls=%async_computation.7 | async-start | bytes 7077888 | tf_op jit(solution)/shard_map/all_gather | solution.py:911
  11.8 108.6 %all-gather.7.cloned.1.call-start = ((), (), s32[]{:S(2)}) async-start(), calls=%async_computation.8 | async-start | bytes 9437184 | tf_op jit(solution)/shard_map/all_gather | solution.py:912
  12.5 198.4 %all-gather.9.cloned.1.call-start = ((), (), s32[]{:S(2)}) async-start(), calls=%async_computation.9 | async-start | bytes 9437184 | tf_op jit(solution)/shard_map/all_gather | solution.py:935
  98.9 192.7 %all-to-all-start = ((bf16[2,4096,768]{2,1,0:T(8,128)(2,1)}), bf16[2,4096,768]{2,1,0:T(8,128)(2,1)}, u32[]{:S(2)}, u32[]{:S(2)}) async-start(bf16[2,4096,768]{2,1,0:T(8,128)(2,1)} %qkv_project.1), calls=%async_computation | async-start | bytes 25165824 | tf_op jit(solution)/shard_map/all_to_all | solution.py:954
  107.3 145.9 %all-gather.11.cloned.1.call-start = ((), (), s32[]{:S(2)}) async-start(), calls=%async_computation.10 | async-start | bytes 2359296 | tf_op jit(solution)/shard_map/all_gather | solution.py:970
  444.4 82.5 %all-to-all-start.1 = ((bf16[2,4096,256]{2,1,0:T(8,128)(2,1)}), bf16[2,4096,256]{2,1,0:T(8,128)(2,1)}, u32[]{:S(2)}, u32[]{:S(2)}) async-start(bf16[2,4096,256]{2,1,0:T(8,128)(2,1)} %grad_attended.1), calls=%async_computation.1 | async-start | bytes 8388608 | tf_op jit(solution)/shard_map/all_to_all | solution.py:954
  450.1 924.7 %reduce-scatter.14.cloned.1.call-start = ((), (), s32[]{:S(2)}) async-start(), calls=%async_computation.15 | async-start | bytes 9437184 | tf_op jit(solution)/shard_map/reduce_scatter | solution.py:1100
  465.7 53.3 %collective-permute-start.6 = (bf16[512,2048]{1,0:T(8,128)(2,1)S(1)}, bf16[512,2048]{1,0:T(8,128)(2,1)S(1)}, u32[]{:S(2)}, u32[]{:S(2)}) collective-permute-start(bf16[512,2048]{1,0:T(8,128)(2,1)S(1)} %copy-done.20), channel_id=1, source_target_pairs={{0,1},{3,2},{1,0},{2,3},{4,5},{7,6},{5,4},{6,7},{8,9},{11,10},{9,8... | collective-permute-start | bytes 6291464 | tf_op jit(solution)/shard_map/ppermute | solution.py:885
  526.9 59.9 %collective-permute-start.9 = (bf16[512,2048]{1,0:T(8,128)(2,1)}, bf16[512,2048]{1,0:T(8,128)(2,1)S(1)}, u32[]{:S(2)}, u32[]{:S(2)}) collective-permute-start(bf16[512,2048]{1,0:T(8,128)(2,1)} %get-tuple-element.465), channel_id=1, source_target_pairs={{0,1},{3,2},{1,0},{2,3},{4,5},{7,6},{5,4},{6,7},{8,9},{11,10},{9,8... | collective-permute-start | bytes 6291464 | tf_op jit(solution)/shard_map/ppermute | solution.py:885
  527.6 59.2 %collective-permute-start.10 = (bf16[512,2048]{1,0:T(8,128)(2,1)}, bf16[512,2048]{1,0:T(8,128)(2,1)S(1)}, u32[]{:S(2)}, u32[]{:S(2)}) collective-permute-start(bf16[512,2048]{1,0:T(8,128)(2,1)} %get-tuple-element.466), channel_id=1, source_target_pairs={{1,2},{2,1},{5,6},{6,5},{9,10},{10,9},{13,14},{14,13},{17,18},{18,... | collective-permute-start | bytes 6291464 | tf_op jit(solution)/shard_map/ppermute | solution.py:886
  593.4 69.1 %collective-permute-start.11 = (bf16[512,2048]{1,0:T(8,128)(2,1)}, bf16[512,2048]{1,0:T(8,128)(2,1)S(1)}, u32[]{:S(2)}, u32[]{:S(2)}) collective-permute-start(bf16[512,2048]{1,0:T(8,128)(2,1)} %line_begin.11.b), channel_id=1, source_target_pairs={{0,1},{3,2},{1,0},{2,3},{4,5},{7,6},{5,4},{6,7},{8,9},{11,10},{9,8... | collective-permute-start | bytes 6291464 | tf_op jit(solution)/shard_map/ppermute | solution.py:885
  597.8 64.8 %collective-permute-start.12 = (bf16[512,2048]{1,0:T(8,128)(2,1)}, bf16[512,2048]{1,0:T(8,128)(2,1)S(1)}, u32[]{:S(2)}, u32[]{:S(2)}) collective-permute-start(bf16[512,2048]{1,0:T(8,128)(2,1)} %line_begin.11.b), channel_id=1, source_target_pairs={{1,2},{2,1},{5,6},{6,5},{9,10},{10,9},{13,14},{14,13},{17,18},{18,... | collective-permute-start | bytes 6291464 | tf_op jit(solution)/shard_map/ppermute | solution.py:886
  669.7 56.1 %collective-permute-start.13 = (bf16[512,2048]{1,0:T(8,128)(2,1)}, bf16[512,2048]{1,0:T(8,128)(2,1)S(1)}, u32[]{:S(2)}, u32[]{:S(2)}) collective-permute-start(bf16[512,2048]{1,0:T(8,128)(2,1)} %get-tuple-element.511), channel_id=1, source_target_pairs={{0,1},{3,2},{1,0},{2,3},{4,5},{7,6},{5,4},{6,7},{8,9},{11,10},{9,8... | collective-permute-start | bytes 6291464 | tf_op jit(solution)/shard_map/ppermute | solution.py:885
  672.5 53.3 %collective-permute-start.14 = (bf16[512,2048]{1,0:T(8,128)(2,1)}, bf16[512,2048]{1,0:T(8,128)(2,1)S(1)}, u32[]{:S(2)}, u32[]{:S(2)}) collective-permute-start(bf16[512,2048]{1,0:T(8,128)(2,1)} %get-tuple-element.512), channel_id=1, source_target_pairs={{1,2},{2,1},{5,6},{6,5},{9,10},{10,9},{13,14},{14,13},{17,18},{18,... | collective-permute-start | bytes 6291464 | tf_op jit(solution)/shard_map/ppermute | solution.py:886
  732.4 76.8 %collective-permute-start.15 = (bf16[512,2048]{1,0:T(8,128)(2,1)}, bf16[512,2048]{1,0:T(8,128)(2,1)S(1)}, u32[]{:S(2)}, u32[]{:S(2)}) collective-permute-start(bf16[512,2048]{1,0:T(8,128)(2,1)} %line_begin.12.b), channel_id=1, source_target_pairs={{0,1},{3,2},{1,0},{2,3},{4,5},{7,6},{5,4},{6,7},{8,9},{11,10},{9,8... | collective-permute-start | bytes 6291464 | tf_op jit(solution)/shard_map/ppermute | solution.py:885
  735.6 73.6 %collective-permute-start.16 = (bf16[512,2048]{1,0:T(8,128)(2,1)}, bf16[512,2048]{1,0:T(8,128)(2,1)S(1)}, u32[]{:S(2)}, u32[]{:S(2)}) collective-permute-start(bf16[512,2048]{1,0:T(8,128)(2,1)} %line_begin.12.b), channel_id=1, source_target_pairs={{1,2},{2,1},{5,6},{6,5},{9,10},{10,9},{13,14},{14,13},{17,18},{18,... | collective-permute-start | bytes 6291464 | tf_op jit(solution)/shard_map/ppermute | solution.py:886
  820.7 51.7 %collective-permute-start.19 = (bf16[1024,768]{1,0:T(8,128)(2,1)}, bf16[1024,768]{1,0:T(8,128)(2,1)}, u32[]{:S(2)}, u32[]{:S(2)}) collective-permute-start(bf16[1024,768]{1,0:T(8,128)(2,1)} %get-tuple-element.826), channel_id=1, source_target_pairs={{0,4},{4,0},{1,5},{5,1},{2,6},{6,2},{3,7},{7,3},{8,12},{12,8},{9,1... | collective-permute-start | bytes 4718600 | tf_op jit(solution)/shard_map/ppermute | solution.py:943
  822.4 78.3 %collective-permute-start.17 = (bf16[512,2048]{1,0:T(8,128)(2,1)}, bf16[512,2048]{1,0:T(8,128)(2,1)S(1)}, u32[]{:S(2)}, u32[]{:S(2)}) collective-permute-start(bf16[512,2048]{1,0:T(8,128)(2,1)} %get-tuple-element.556), channel_id=1, source_target_pairs={{0,1},{3,2},{1,0},{2,3},{4,5},{7,6},{5,4},{6,7},{8,9},{11,10},{9,8... | collective-permute-start | bytes 6291464 | tf_op jit(solution)/shard_map/ppermute | solution.py:885
  825.1 75.6 %collective-permute-start.18 = (bf16[512,2048]{1,0:T(8,128)(2,1)}, bf16[512,2048]{1,0:T(8,128)(2,1)S(1)}, u32[]{:S(2)}, u32[]{:S(2)}) collective-permute-start(bf16[512,2048]{1,0:T(8,128)(2,1)} %get-tuple-element.557), channel_id=1, source_target_pairs={{1,2},{2,1},{5,6},{6,5},{9,10},{10,9},{13,14},{14,13},{17,18},{18,... | collective-permute-start | bytes 6291464 | tf_op jit(solution)/shard_map/ppermute | solution.py:886
  960.7 416.8 %reduce-scatter.10.cloned.1.call-start = ((), (), s32[]{:S(2)}) async-start(), calls=%async_computation.13 | async-start | bytes 4718592 | tf_op jit(solution)/shard_map/reduce_scatter | solution.py:1100
  1081.6 295.9 %reduce-scatter.12.cloned.1.call-start = ((), (), s32[]{:S(2)}) async-start(), calls=%async_computation.14 | async-start | bytes 4718592 | tf_op jit(solution)/shard_map/reduce_scatter | solution.py:1100
  1184.1 231.5 %reduce-scatter.8.cloned.1.call-start = ((), (), s32[]{:S(2)}) async-start(), calls=%async_computation.12 | async-start | bytes 2359296 | tf_op jit(solution)/shard_map/reduce_scatter | solution.py:1100
  1313.4 113.3 %reduce-scatter.6.cloned.1.call-start = ((), (), s32[]{:S(2)}) async-start(), calls=%async_computation.11 | async-start | bytes 7077888 | tf_op jit(solution)/shard_map/reduce_scatter | solution.py:1100
  1363.3 54.0 %collective-permute-start.43 = (bf16[512,2048]{1,0:T(8,128)(2,1)}, bf16[512,2048]{1,0:T(8,128)(2,1)}, u32[]{:S(2)}, u32[]{:S(2)}) collective-permute-start(bf16[512,2048]{1,0:T(8,128)(2,1)} %collective-permute-done.40.d), channel_id=1, source_target_pairs={{0,1},{3,2},{1,0},{2,3},{4,5},{7,6},{5,4},{6,7},{8,9},{11,10},{9,8... | collective-permute-start | bytes 6291464 | tf_op jit(solution)/shard_map/ppermute | solution.py:885
  (100 other events, 1673.5 us)
Sparse Core Ops, SparseCore 0:
  11.9 48.2 all-gather.4
  62.1 58.2 all-gather.6
  122.2 88.6 all-gather.8
  212.7 36.2 all-gather.10
  960.8 74.9 reduce-scatter.13
  1081.8 54.0 reduce-scatter.9
  1184.2 50.3 reduce-scatter.11
  1313.5 42.8 reduce-scatter.7
  1359.8 63.0 reduce-scatter.5

commit v5 on v4

--- a/solution.py
+++ b/solution.py
@@ -887,6 +887,15 @@
     )
 
 
+def unwritten(shape):
+    return pl.pallas_call(
+        lambda out_ref: None,
+        out_specs=pl.BlockSpec(memory_space=pl.ANY),
+        out_shape=jax.ShapeDtypeStruct(shape, BF16),
+        name="unwritten",
+    )()
+
+
 def body(
     tokens, cotangent, membership, ln_gain, ln_bias, w_query, b_query, w_key, b_key, w_value,
     b_value, w_dense, b_dense, w_fc1, b_fc1, w_fc2, b_fc2,
@@ -993,9 +1002,10 @@
         def keep(out):
             came, env["turned", b], env["lse", b] = out
             env["attended", b] = end_exchange(came)
+            whole = env["whole"] if b else unwritten((rows, local))
             for c, part in enumerate(env["attended", b]):
-                before = env.get(("whole", c), jnp.zeros((rows, share), BF16))
-                env["whole", c] = lax.dynamic_update_slice(before, part, (b * block, 0))
+                whole = lax.dynamic_update_slice(whole, part, (b * block, c * share))
+            env["whole"] = whole
 
         return run, (qkv_all, turned_v), keep
 
@@ -1085,7 +1095,7 @@
 
         def keep(out):
             env["part", blocks + b], grad, env["qkv_sum", b] = out
-            before = env.get("all_qkv", jnp.zeros((rows, 3 * local), BF16))
+            before = env["all_qkv"] if b else unwritten((rows, 3 * local))
             env["all_qkv"] = lax.dynamic_update_slice(before, grad, (b * block, 0))
 
         return run, (env["grad_expand"], expand_weight, env["sent_back", b], qkv_weight), keep
@@ -1140,24 +1150,10 @@
 
         return run, (pieces(),), keep
 
-    def share_sums():
-        def run(parts):
-            own = jnp.concatenate([sum(part) for part in parts])
-            both = own + lax.ppermute(own, "tp", [(1, 2), (2, 1)])
-            return jnp.where(line.outer, lax.ppermute(both, "tp", [(1, 0), (2, 3)]), both)
-
-        def keep(out):
-            env["norm_sums"] = out
-
-        parts = [[env[name, b] for b in range(blocks)] for name in ("gain", "shift")]
-        return run, (parts,), keep
-
     def all_pieces():
         total = sum(env["qkv_sum", b] for b in range(blocks))
-        return [env["norm_sums"].reshape(-1), total, env["expand_sum"][0], env["cot_sum"][0]]
-
-    def all_attended():
-        return jnp.concatenate([env["whole", c] for c in range(ctx_count)], axis=1)
+        own = [sum(env[name, b][0] for b in range(blocks)) for name in ("gain", "shift")]
+        return [*own, total, env["expand_sum"][0], env["cot_sum"][0]]
 
     ticks = 4 * blocks + 2
     plan = [[] for _ in range(ticks + 8)]
@@ -1175,7 +1171,7 @@
             add(turn - 1 + 2 * b, grad_part, b)
         add(turn + 1 + 2 * b, put_out, b)
         add(turn + 2 * b + 2, sums, b)
-        if b < last - 1:
+        if b < last:
             add(turn + 2 * b + 4 + b % 2, put_grad, b, 0, 2)
     add(0, turn_keys)
     after[turn - 2].append(finish)
@@ -1186,9 +1182,7 @@
     add(turn + 2, lambda: weight_grad("fc1", hidden, env["grad_expand"], 0, 0, 2))
     add(turn + 4, lambda: weight_grad("fc1", hidden, env["grad_expand"], 0, 1, 2))
     add(2 * turn - 2, lambda: weight_grad("qkv", hidden, env["all_qkv"], 0, 0, 1))
-    add(2 * turn - 1, lambda: weight_grad("dense", all_attended(), cotangent, 1, 0, 1))
-    after[ticks - 2].append(share_sums)
-    after[ticks - 2].append(functools.partial(put_grad, last - 1, 0, 2))
+    add(2 * turn - 1, lambda: weight_grad("dense", env["whole"], cotangent, 1, 0, 1))
     add(ticks - 1, add_all, "total", ("dp", "ctx"), all_pieces)
     add(ticks - 1, put_grad, last, 0, 1)
     add(ticks, put_grad, last, 1, 1)
@@ -1229,14 +1223,17 @@
         if not stages:
             arrived = send(*operands)
     env["total", 2 * blocks - 1] = line.end(*arrived)
+    own = env["total"][: 2 * width]
+    both = own + lax.ppermute(own, "tp", [(1, 2), (2, 1)])
+    norm_total = jnp.where(line.outer, lax.ppermute(both, "tp", [(1, 0), (2, 3)]), both)
     for late in plan[ticks:]:
         for make in late:
             perform(make)
 
     layer_out, grad_tokens = env["layer_out"], env["grad_tokens"]
-    sizes = (width, width, 3 * local, w_fc1.shape[1])
-    gain_sum, shift_sum, qkv_sum, expand_total, out_sum = jnp.split(
-        env["total"], [sum(sizes[: i + 1]) for i in range(len(sizes))]
+    gain_sum, shift_sum = jnp.split(norm_total, 2)
+    qkv_sum, expand_total, out_sum = jnp.split(
+        env["total"][2 * width :], (3 * local, 3 * local + w_fc1.shape[1])
     )
 
     def unmixed(array):

time: 1450 us -> 1440 us (level)
    ppermute x18, waiting for transfers between devices: 8.52 us -> 33.4 us  [send(): lax.ppermute(swap, 'tp', outer)]
    ppermute x2, waiting for transfers between devices: 19.4 us -> 0.01 us  [the longest x1 0.01 us: body(): both = own + lax.ppermute(own, 'tp', [(1, 2), (2, 1)])]
  transfers between devices with their start and end apart: 55 -> 55, of which waited for: 11 -> 15; matrix products, arithmetic and copies ran while one was open for 16% -> 15% of each run, Pallas kernels for 57% -> 58%
where the time goes in v5:
time: 1440 us
  Pallas kernels  899 us (62%)
  matrix products  138 us (10%)
  waiting for transfers between devices  132 us (9%)
  starting transfers between devices  102 us (7%)
  local copies, waits for them, and re-layouts  63.5 us (4%)
  other arithmetic  59.1 us (4%)
  blocking collectives  26.3 us (2%)
  between operations  15.3 us (1%)
    pallas_call x4, Pallas kernels, attend_back(): pl.pallas_call(functools.partial(attend_back_kernel, 1024, first, GPR * P...  230 us
    pallas_call x4, Pallas kernels, row_call(): pl.pallas_call(kernel, grid=(rows // count,), in_specs=[spec(a.shape) for...  170 us
    dot_general x5, matrix products, transpose_dot(): return jnp.einsum('ra,rb->ab', left, right, preferred_element_type=F32)  138 us
    pallas_call x8, Pallas kernels, products(): pl.pallas_call(functools.partial(products_kernel, kinds, base is not None...  130 us
    pallas_call x4, Pallas kernels, attend(): pl.pallas_call(functools.partial(attend_kernel, 1024), grid_spec=pltpu.Pr...  126 us
    pallas_call x17, Pallas kernels, line_call(): pl.pallas_call(functools.partial(kernel, [i[0] for i in ins] + outs), gri...  80.4 us
    pallas_call x5, Pallas kernels, norm_back(): pl.pallas_call(functools.partial(norm_back_kernel, begin), grid_spec=pltp...  55.3 us
    ppermute x18, starting transfers between devices, send(): lax.ppermute(swap, 'tp', outer)  53.2 us
  transfers between devices with their start and end apart: 55, of which 15 were waited for; matrix products, arithmetic and copies ran while one was open for 15% of the time, Pallas kernels for 58%

profile of v5, /device:TPU:0, one launch (start us, length us, event | category | flops | bytes accessed | tf_op | source)
XLA Modules:
  0.0 1435.4 jit_solution(13497907609430748153)
XLA Ops:
  62.1 36.7 %qkv_project.1 = bf16[2,4096,768]{2,1,0:T(8,128)(2,1)} custom-call(s32[16]{0:T(128)} %dynamic_slice.3.where_ref, bf16[4096,2048]{1,0:T(8,128)(2,1)} %norm.1.hidden_ref, bf16[2048,1536]{1,0:T(8,128)(2,1)} %all-gather.5.cloned.1.call-done.weight_ref.refs_3_, f32[1,1536]{1,0:T(1,128)} %reshape.165.bias_ref, f32[2304,128]{1,0:T(8,128)} %concatenate.63.cos_ref.refs_12_, ...), custom_call_target="tpu_custom_call" | custom-call | flops 25769803776 | bytes 46137344 | tf_op jit(solution)/shard_map/qkv_project/pallas_call | solution.py:132
  120.4 60.7 %expand.1 = (bf16[4096,2048]{1,0:T(8,128)(2,1)}, bf16[4096,2048]{1,0:T(8,128)(2,1)}) custom-call(bf16[4096,2048]{1,0:T(8,128)(2,1)} %norm.1.hidden_ref, bf16[2048,2048]{1,0:T(8,128)(2,1)} %all-gather.7.cloned.1.call-done.weight_ref.refs_1_, f32[1,2048]{1,0:T(1,128)} %bitcast.87), custom_call_target="tpu_custom_call" | custom-call | flops 34359738368 | bytes 58728448 | tf_op jit(solution)/shard_map/expand/pallas_call | solution.py:236
  182.3 28.7 %all-gather.9.cloned.1.call-done.weight_ref = bf16[2048,2048]{1,0:T(8,128)(2,1)} async-done(((bf16[2048,256]{1,0:T(8,128)(2,1)}), bf16[2048,2048]{1,0:T(8,128)(2,1)}) %all-gather.9.cloned.1.call-update) | async-done | bytes 8388624 | tf_op jit(solution)/shard_map/all_gather | solution.py:944
  211.0 42.2 %shrink.1.refs_0_ = bf16[4096,2048]{1,0:T(8,128)(2,1)} custom-call(bf16[4096,2048]{1,0:T(8,128)(2,1)} %get-tuple-element.579.act_ref, bf16[2048,2048]{1,0:T(8,128)(2,1)} %all-gather.9.cloned.1.call-done.weight_ref), custom_call_target="tpu_custom_call" | custom-call | flops 34359738368 | bytes 41943040 | tf_op jit(solution)/shard_map/shrink/pallas_call | solution.py:236
  268.3 23.2 %all-to-all-done = bf16[2,4096,768]{2,1,0:T(8,128)(2,1)} async-done(((bf16[2,4096,768]{2,1,0:T(8,128)(2,1)}), bf16[2,4096,768]{2,1,0:T(8,128)(2,1)}, u32[]{:S(2)}, u32[]{:S(2)}) %all-to-all-start) | async-done | bytes 12582944 | tf_op jit(solution)/shard_map/all_to_all | solution.py:963
  295.7 28.0 %attend.4 = (bf16[2048,256]{1,0:T(8,128)(2,1)}, f32[256,2048]{1,0:T(8,128)}, f32[1,4,2048]{2,1,0:T(4,128)}) custom-call(s32[32]{0:T(128)} %pad_add_fusion.1.group_ref.refs_0_, s32[32]{0:T(128)} %copy-done.69, s32[8]{0:T(128)} %reshape_squeeze.38.item_ref.refs_2_, ...), custom_call_target="tpu_custom_call" | custom-call | flops 19327352832 | bytes 6291456 | tf_op jit(solution)/shard_map/attend/pallas_call | solution.py:531
  354.2 34.9 %attend.5 = (bf16[2048,256]{1,0:T(8,128)(2,1)}, f32[256,2048]{1,0:T(8,128)}, f32[1,4,2048]{2,1,0:T(4,128)}) custom-call(s32[32]{0:T(128)} %pad_add_fusion.1.group_ref.refs_0_, s32[32]{0:T(128)} %copy-done.69, s32[8]{0:T(128)} %reshape_squeeze.39.item_ref.refs_2_, ...), custom_call_target="tpu_custom_call" | custom-call | flops 19327352832 | bytes 6291456 | tf_op jit(solution)/shard_map/attend/pallas_call | solution.py:531
  413.6 28.0 %attend.6 = (bf16[2048,256]{1,0:T(8,128)(2,1)}, f32[256,2048]{1,0:T(8,128)}, f32[1,4,2048]{2,1,0:T(4,128)}) custom-call(s32[32]{0:T(128)} %pad_add_fusion.1.group_ref.refs_0_, s32[32]{0:T(128)} %copy-done.69, s32[8]{0:T(128)} %reshape_squeeze.40.item_ref.refs_2_, ...), custom_call_target="tpu_custom_call" | custom-call | flops 19327352832 | bytes 6291456 | tf_op jit(solution)/shard_map/attend/pallas_call | solution.py:531
  471.8 34.9 %attend.7 = (bf16[2048,256]{1,0:T(8,128)(2,1)}, f32[256,2048]{1,0:T(8,128)}, f32[1,4,2048]{2,1,0:T(4,128)}) custom-call(s32[32]{0:T(128)} %pad_add_fusion.1.group_ref.refs_0_, s32[32]{0:T(128)} %copy-done.69, s32[8]{0:T(128)} %reshape_squeeze.41.item_ref.refs_2_, ...), custom_call_target="tpu_custom_call" | custom-call | flops 19327352832 | bytes 6291456 | tf_op jit(solution)/shard_map/attend/pallas_call | solution.py:531
  542.0 49.9 %attend_back.4 = (bf16[2048,256]{1,0:T(8,128)(2,1)}, bf16[1024,256]{1,0:T(8,128)(2,1)}, bf16[1024,256]{1,0:T(8,128)(2,1)}, f32[4096,256]{1,0:T(8,128)}, f32[4096,256]{1,0:T(8,128)}) custom-call(s32[32]{0:T(128)} %pad_add_fusion.1.group_ref.refs_0_, s32[32]{0:T(128)} %copy-done.69, s32[8]{0:T(128)} %reshape_squeeze.38.item_ref.refs_2_, ...), custom_call_target="tpu_custom_call" | custom-call | flops 38654705664 | bytes 12582912 | tf_op jit(solution)/shard_map/attend_back/pallas_call | solution.py:572
  600.8 64.0 %attend_back.5 = (bf16[2048,256]{1,0:T(8,128)(2,1)}, bf16[1024,256]{1,0:T(8,128)(2,1)}, bf16[1024,256]{1,0:T(8,128)(2,1)}, f32[4096,256]{1,0:T(8,128)}, f32[4096,256]{1,0:T(8,128)}) custom-call(s32[32]{0:T(128)} %pad_add_fusion.1.group_ref.refs_0_, s32[32]{0:T(128)} %copy-done.69, ...), custom_call_target="tpu_custom_call", output_to_operand_aliasing={{3}: (15, {}), {4}: (16, {})} | custom-call | flops 38654705664 | bytes 12582912 | tf_op jit(solution)/shard_map/attend_back/pallas_call | solution.py:572
  675.2 52.4 %attend_back.6 = (bf16[2048,256]{1,0:T(8,128)(2,1)}, bf16[1024,256]{1,0:T(8,128)(2,1)}, bf16[1024,256]{1,0:T(8,128)(2,1)}, f32[4096,256]{1,0:T(8,128)}, f32[4096,256]{1,0:T(8,128)}) custom-call(s32[32]{0:T(128)} %pad_add_fusion.1.group_ref.refs_0_, s32[32]{0:T(128)} %copy-done.69, ...), custom_call_target="tpu_custom_call", output_to_operand_aliasing={{3}: (15, {}), {4}: (16, {})} | custom-call | flops 38654705664 | bytes 12582912 | tf_op jit(solution)/shard_map/attend_back/pallas_call | solution.py:572
  739.4 64.1 %attend_back.7 = (bf16[2048,256]{1,0:T(8,128)(2,1)}, bf16[1024,256]{1,0:T(8,128)(2,1)}, bf16[1024,256]{1,0:T(8,128)(2,1)}, f32[4096,256]{1,0:T(8,128)}, f32[4096,256]{1,0:T(8,128)}) custom-call(s32[32]{0:T(128)} %pad_add_fusion.1.group_ref.refs_0_, s32[32]{0:T(128)} %copy-done.69, ...), custom_call_target="tpu_custom_call", output_to_operand_aliasing={{3}: (15, {}), {4}: (16, {})} | custom-call | flops 38654705664 | bytes 12582912 | tf_op jit(solution)/shard_map/attend_back/pallas_call | solution.py:572
  826.9 46.0 %slope.1 = (bf16[4096,2048]{1,0:T(8,128)(2,1)}, f32[1,2048]{1,0:T(1,128)}, f32[1,2048]{1,0:T(1,128)}) custom-call(bf16[4096,2048]{1,0:T(8,128)(2,1)} %cot_ref.7, bf16[4096,2048]{1,0:T(8,128)(2,1)} %get-tuple-element.553.slope_ref, bf16[2048,2048]{1,0:T(8,128)(2,1)} %all-gather.9.cloned.1.call-done.weight_ref), custom_call_target="tpu_custom_call" | custom-call | flops 34359738368 | bytes 58736640 | tf_op jit(solution)/shard_map/slope/pallas_call | solution.py:236
  877.6 23.6 %grad_part.4.refs_5_.refs_0_.refs_1_ = bf16[1024,2048]{1,0:T(8,128)(2,1)} custom-call(bf16[4096,2048]{1,0:T(8,128)(2,1)} %get-tuple-element.675.refs_0_, bf16[2048,2048]{1,0:T(8,128)(2,1)} %all-gather.7.cloned.1.call-done.weight_ref.refs_1_, bf16[1024,1536]{1,0:T(8,128)(2,1)} %pad_maximum_fusion.refs_2_, ...), custom_call_target="tpu_custom_call" | custom-call | flops 15032385536 | bytes 29360128 | tf_op jit(solution)/shard_map/grad_part/pallas_call | solution.py:286
  918.5 43.3 %convolution_convert_fusion.1 = bf16[2048,2048]{1,0:T(8,128)(2,1)} fusion(bf16[4096,2048]{1,0:T(8,128)(2,1)} %get-tuple-element.579.act_ref, bf16[4096,2048]{1,0:T(8,128)(2,1)} %cot_ref.7), kind=kOutput, calls=%fused_computation.5 | convolution fusion | flops 34363932672 | bytes 41943040 | tf_op jit(solution)/shard_map/ra,rb->ab/dot_general | solution.py:32
  985.3 24.2 %grad_part.5.refs_3_.refs_0_.refs_1_ = bf16[1024,2048]{1,0:T(8,128)(2,1)} custom-call(bf16[4096,2048]{1,0:T(8,128)(2,1)} %get-tuple-element.675.refs_0_, bf16[2048,2048]{1,0:T(8,128)(2,1)} %all-gather.7.cloned.1.call-done.weight_ref.refs_1_, bf16[1024,1536]{1,0:T(8,128)(2,1)} %pad_maximum_fusion.1.refs_2_, ...), custom_call_target="tpu_custom_call" | custom-call | flops 15032385536 | bytes 29360128 | tf_op jit(solution)/shard_map/grad_part/pallas_call | solution.py:286
  1030.0 23.8 %fusion.4 = bf16[2048,1024]{1,0:T(8,128)(2,1)} fusion(bf16[4096,2048]{1,0:T(8,128)(2,1)} %norm.1.hidden_ref, bf16[4096,2048]{1,0:T(8,128)(2,1)} %get-tuple-element.675.refs_0_), kind=kOutput, calls=%fused_computation.10 | convolution fusion | flops 17181966336 | bytes 29360128 | tf_op jit(solution)/shard_map/ra,rb->ab/dot_general | solution.py:32
  1086.4 23.9 %grad_part.6.refs_3_.refs_0_.refs_1_ = bf16[1024,2048]{1,0:T(8,128)(2,1)} custom-call(bf16[4096,2048]{1,0:T(8,128)(2,1)} %get-tuple-element.675.refs_0_, bf16[2048,2048]{1,0:T(8,128)(2,1)} %all-gather.7.cloned.1.call-done.weight_ref.refs_1_, bf16[1024,1536]{1,0:T(8,128)(2,1)} %pad_maximum_fusion.2.refs_2_, ...), custom_call_target="tpu_custom_call" | custom-call | flops 15032385536 | bytes 29360128 | tf_op jit(solution)/shard_map/grad_part/pallas_call | solution.py:286
  1129.4 23.7 %fusion.7 = bf16[2048,1024]{1,0:T(8,128)(2,1)} fusion(bf16[4096,2048]{1,0:T(8,128)(2,1)} %norm.1.hidden_ref, bf16[4096,2048]{1,0:T(8,128)(2,1)} %get-tuple-element.675.refs_0_), kind=kOutput, calls=%fused_computation.11 | convolution fusion | flops 17181966336 | bytes 29360128 | tf_op jit(solution)/shard_map/ra,rb->ab/dot_general | solution.py:32
  1185.1 24.5 %grad_part.7.refs_3_.refs_0_.refs_1_ = bf16[1024,2048]{1,0:T(8,128)(2,1)} custom-call(bf16[4096,2048]{1,0:T(8,128)(2,1)} %get-tuple-element.675.refs_0_, bf16[2048,2048]{1,0:T(8,128)(2,1)} %all-gather.7.cloned.1.call-done.weight_ref.refs_1_, bf16[1024,1536]{1,0:T(8,128)(2,1)} %pad_maximum_fusion.3.refs_2_, ...), custom_call_target="tpu_custom_call" | custom-call | flops 15032385536 | bytes 29360128 | tf_op jit(solution)/shard_map/grad_part/pallas_call | solution.py:286
  1233.8 34.0 %convolution_convert_fusion = bf16[2048,1536]{1,0:T(8,128)(2,1)} fusion(bf16[4096,2048]{1,0:T(8,128)(2,1)} %norm.1.hidden_ref, bf16[4096,1536]{1,0:T(8,128)(2,1)} %constant_dynamic-update-slice_fusion.10), kind=kOutput, calls=%fused_computation.4 | convolution fusion | flops 25772949504 | bytes 35651584 | tf_op jit(solution)/shard_map/ra,rb->ab/dot_general | solution.py:32
  1340.8 24.2 %collective-permute-done.39.a.c = bf16[512,2048]{1,0:T(8,128)(2,1)S(1)} collective-permute-done((bf16[512,2048]{1,0:T(8,128)(2,1)}, bf16[512,2048]{1,0:T(8,128)(2,1)S(1)}, u32[]{:S(2)}, u32[]{:S(2)}) %collective-permute-start.39) | collective-permute-done | bytes 2097184 | tf_op jit(solution)/shard_map/ppermute | solution.py:885
  1381.5 26.3 %psum.7 = f32[9728]{0:T(1024)S(1)} all-reduce(f32[9728]{0:T(1024)S(1)} %constant_dynamic-update-slice_fusion), channel_id=1, replica_groups=mesh['dp'=4,'ctx'=2,'tp'=4] {'dp','ctx'}, use_global_device_ids=true, to_apply=%region_4.5 | all-reduce | flops 9728 | bytes 77824 | tf_op jit(solution)/shard_map/psum | solution.py:1146
  (401 shorter events, 554.9 us)
Async XLA Ops:
  7.2 53.0 %all-gather.5.cloned.1.call-start = ((), (), s32[]{:S(2)}) async-start(), calls=%async_computation.7 | async-start | bytes 7077888 | tf_op jit(solution)/shard_map/all_gather | solution.py:920
  11.8 108.6 %all-gather.7.cloned.1.call-start = ((), (), s32[]{:S(2)}) async-start(), calls=%async_computation.8 | async-start | bytes 9437184 | tf_op jit(solution)/shard_map/all_gather | solution.py:921
  12.6 198.4 %all-gather.9.cloned.1.call-start = ((), (), s32[]{:S(2)}) async-start(), calls=%async_computation.9 | async-start | bytes 9437184 | tf_op jit(solution)/shard_map/all_gather | solution.py:944
  98.9 192.7 %all-to-all-start = ((bf16[2,4096,768]{2,1,0:T(8,128)(2,1)}), bf16[2,4096,768]{2,1,0:T(8,128)(2,1)}, u32[]{:S(2)}, u32[]{:S(2)}) async-start(bf16[2,4096,768]{2,1,0:T(8,128)(2,1)} %qkv_project.1), calls=%async_computation | async-start | bytes 25165824 | tf_op jit(solution)/shard_map/all_to_all | solution.py:963
  107.3 145.9 %all-gather.11.cloned.1.call-start = ((), (), s32[]{:S(2)}) async-start(), calls=%async_computation.10 | async-start | bytes 2359296 | tf_op jit(solution)/shard_map/all_gather | solution.py:979
  352.7 51.2 %collective-permute-start.1 = (bf16[512,2048]{1,0:T(8,128)(2,1)}, bf16[512,2048]{1,0:T(8,128)(2,1)S(1)}, u32[]{:S(2)}, u32[]{:S(2)}) collective-permute-start(bf16[512,2048]{1,0:T(8,128)(2,1)} %line_begin.9), channel_id=1, source_target_pairs={{0,1},{3,2},{1,0},{2,3},{4,5},{7,6},{5,4},{6,7},{8,9},{11,10},{9,8... | collective-permute-start | bytes 6291464 | tf_op jit(solution)/shard_map/ppermute | solution.py:885
  445.4 82.6 %all-to-all-start.1 = ((bf16[2,4096,256]{2,1,0:T(8,128)(2,1)}), bf16[2,4096,256]{2,1,0:T(8,128)(2,1)}, u32[]{:S(2)}, u32[]{:S(2)}) async-start(bf16[2,4096,256]{2,1,0:T(8,128)(2,1)} %grad_attended.1), calls=%async_computation.1 | async-start | bytes 8388608 | tf_op jit(solution)/shard_map/all_to_all | solution.py:963
  451.0 915.9 %reduce-scatter.14.cloned.1.call-start = ((), (), s32[]{:S(2)}) async-start(), calls=%async_computation.15 | async-start | bytes 9437184 | tf_op jit(solution)/shard_map/reduce_scatter | solution.py:1110
  466.5 52.2 %collective-permute-start.6 = (bf16[512,2048]{1,0:T(8,128)(2,1)}, bf16[512,2048]{1,0:T(8,128)(2,1)S(1)}, u32[]{:S(2)}, u32[]{:S(2)}) collective-permute-start(bf16[512,2048]{1,0:T(8,128)(2,1)} %line_begin.10.b), channel_id=1, source_target_pairs={{0,1},{3,2},{1,0},{2,3},{4,5},{7,6},{5,4},{6,7},{8,9},{11,10},{9,8... | collective-permute-start | bytes 6291464 | tf_op jit(solution)/shard_map/ppermute | solution.py:885
  528.1 63.9 %collective-permute-start.10 = (bf16[512,2048]{1,0:T(8,128)(2,1)}, bf16[512,2048]{1,0:T(8,128)(2,1)S(1)}, u32[]{:S(2)}, u32[]{:S(2)}) collective-permute-start(bf16[512,2048]{1,0:T(8,128)(2,1)} %get-tuple-element.460), channel_id=1, source_target_pairs={{1,2},{2,1},{5,6},{6,5},{9,10},{10,9},{13,14},{14,13},{17,18},{18,... | collective-permute-start | bytes 6291464 | tf_op jit(solution)/shard_map/ppermute | solution.py:886
  528.9 63.1 %collective-permute-start.9 = (bf16[512,2048]{1,0:T(8,128)(2,1)S(1)}, bf16[512,2048]{1,0:T(8,128)(2,1)S(1)}, u32[]{:S(2)}, u32[]{:S(2)}) collective-permute-start(bf16[512,2048]{1,0:T(8,128)(2,1)S(1)} %copy-done.67), channel_id=1, source_target_pairs={{0,1},{3,2},{1,0},{2,3},{4,5},{7,6},{5,4},{6,7},{8,9},{11,10},{9,8... | collective-permute-start | bytes 6291464 | tf_op jit(solution)/shard_map/ppermute | solution.py:885
  598.5 66.3 %collective-permute-start.11 = (bf16[512,2048]{1,0:T(8,128)(2,1)}, bf16[512,2048]{1,0:T(8,128)(2,1)S(1)}, u32[]{:S(2)}, u32[]{:S(2)}) collective-permute-start(bf16[512,2048]{1,0:T(8,128)(2,1)} %line_begin.11.b), channel_id=1, source_target_pairs={{0,1},{3,2},{1,0},{2,3},{4,5},{7,6},{5,4},{6,7},{8,9},{11,10},{9,8... | collective-permute-start | bytes 6291464 | tf_op jit(solution)/shard_map/ppermute | solution.py:885
  600.0 64.9 %collective-permute-start.12 = (bf16[512,2048]{1,0:T(8,128)(2,1)}, bf16[512,2048]{1,0:T(8,128)(2,1)S(1)}, u32[]{:S(2)}, u32[]{:S(2)}) collective-permute-start(bf16[512,2048]{1,0:T(8,128)(2,1)} %line_begin.11.b), channel_id=1, source_target_pairs={{1,2},{2,1},{5,6},{6,5},{9,10},{10,9},{13,14},{14,13},{17,18},{18,... | collective-permute-start | bytes 6291464 | tf_op jit(solution)/shard_map/ppermute | solution.py:886
  671.8 55.7 %collective-permute-start.13 = (bf16[512,2048]{1,0:T(8,128)(2,1)}, bf16[512,2048]{1,0:T(8,128)(2,1)S(1)}, u32[]{:S(2)}, u32[]{:S(2)}) collective-permute-start(bf16[512,2048]{1,0:T(8,128)(2,1)} %get-tuple-element.505), channel_id=1, source_target_pairs={{0,1},{3,2},{1,0},{2,3},{4,5},{7,6},{5,4},{6,7},{8,9},{11,10},{9,8... | collective-permute-start | bytes 6291464 | tf_op jit(solution)/shard_map/ppermute | solution.py:885
  674.2 53.4 %collective-permute-start.14 = (bf16[512,2048]{1,0:T(8,128)(2,1)}, bf16[512,2048]{1,0:T(8,128)(2,1)S(1)}, u32[]{:S(2)}, u32[]{:S(2)}) collective-permute-start(bf16[512,2048]{1,0:T(8,128)(2,1)} %get-tuple-element.506), channel_id=1, source_target_pairs={{1,2},{2,1},{5,6},{6,5},{9,10},{10,9},{13,14},{14,13},{17,18},{18,... | collective-permute-start | bytes 6291464 | tf_op jit(solution)/shard_map/ppermute | solution.py:886
  734.2 77.9 %collective-permute-start.15 = (bf16[512,2048]{1,0:T(8,128)(2,1)}, bf16[512,2048]{1,0:T(8,128)(2,1)S(1)}, u32[]{:S(2)}, u32[]{:S(2)}) collective-permute-start(bf16[512,2048]{1,0:T(8,128)(2,1)} %line_begin.12.b), channel_id=1, source_target_pairs={{0,1},{3,2},{1,0},{2,3},{4,5},{7,6},{5,4},{6,7},{8,9},{11,10},{9,8... | collective-permute-start | bytes 6291464 | tf_op jit(solution)/shard_map/ppermute | solution.py:885
  738.4 73.7 %collective-permute-start.16 = (bf16[512,2048]{1,0:T(8,128)(2,1)}, bf16[512,2048]{1,0:T(8,128)(2,1)S(1)}, u32[]{:S(2)}, u32[]{:S(2)}) collective-permute-start(bf16[512,2048]{1,0:T(8,128)(2,1)} %line_begin.12.b), channel_id=1, source_target_pairs={{1,2},{2,1},{5,6},{6,5},{9,10},{10,9},{13,14},{14,13},{17,18},{18,... | collective-permute-start | bytes 6291464 | tf_op jit(solution)/shard_map/ppermute | solution.py:886
  822.3 50.7 %collective-permute-start.19 = (bf16[1024,768]{1,0:T(8,128)(2,1)}, bf16[1024,768]{1,0:T(8,128)(2,1)}, u32[]{:S(2)}, u32[]{:S(2)}) collective-permute-start(bf16[1024,768]{1,0:T(8,128)(2,1)} %get-tuple-element.818), channel_id=1, source_target_pairs={{0,4},{4,0},{1,5},{5,1},{2,6},{6,2},{3,7},{7,3},{8,12},{12,8},{9,1... | collective-permute-start | bytes 4718600 | tf_op jit(solution)/shard_map/ppermute | solution.py:952
  823.9 77.3 %collective-permute-start.17 = (bf16[512,2048]{1,0:T(8,128)(2,1)}, bf16[512,2048]{1,0:T(8,128)(2,1)S(1)}, u32[]{:S(2)}, u32[]{:S(2)}) collective-permute-start(bf16[512,2048]{1,0:T(8,128)(2,1)} %get-tuple-element.550), channel_id=1, source_target_pairs={{0,1},{3,2},{1,0},{2,3},{4,5},{7,6},{5,4},{6,7},{8,9},{11,10},{9,8... | collective-permute-start | bytes 6291464 | tf_op jit(solution)/shard_map/ppermute | solution.py:885
  825.7 75.6 %collective-permute-start.18 = (bf16[512,2048]{1,0:T(8,128)(2,1)}, bf16[512,2048]{1,0:T(8,128)(2,1)S(1)}, u32[]{:S(2)}, u32[]{:S(2)}) collective-permute-start(bf16[512,2048]{1,0:T(8,128)(2,1)} %get-tuple-element.551), channel_id=1, source_target_pairs={{1,2},{2,1},{5,6},{6,5},{9,10},{10,9},{13,14},{14,13},{17,18},{18,... | collective-permute-start | bytes 6291464 | tf_op jit(solution)/shard_map/ppermute | solution.py:886
  961.9 407.9 %reduce-scatter.10.cloned.1.call-start = ((), (), s32[]{:S(2)}) async-start(), calls=%async_computation.13 | async-start | bytes 4718592 | tf_op jit(solution)/shard_map/reduce_scatter | solution.py:1110
  1075.0 294.8 %reduce-scatter.12.cloned.1.call-start = ((), (), s32[]{:S(2)}) async-start(), calls=%async_computation.14 | async-start | bytes 4718592 | tf_op jit(solution)/shard_map/reduce_scatter | solution.py:1110
  1181.0 226.8 %reduce-scatter.8.cloned.1.call-start = ((), (), s32[]{:S(2)}) async-start(), calls=%async_computation.12 | async-start | bytes 2359296 | tf_op jit(solution)/shard_map/reduce_scatter | solution.py:1110
  1313.5 109.8 %reduce-scatter.6.cloned.1.call-start = ((), (), s32[]{:S(2)}) async-start(), calls=%async_computation.11 | async-start | bytes 7077888 | tf_op jit(solution)/shard_map/reduce_scatter | solution.py:1110
  (101 other events, 1964.8 us)
Sparse Core Ops, SparseCore 0:
  11.9 48.2 all-gather.4
  62.1 58.2 all-gather.6
  122.3 88.6 all-gather.8
  212.7 36.2 all-gather.10
  962.0 79.5 reduce-scatter.13
  1075.1 53.3 reduce-scatter.9
  1181.1 49.9 reduce-scatter.11
  1313.6 42.4 reduce-scatter.7
  1359.5 63.7 reduce-scatter.5
